TPU v7x, 32 devices: a whole 2x2x4 slice. The times are simulated.
32 devices in a mesh: dp: 8 (over z, x), mode: 4 (over y, core).
Axes of the slice: x: 2, y: 2, z: 4, core: 2. Of those that a mesh axis runs over, the one named last changes fastest.
Arguments:
- series: bfloat16 [768, 128, 7], P('mode', 'dp'), may hold values from -6 to 6
- future_values: float32 [768, 128, 7], P('mode', 'dp'), may hold values from -6 to 6
- step_mask: int32 [768, 128], P('mode', 'dp'), may hold values from 0 to 1
- mode_index: int32 [64], replicated, may hold values from 1 to 383, as said below
- dense: float32 [512, 5134], P(('dp', 'mode'))
- dense_m: float32 [512, 5134], P(('dp', 'mode'))
- dense_v: float32 [512, 5134], P(('dp', 'mode'))
- dense_ema: float32 [512, 5134], P(('dp', 'mode'))
- spectral: float32 [2, 64, 32768], P(None, 'mode', 'dp')
- spec_m: float32 [2, 64, 32768], P(None, 'mode', 'dp')
- fourier_variance_moment: float32 [2, 64, 32768], P(None, 'mode', 'dp')
- spec_ema: float32 [2, 64, 32768], P(None, 'mode', 'dp')
Outputs:
- loss: float32 [], replicated
- dense_new: float32 [512, 5134], P(('dp', 'mode'))
- dense_m_new: float32 [512, 5134], P(('dp', 'mode'))
- dense_v_new: float32 [512, 5134], P(('dp', 'mode'))
- dense_ema_new: float32 [512, 5134], P(('dp', 'mode'))
- dense_low: bfloat16 [512, 5134], P(('dp', 'mode'))
- spec_new: float32 [2, 64, 32768], P(None, 'mode', 'dp')
- spec_m_new: float32 [2, 64, 32768], P(None, 'mode', 'dp')
- spec_v_new: float32 [2, 64, 32768], P(None, 'mode', 'dp')
- spec_ema_new: float32 [2, 64, 32768], P(None, 'mode', 'dp')
- spec_low: bfloat16 [2, 64, 32768], P(None, 'mode', 'dp')
Inputs may be any that keep to these rules, and one draw needn't show every extreme that they name: `mode_index`: distinct values.
All inputs are finite; a program needn't handle non-finite values.
Results may differ from a plain program's by a relative error of at most 0.0072.
Values may be sent and summed in bfloat16 or wider, within the bound.
No kernel may reach another device: no remote copies, remote signals or barrier semaphores. Data moves between devices by JAX's collectives and lax.ppermute only.
A program may use at most 192 MiB of HBM per device.

v0:
```python
import math
from functools import partial

import jax
import jax.numpy as jnp
from jax import lax
from jax.experimental import pallas as pl
from jax.experimental.pallas import tpu as pltpu
from jax.sharding import PartitionSpec as P

D = 512
H = 8
E = 64
FF = 2048
M = 64
C = 7
S = 768
LANES = 128

SPECTRAL_WEIGHT = 0.5
RATE_DENSE = 0.02
RATE_SPEC = 0.1
BF = jnp.bfloat16
F32 = jnp.float32
AXES = ("dp", "mode")
SLOPE = jnp.bfloat16
VMEM_BYTES = 52 * 1024 * 1024


def plain(spec, left, right):
    return jnp.einsum(spec, left, right, preferred_element_type=F32)


def exact(spec, left, right):
    return jnp.einsum(
        spec, left, right, precision=lax.Precision.HIGHEST, preferred_element_type=F32
    )


def tables(mode_index):
    steps = jnp.arange(S, dtype=jnp.int32)
    phase = mode_index[:, None] * steps[None, :] % S
    angle = phase.astype(F32) * (2.0 * math.pi / S)
    return (jnp.cos(angle), jnp.sin(angle))


def unpack(whole):
    return (
        whole[:, :D],
        whole[:, D : 2 * D],
        whole[:, 2 * D : 2 * D + FF],
        whole[:, 2 * D + FF : 2 * D + 2 * FF],
        whole[:, 2 * D + 2 * FF : 2 * D + 2 * FF + C],
        whole[:, 2 * D + 2 * FF + C :],
    )


def adamw(weight, grad, first, second, average, rate):
    first_new = 0.5 * first + 0.5 * grad
    second_new = 0.5 * second + 0.5 * grad * grad
    weight_new = weight - rate * (first_new / (jnp.sqrt(second_new) + 1e-08) + 0.01 * weight)
    average_new = 0.9 * average + 0.1 * weight_new
    return (weight_new, first_new, second_new, average_new, weight_new.astype(BF))


def halves(x):
    high = x.astype(BF)
    return high, (x - high.astype(F32)).astype(BF)


def fill(x, size, axis):
    wanted = list(x.shape)
    wanted[axis] = size - x.shape[axis]
    return jnp.concatenate([x, jnp.zeros(wanted, x.dtype)], axis=axis) if wanted[axis] else x


def exchange(x, axes):
    return lax.all_to_all(x, axes, 0, 0, tiled=True)


def partners(step):
    count = lax.axis_size("mode")
    return [(index, index ^ step) for index in range(count)]


def bit_of(step):
    return lax.div(lax.axis_index("mode"), step) % 2


def steps_of_mode():
    return [1 << bit for bit in range(lax.axis_size("mode").bit_length() - 1)]


def gather_rows(x):
    n_data = lax.axis_size("dp")
    held = exchange(jnp.broadcast_to(x[None], (n_data,) + x.shape), "dp")[:, None]
    for step in reversed(steps_of_mode()):
        other = lax.ppermute(held, "mode", partners(step))
        first = bit_of(step) == 0
        pair = [jnp.where(first, held, other), jnp.where(first, other, held)]
        held = jnp.concatenate(pair, axis=1) if step > 1 else jnp.stack(pair, axis=2)
    return held.reshape(-1, x.shape[1])


def scatter_rows(x, rows):
    n_data, n_mode = lax.axis_size("dp"), lax.axis_size("mode")
    held = x.reshape(n_data, n_mode, rows, x.shape[1])
    for step in steps_of_mode():
        held = held.reshape(n_data, held.shape[1] // 2, 2, rows, x.shape[1])
        bit = bit_of(step)
        away = lax.dynamic_index_in_dim(held, 1 - bit, 2, keepdims=False)
        stay = lax.dynamic_index_in_dim(held, bit, 2, keepdims=False)
        other = lax.ppermute(away, "mode", partners(step))
        held = (stay.astype(F32) + other.astype(F32)).astype(BF)
    held = exchange(held.reshape(n_data, rows, x.shape[1]), "dp")
    return jnp.sum(held.astype(F32), axis=0)


NN = (((1,), (0,)), ((), ()))
NT = (((1,), (1,)), ((), ()))
TN = (((0,), (0,)), ((), ()))
FIRST = 2.0 * math.sqrt(2.0 / math.pi)
THIRD = FIRST * 0.044715
GATES = 256
LEAD = 8
HALF = 64


def mm(left, right, dims=NN):
    return lax.dot_general(left, right, dims, preferred_element_type=F32)


def iota(shape, axis):
    return lax.broadcasted_iota(jnp.int32, shape, axis)


def split(x):
    high = x.astype(BF).astype(F32)
    return high, x - high


def by_halves(x):
    high, low = split(x)
    return jnp.where(iota(x.shape, 1) < HALF, high, low).astype(BF)


def fold(x):
    return x + pltpu.roll(x, HALF, 1)


def rows_at(x, first, count):
    parts = []
    if first:
        parts.append(jnp.zeros((first, x.shape[1]), F32))
    parts.append(x)
    if count - first - x.shape[0]:
        parts.append(jnp.zeros((count - first - x.shape[0], x.shape[1]), F32))
    return jnp.concatenate(parts, axis=0)


def row_groups(x):
    return sum(x[at : at + LEAD] for at in range(0, x.shape[0], LEAD))


def block_kernel(
    sizes,
    count_ref,
    got_ref,
    w_ref,
    a_ref,
    at_ref,
    rest_ref,
    rest_t_ref,
    target_ref,
    keep_ref,
    send_ref,
    big_ref,
    stat_ref,
    wdup_ref,
    x_ref,
    v_ref,
    r_ref,
    wd_ref,
    act_ref,
    slope_ref,
    fc_ref,
    zx_ref,
    j_ref,
):
    n_data, n_mode, nb, total = sizes
    n_all = n_data * n_mode
    modes = M // n_mode
    nbm = nb * modes
    share = FF // n_all
    rows = D // n_all
    scale = 2.0 / S
    norm = SPECTRAL_WEIGHT / (total * M * S)
    chunks = FF // GATES

    for i in range(n_data):
        head = i * H // n_data
        block = w_ref[head * E : (head + 1) * E, :D]
        wdup_ref[2 * i * E : (2 * i + 1) * E, :] = block
        wdup_ref[(2 * i + 1) * E : (2 * i + 2) * E, :] = block
    for i in range(n_data):
        blocks = [got_ref[i * n_mode + j, :nbm, :].astype(F32) for j in range(n_mode)]
        for k in range(nb):
            column = [block[k * modes : (k + 1) * modes] for block in blocks]
            x_ref[k * M : (k + 1) * M, i * LANES : (i + 1) * LANES] = jnp.concatenate(
                column, axis=0
            ).astype(BF)
    x_all = x_ref[...]
    real_lane = iota(x_all.shape, 1) % LANES < HALF
    zero = jnp.zeros_like(x_all)
    x_real = jnp.where(real_lane, x_all, zero)
    x_imag = jnp.where(real_lane, zero, x_all)
    line_real = scale * mm(x_real, wdup_ref[...])
    line_imag = scale * mm(x_imag, wdup_ref[...])
    for k in range(nb):
        v_ref[2 * k * M : (2 * k + 1) * M, :] = line_real[k * M : (k + 1) * M].astype(BF)
        v_ref[(2 * k + 1) * M : (2 * k + 2) * M, :] = line_imag[k * M : (k + 1) * M].astype(BF)

    thin_t = w_ref[:, D + FF :].astype(F32).T
    embed_t = thin_t[:LEAD]
    head_t = thin_t[LEAD : 2 * LEAD]
    pad = [jnp.zeros((HALF - nb * LEAD, D), F32)] if nb * LEAD < HALF else []
    embed_all = jnp.concatenate([embed_t] * nb + pad, axis=0).astype(BF)
    head_all = jnp.concatenate([head_t] * nb + pad, axis=0).astype(BF)
    head_twice = jnp.concatenate([head_all, head_all], axis=0)
    embed_twice = jnp.concatenate([embed_t, embed_t], axis=0).astype(BF)

    per = LANES // share
    for at in range(FF // LANES):
        block = jnp.zeros((16, LANES), F32)
        for q in range(per):
            piece = got_ref[at * per + q, nbm : nbm + 16, :].astype(F32)
            piece = pltpu.roll(piece, q * share, 1) if q else piece
            block = jnp.where(iota(block.shape, 1) // share == q, piece, block)
        for k in range(nb):
            spread = jnp.concatenate(
                [rows_at(block[:LEAD], k * LEAD, HALF), rows_at(block[LEAD:], k * LEAD, HALF)],
                axis=0,
            )
            wd_ref[k, :, at * LANES : (at + 1) * LANES] = spread.astype(BF)

    for c in range(FF // 512):
        cols = slice(c * 512, (c + 1) * 512)
        w_up = w_ref[:, D + c * 512 : D + (c + 1) * 512]
        lifted = mm(v_ref[...], w_up)
        thin = mm(embed_twice, w_up)[:LEAD]
        high, low = split(thin)
        for k in range(nb):
            r_ref[k, : 2 * M, cols] = lifted[2 * k * M : 2 * (k + 1) * M].astype(BF)
            r_ref[k, 2 * M :, cols] = jnp.concatenate(
                [rows_at(high, k * LEAD, HALF), rows_at(low, k * LEAD, HALF)], axis=0
            ).astype(BF)

    parts = [mm(head_all[:16], v_ref[2 * k * M : 2 * (k + 1) * M, :], NT)[:LEAD] for k in range(nb)]
    by_head = rows_at(jnp.concatenate(parts, axis=0), 0, HALF)
    cross = mm(head_all, jnp.concatenate([embed_all, jnp.zeros_like(embed_all)], axis=0), NT)
    cross = jnp.where(iota(cross.shape, 0) // LEAD == iota(cross.shape, 1) // LEAD, cross, 0.0)
    high, low = split(jnp.concatenate([by_head, cross], axis=1))
    by_head = jnp.concatenate([high, low], axis=0).astype(BF)
    fc_ref[...] = mm(a_ref[...], by_head, NT)

    def forward(step, carry):
        k = step // chunks
        cols = pl.ds(pl.multiple_of(step % chunks * GATES, GATES), GATES)
        gate = mm(a_ref[...], r_ref[k, :, cols])
        square = gate * gate
        sig = 0.5 * jnp.tanh(gate * (square * (0.5 * THIRD) + 0.5 * FIRST)) + 0.5
        act = gate * sig
        low = act.astype(BF)
        act_ref[k, :, cols] = low
        slope = sig + act * (1.0 - sig) * (square * (3.0 * THIRD) + FIRST)
        slope_ref[k, :, cols] = slope.astype(slope_ref.dtype)
        fc_ref[...] += mm(low, wd_ref[k, :, cols], NT)
        return carry

    lax.fori_loop(0, nb * chunks, forward, 0)

    keep = keep_ref[...]
    masked = keep * (fold(fc_ref[...]) - target_ref[...])
    two = by_halves(masked)
    err = fold(mm(at_ref[: 2 * M, :], two) + mm(rest_ref[...], two))
    stat_ref[...] = jnp.concatenate(
        [
            jnp.full((1, LANES), 0.5 * jnp.sum(masked * masked)),
            jnp.full((1, LANES), 0.5 * jnp.sum(err * err)),
            jnp.zeros((6, LANES), F32),
        ],
        axis=0,
    )
    two = by_halves(err)
    back = fold(mm(a_ref[:, : 2 * M], two) + mm(rest_t_ref[...], two))
    g_fc = keep * ((2.0 / count_ref[0]) * masked + (2.0 * norm) * back)
    g_low = g_fc.astype(BF)
    g_turn = g_fc.T[:HALF].astype(BF)
    fc_ref[...] = g_fc
    zx_ref[...] = jnp.zeros_like(zx_ref)
    j_ref[...] = jnp.zeros_like(j_ref)

    def backward(step, carry):
        k = step // chunks
        cols = pl.ds(pl.multiple_of(step % chunks * GATES, GATES), GATES)
        fed = mm(g_low, wd_ref[k, :, cols])
        g_gate = (fed * slope_ref[k, :, cols].astype(F32)).astype(BF)
        turned = mm(at_ref[...], g_gate)
        r_ref[k, : 2 * M, cols] = turned[: 2 * M].astype(BF)
        own = iota((HALF, GATES), 0) // LEAD == k
        zx_ref[:, cols] += jnp.where(own, turned[2 * M :], 0.0)
        j_ref[:, cols] += jnp.where(own, mm(g_turn, act_ref[k, :, cols]), 0.0)
        return carry

    lax.fori_loop(0, nb * chunks, backward, 0)

    back_fc = by_halves(mm(at_ref[...], g_low))
    lane_of = iota((2 * M, LANES), 1) % HALF // LEAD
    nothing = jnp.zeros((2 * M, LANES), F32)
    back_rows = jnp.concatenate(
        [jnp.where(lane_of == k, back_fc[: 2 * M].astype(F32), nothing) for k in range(nb)], axis=0
    ).astype(BF)
    cross = jnp.where(
        iota((HALF, LANES), 0) // LEAD == iota((HALF, LANES), 1) % HALF // LEAD,
        back_fc[2 * M :].astype(F32),
        0.0,
    ).astype(BF)
    v_all = v_ref[...]
    z_all = r_ref[:, : 2 * M, :].reshape(nb * 2 * M, FF)
    high, low = split(row_groups(zx_ref[...]))
    zx = jnp.concatenate([high, low], axis=0).astype(BF)
    w_up = w_ref[:, D : D + FF]
    back_block = mm(z_all, w_up, NT) + mm(back_rows, head_twice)
    turned = (scale * back_block).astype(BF)
    embed_grad = row_groups(mm(zx, w_up, NT)) + row_groups(mm(cross, head_twice))
    head_grad = row_groups(mm(back_rows, v_all, TN)) + row_groups(mm(cross, embed_all, TN))
    down_grad = row_groups(j_ref[...])

    turned_real = jnp.concatenate(
        [turned[2 * k * M : (2 * k + 1) * M] for k in range(nb)], axis=0
    )
    turned_imag = jnp.concatenate(
        [turned[(2 * k + 1) * M : (2 * k + 2) * M] for k in range(nb)], axis=0
    )
    p_real = mm(turned_real, wdup_ref[...], NT)
    p_imag = mm(turned_imag, wdup_ref[...], NT)
    real_lane = iota((modes, LANES), 1) < HALF
    lane = iota((LEAD, LANES), 1)
    for i in range(n_data):
        cols = slice(i * LANES, (i + 1) * LANES)
        for j in range(n_mode):
            d = i * n_mode + j
            pieces = []
            for k in range(nb):
                at = slice(k * M + j * modes, k * M + (j + 1) * modes)
                pieces.append(jnp.where(real_lane, p_real[at, cols], p_imag[at, cols]))
            send_ref[d, :nbm, :] = jnp.concatenate(pieces, axis=0).astype(BF)
            out = jnp.zeros((LEAD, LANES), F32)
            for source, width, place in (
                (down_grad, share, 0),
                (embed_grad, rows, HALF),
                (head_grad, rows, HALF + rows),
            ):
                first = d * width // LANES * LANES
                piece = source[:, first : first + LANES]
                shift = (place - (d * width - first)) % LANES
                piece = pltpu.roll(piece, shift, 1) if shift else piece
                out = jnp.where((lane >= place) & (lane < place + width), piece, out)
            high, low = split(out)
            send_ref[d, nbm:, :] = jnp.concatenate([high, low], axis=0).astype(BF)

    x_all = x_ref[...]
    real_lane = iota(x_all.shape, 1) % LANES < HALF
    x_real = jnp.where(real_lane, x_all, zero)
    x_imag = jnp.where(real_lane, zero, x_all)
    out_grad = mm(x_real, turned_real, TN) + mm(x_imag, turned_imag, TN)
    each = n_data // H
    for head in range(H):
        block = 0.0
        for i in range(head * each, (head + 1) * each):
            block += out_grad[2 * i * E : (2 * i + 1) * E] + out_grad[(2 * i + 1) * E : (2 * i + 2) * E]
        big_ref[head * E : (head + 1) * E, :D] = block.astype(BF)
    for c in range(FF // 512):
        cols = slice(c * 512, (c + 1) * 512)
        up_grad = mm(v_all, z_all[:, cols], TN) + mm(embed_twice, zx[:, cols], TN)
        big_ref[:, D + c * 512 : D + (c + 1) * 512] = up_grad.astype(BF)


def block(count, got, weights, a, at, rest, rest_t, target, keep, sizes):
    n_data, n_mode, nb, _ = sizes
    whole = pl.BlockSpec(memory_space=pltpu.VMEM)
    return pl.pallas_call(
        partial(block_kernel, sizes),
        out_shape=(
            jax.ShapeDtypeStruct(got.shape, BF),
            jax.ShapeDtypeStruct((D, D + FF), BF),
            jax.ShapeDtypeStruct((8, LANES), F32),
        ),
        in_specs=[pl.BlockSpec(memory_space=pltpu.SMEM)] + [whole] * 8,
        out_specs=(whole,) * 3,
        scratch_shapes=[
            pltpu.VMEM((2 * n_data * E, D), BF),
            pltpu.VMEM((nb * M, n_data * LANES), BF),
            pltpu.VMEM((nb * 2 * M, D), BF),
            pltpu.VMEM((nb, 4 * M, FF), BF),
            pltpu.VMEM((nb, LANES, FF), BF),
            pltpu.VMEM((nb, S, FF), BF),
            pltpu.VMEM((nb, S, FF), SLOPE),
            pltpu.VMEM((S, LANES), F32),
            pltpu.VMEM((HALF, FF), F32),
            pltpu.VMEM((HALF, FF), F32),
        ],
        compiler_params=pltpu.CompilerParams(vmem_limit_bytes=VMEM_BYTES),
        name="block",
    )(count, got, weights, a, at, rest, rest_t, target, keep)


def per_device(
    series,
    future_values,
    step_mask,
    mode_index,
    dense,
    dense_m,
    dense_v,
    dense_ema,
    spectral,
    spec_m,
    fourier_variance_moment,
    spec_ema,
):
    n_mode = lax.axis_size("mode")
    n_data = lax.axis_size("dp")
    n_all = n_mode * n_data
    time_rows, batch, chans = series.shape
    nb = batch // n_mode
    total = batch * n_data
    modes = M // n_mode
    wide = D // n_data
    share = FF // n_all
    rows = dense.shape[0]
    msg_rows = max(modes, 16)

    packed = jnp.concatenate(
        [series.astype(F32), future_values, step_mask.astype(F32)[..., None]], axis=2
    )
    packed = packed.reshape(time_rows, n_mode, nb, 2 * chans + 1).transpose(1, 0, 2, 3)
    packed = exchange(packed, "mode").reshape(S, nb, 2 * chans + 1)
    x_in = packed[..., :chans].astype(BF)
    target = packed[..., chans : 2 * chans]
    keep = packed[..., 2 * chans :]

    cosv, sinv = tables(mode_index)
    basis = jnp.concatenate([cosv, -sinv], axis=0)
    low = basis.astype(BF)
    rest = (basis - low.astype(F32)).astype(BF)

    def lanes(x):
        return fill(fill(x, LEAD, 2).reshape(S, nb * LEAD), HALF, 1)

    x_lanes = lanes(x_in)
    a = jnp.concatenate([low.T, x_lanes, x_lanes], axis=1)
    a_turn = jnp.concatenate([low, x_lanes.T], axis=0)
    target = jnp.concatenate([lanes(target)] * 2, axis=1)
    keep_lanes = lanes(jnp.broadcast_to(keep, (S, nb, LEAD)))
    keep_lanes = jnp.concatenate([keep_lanes] * 2, axis=1)

    mine = dense.astype(BF)
    q_rows, o_rows, u_rows, d_rows, e_rows, h_rows = unpack(mine)
    weights = gather_rows(
        jnp.concatenate(
            [o_rows, u_rows, fill(e_rows, LEAD, 1), fill(h_rows, LANES - LEAD, 1)], axis=1
        )
    )

    inner = plain("rt,tx->rx", low, x_in.reshape(S, nb * chans))
    inner = jnp.concatenate([inner[:M], inner[M:]], axis=1).reshape(n_mode, modes, 2 * nb * chans)
    query_part = plain("rc,re->ce", e_rows, q_rows).reshape(chans, n_data, wide).transpose(1, 0, 2)
    down_part = plain("rc,rf->cf", h_rows, d_rows).reshape(chans, n_all, share).transpose(1, 0, 2)
    steps_local = jnp.sum(keep)
    inner = fill(fill(inner, 64, 2), msg_rows, 1)
    count = jnp.broadcast_to(steps_local, (n_data, n_mode, 1, 64))
    thin = jnp.concatenate(
        [
            jnp.broadcast_to(fill(query_part, 64, 2)[:, None], (n_data, n_mode, chans, 64)),
            count,
            fill(down_part, 64, 2).reshape(n_data, n_mode, chans, 64),
        ],
        axis=2,
    )
    send = jnp.concatenate(
        [jnp.broadcast_to(inner[None], (n_data,) + inner.shape), fill(thin, msg_rows, 2)], axis=3
    ).reshape(n_all, msg_rows, LANES)
    got = exchange(send, AXES)
    thin = jnp.sum(got[:, :, 64:], axis=0)
    query_thin = thin[:chans, :wide]
    down_slice = thin[8 : 8 + chans, :share]
    steps_total = thin[7, 0]
    inner_all = got[:, :modes, : 2 * nb * chans].reshape(n_all, modes, 2, nb, chans)

    spec = exact("dmpkc,cf->mdkpf", inner_all, query_thin).astype(BF)
    spec = spec.reshape(modes, total, 2 * wide)
    w_low = spectral.astype(BF).reshape(2, modes, wide, E)
    mixer = jnp.concatenate(
        [
            jnp.concatenate([w_low[0], w_low[1]], axis=2),
            jnp.concatenate([-w_low[1], w_low[0]], axis=2),
        ],
        axis=1,
    )
    mixed = plain("mbi,mio->mbo", spec, mixer).astype(BF)
    mixed = mixed.reshape(modes, n_all, nb, 2 * E).transpose(1, 2, 0, 3)
    down_high, down_low = halves(down_slice)
    thin = jnp.concatenate([fill(down_high, 8, 0), fill(down_low, 8, 0)], axis=0)
    send = jnp.concatenate(
        [
            mixed.reshape(n_all, nb * modes, 2 * E),
            jnp.broadcast_to(fill(thin, LANES, 1)[None], (n_all, 16, LANES)),
        ],
        axis=1,
    )
    got = exchange(send, AXES)
    send, big, stats = block(
        steps_total.reshape(1),
        got,
        weights,
        a,
        a_turn,
        rest,
        rest.T,
        target,
        keep_lanes,
        (n_data, n_mode, nb, total),
    )
    got = exchange(send, AXES)
    big_sum = scatter_rows(big, rows)
    thin = jnp.sum(got[:, nb * modes :].astype(F32), axis=0)
    thin = (thin[:8] + thin[8:])[:chans]
    down_slice = thin[:, :share]
    embed_own = thin[:, HALF : HALF + rows].T
    head_own = thin[:, HALF + rows : HALF + 2 * rows].T

    g_mixed = got[:, : nb * modes].reshape(n_all, nb, modes, 2 * E)
    g_mixed = g_mixed.transpose(2, 0, 1, 3).reshape(modes, total, 2 * E)
    g_spec = plain("mbo,mio->mbi", g_mixed, mixer).astype(BF)
    g_mixer = plain("mbi,mbo->mio", spec, g_mixed)
    grad_spec = jnp.stack(
        [
            g_mixer[:, :wide, :E] + g_mixer[:, wide:, E:],
            g_mixer[:, :wide, E:] - g_mixer[:, wide:, :E],
        ]
    ).reshape(spectral.shape)
    g_spec = g_spec.reshape(modes, n_all, nb, 2, wide)
    query_back = exact("dmpkc,mdkpf->cf", inner_all, g_spec.astype(F32))
    send = jnp.concatenate([fill(query_back, 64, 1), fill(down_slice, 64, 1)], axis=1)
    send = jnp.concatenate([fill(send, 8, 0), stats], axis=0)
    got = exchange(jnp.broadcast_to(send[None], (n_all, 16, LANES)), AXES)
    query_total = jnp.sum(got[:, :chans, :wide].reshape(n_data, n_mode, chans, wide), axis=1)
    query_total = query_total.transpose(1, 0, 2).reshape(chans, D)
    down_total = got[:, :chans, 64 : 64 + share].transpose(1, 0, 2).reshape(chans, FF)
    spec_norm = SPECTRAL_WEIGHT / (total * M * S)
    loss = jnp.sum(got[:, 8, 0]) / steps_total + spec_norm * jnp.sum(got[:, 9, 0])

    up = lambda x: x.astype(F32)
    dense_sum = jnp.concatenate(
        [
            exact("rc,ce->re", up(e_rows), query_total),
            big_sum,
            exact("rc,cf->rf", up(h_rows), down_total),
            embed_own + exact("re,ce->rc", up(q_rows), query_total),
            head_own + exact("rf,cf->rc", up(d_rows), down_total),
        ],
        axis=1,
    )
    dense_out = adamw(dense, dense_sum, dense_m, dense_v, dense_ema, RATE_DENSE)
    spec_out = adamw(spectral, grad_spec, spec_m, fourier_variance_moment, spec_ema, RATE_SPEC)
    return (loss,) + dense_out + spec_out


def solution(mesh):
    rows = P(("dp", "mode"), None)
    mixing = P(None, "mode", "dp")
    return jax.shard_map(
        per_device,
        mesh=mesh,
        in_specs=(P("mode", "dp", None), P("mode", "dp", None), P("mode", "dp"), P())
        + (rows,) * 4
        + (mixing,) * 4,
        out_specs=(P(),) + (rows,) * 5 + (mixing,) * 5,
        check_vma=False,
    )
```

profile of v0, /device:TPU:0, one launch (start us, length us, event | category | flops | bytes accessed | tf_op | source)
XLA Modules:
  0.0 231.2 jit_solution(9535657022282469824)
XLA Ops:
  0.7 1.0 concatenate.91
  1.7 0.9 reshape.141
  2.5 0.7 convert_element_type.86
  4.1 4.2 %all-to-all-start = ((f32[4,192,4,15]{1,2,3,0:T(4,128)}), f32[4,192,4,15]{1,2,3,0:T(4,128)S(1)}, u32[]{:S(2)}, u32[]{:S(2)}) async-start(f32[4,192,4,15]{1,2,3,0:T(4,128)} %copy.148), calls=%async_computation | async-start | bytes 491520 | tf_op jit(solution)/shard_map/all_to_all | solution.py:78
  8.9 5.3 %all-to-all-done = f32[4,192,4,15]{1,2,3,0:T(4,128)S(1)} async-done(((f32[4,192,4,15]{1,2,3,0:T(4,128)}), f32[4,192,4,15]{1,2,3,0:T(4,128)S(1)}, u32[]{:S(2)}, u32[]{:S(2)}) %all-to-all-start) | async-done | bytes 184352 | tf_op jit(solution)/shard_map/all_to_all | solution.py:78
  14.2 0.9 broadcast_in_dim.32
  15.1 6.5 %all-to-all-start.3 = ((bf16[8,16,2688]{2,1,0:T(8,128)(2,1)}), bf16[8,16,2688]{2,1,0:T(8,128)(2,1)S(1)}, u32[]{:S(2)}, u32[]{:S(2)}) async-start(bf16[8,16,2688]{2,1,0:T(8,128)(2,1)} %broadcast_in_dim.32), calls=%async_computation.3 | async-start | bytes 1376256 | tf_op jit(solution)/shard_map/all_to_all | solution.py:78
  22.3 0.8 neg.7
  23.1 1.0 squeeze.23
  24.0 1.6 fusion.15
  28.2 11.1 %all-to-all-done.3 = bf16[8,16,2688]{2,1,0:T(8,128)(2,1)S(1)} async-done(((bf16[8,16,2688]{2,1,0:T(8,128)(2,1)}), bf16[8,16,2688]{2,1,0:T(8,128)(2,1)S(1)}, u32[]{:S(2)}, u32[]{:S(2)}) %all-to-all-start.3) | async-done | bytes 688160 | tf_op jit(solution)/shard_map/all_to_all | solution.py:78
  40.1 0.8 maximum_maximum_fusion.1
  40.9 3.9 %all-to-all-start.1 = ((f32[32,16,128]{2,1,0:T(8,128)}), f32[32,16,128]{2,1,0:T(8,128)}, u32[]{:S(2)}, u32[]{:S(2)}) async-start(f32[32,16,128]{2,1,0:T(8,128)} %bitcast.5), calls=%async_computation.1 | async-start | bytes 524288 | tf_op jit(solution)/shard_map/all_to_all | solution.py:78
  45.1 0.7 pad_bitcast_fusion
  45.8 11.8 %collective-permute-done = bf16[8,1,16,2688]{3,2,1,0:T(8,128)(2,1)} collective-permute-done((bf16[8,1,16,2688]{3,2,1,0:T(8,128)(2,1)S(1)}, bf16[8,1,16,2688]{3,2,1,0:T(8,128)(2,1)}, u32[]{:S(2)}, u32[]{:S(2)}) %collective-permute-start) | collective-permute-done | bytes 688160 | tf_op jit(solution)/shard_map/ppermute | solution.py:98
  57.6 1.2 broadcast_select_fusion.1
  58.8 1.2 pad_maximum_fusion.1
  61.0 1.2 copy.154
  62.2 1.2 slice_reduce_fusion
  63.5 3.5 %fusion.1 = bf16[16,32,4,2,64]{4,1,2,3,0:T(8,128)(2,1)S(1)} fusion(f32[32,16,2,4,7]{0,1,4,3,2:T(8,128)S(1)} %bitcast.98, f32[16,64]{1,0:T(8,128)S(1)} %slice_reduce_fusion), kind=kOutput, calls=%fused_computation.8 | convolution fusion | flops 22282240 | bytes 987136 | tf_op jit(solution)/shard_map/dmpkc,cf->mdkpf/dot_general | solution.py:35
  67.0 2.1 copy.156
  69.0 3.1 %reshape.127 = bf16[16,128,128]{2,1,0:T(8,128)(2,1)} reshape(bf16[16,32,4,2,64]{4,3,2,1,0:T(2,128)(2,1)} %copy.156) | data formatting | bytes 1048576 | tf_op jit(solution)/shard_map/reshape | solution.py:502
  72.1 1.7 convolution_convert_fusion.2
  74.6 0.9 pad_maximum_fusion.2
  75.4 5.1 %all-to-all-start.2 = ((bf16[32,80,128]{2,1,0:T(8,128)(2,1)}), bf16[32,80,128]{2,1,0:T(8,128)(2,1)}, u32[]{:S(2)}, u32[]{:S(2)}) async-start(bf16[32,80,128]{2,1,0:T(8,128)(2,1)} %pad_maximum_fusion.2), calls=%async_computation.2 | async-start | bytes 1310720 | tf_op jit(solution)/shard_map/all_to_all | solution.py:78
  81.5 1.4 concatenate.107.a_ref
  83.4 1.6 select_bitcast_fusion.1
  85.1 1.8 pad_maximum_fusion
  86.9 11.4 %all-to-all-done.2.got_ref = bf16[32,80,128]{2,1,0:T(8,128)(2,1)} async-done(((bf16[32,80,128]{2,1,0:T(8,128)(2,1)}), bf16[32,80,128]{2,1,0:T(8,128)(2,1)}, u32[]{:S(2)}, u32[]{:S(2)}) %all-to-all-start.2) | async-done | bytes 655392 | tf_op jit(solution)/shard_map/all_to_all | solution.py:78
  98.2 53.3 %block.1 = (bf16[32,80,128]{2,1,0:T(8,128)(2,1)}, bf16[512,2560]{1,0:T(8,128)(2,1)}, f32[8,128]{1,0:T(8,128)S(1)}) custom-call(f32[1]{0:T(128)} %bitcast.7.count_ref, bf16[32,80,128]{2,1,0:T(8,128)(2,1)} %all-to-all-done.2.got_ref, bf16[512,2688]{1,0:T(8,128)(2,1)} %bitcast.97, bf16[768,256]{1,0:T(8,128)(2,1)S(1)} %concatenate.107.a_ref, ...), custom_call_target="tpu_custom_call" | custom-call | tf_op jit(solution)/shard_map/block/pallas_call | solution.py:392
  151.6 3.8 %all-to-all-start.4 = ((bf16[32,80,128]{2,1,0:T(8,128)(2,1)}), bf16[32,80,128]{2,1,0:T(8,128)(2,1)S(1)}, u32[]{:S(2)}, u32[]{:S(2)}) async-start(bf16[32,80,128]{2,1,0:T(8,128)(2,1)} %get-tuple-element.14), calls=%async_computation.4 | async-start | bytes 1310720 | tf_op jit(solution)/shard_map/all_to_all | solution.py:78
  155.4 2.5 %dynamic-slice_bitcast_fusion = bf16[8,2,16,2560]{3,2,1,0:T(8,128)(2,1)} fusion(bf16[8,2,2,16,2560]{4,3,2,1,0:T(8,128)(2,1)} %bitcast.102, s32[]{:T(128)S(6)} %select_n.69), kind=kLoop, calls=%fused_computation.11 | loop fusion | bytes 2621444 | tf_op jit(solution)/shard_map/jit(dynamic_index_in_dim)/squeeze | solution.py:111
  157.9 15.1 %all-to-all-done.4 = bf16[32,80,128]{2,1,0:T(8,128)(2,1)S(1)} async-done(((bf16[32,80,128]{2,1,0:T(8,128)(2,1)}), bf16[32,80,128]{2,1,0:T(8,128)(2,1)S(1)}, u32[]{:S(2)}, u32[]{:S(2)}) %all-to-all-start.4) | async-done | bytes 655392 | tf_op jit(solution)/shard_map/all_to_all | solution.py:78
  175.3 0.7 constant_dynamic-update-slice_fusion.1
  176.6 0.8 convolution_bitcast_fusion.2
  177.5 0.7 broadcast_in_dim.74
  178.3 3.5 %all-to-all-start.5 = ((f32[32,16,128]{2,1,0:T(8,128)}), f32[32,16,128]{2,1,0:T(8,128)S(1)}, u32[]{:S(2)}, u32[]{:S(2)}) async-start(f32[32,16,128]{2,1,0:T(8,128)} %broadcast_in_dim.74), calls=%async_computation.5 | async-start | bytes 524288 | tf_op jit(solution)/shard_map/all_to_all | solution.py:78
  181.8 0.7 constant_dynamic-update-slice_fusion
  182.5 2.8 %fusion.36 = (bf16[2,16,4096]{2,1,0:T(8,128)(2,1)}, f32[2,16,4096]{2,1,0:T(8,128)S(1)}, f32[2,16,4096]{2,1,0:T(8,128)}, f32[2,16,4096]{2,1,0:T(8,128)}) fusion(f32[2,16,4096]{2,1,0:T(8,128)S(1)} %copy-done.6, f32[2,16,4096]{2,1,0:T(8,128)} %constant_dynamic-update-slice_fusion, f32[2,16,4096]{2,1,0:T(8,128)} %param.22, f32[2,16,4096]{2,1,0:T(8,128)} %param.21), kind=kLoop, calls=%fused_computation.101 | loop fusion | flops 1703936 | bytes 3932160 | tf_op jit(solution)/shard_map/convert_element_type | solution.py:63
  185.3 1.9 fusion
  187.4 1.8 collective-permute-start.3
  189.2 0.9 multiply_add_fusion.1
  190.1 14.6 %collective-permute-done.3 = bf16[8,1,16,2560]{3,2,1,0:T(8,128)(2,1)S(1)} collective-permute-done((bf16[8,1,16,2560]{3,2,1,0:T(8,128)(2,1)S(1)}, bf16[8,1,16,2560]{3,2,1,0:T(8,128)(2,1)S(1)}, u32[]{:S(2)}, u32[]{:S(2)}) %collective-permute-start.3) | collective-permute-done | bytes 655392 | tf_op jit(solution)/shard_map/ppermute | solution.py:113
  204.7 1.0 fusion.5
  205.7 5.5 %all-to-all-start.6 = ((bf16[8,16,2560]{2,1,0:T(8,128)(2,1)}), bf16[8,16,2560]{2,1,0:T(8,128)(2,1)S(1)}, u32[]{:S(2)}, u32[]{:S(2)}) async-start(bf16[8,16,2560]{2,1,0:T(8,128)(2,1)} %fusion.5), calls=%async_computation.6 | async-start | bytes 1310720 | tf_op jit(solution)/shard_map/all_to_all | solution.py:78
  215.1 12.9 %all-to-all-done.6 = bf16[8,16,2560]{2,1,0:T(8,128)(2,1)S(1)} async-done(((bf16[8,16,2560]{2,1,0:T(8,128)(2,1)}), bf16[8,16,2560]{2,1,0:T(8,128)(2,1)S(1)}, u32[]{:S(2)}, u32[]{:S(2)}) %all-to-all-start.6) | async-done | bytes 655392 | tf_op jit(solution)/shard_map/all_to_all | solution.py:78
  228.2 1.0 fusion.38
  229.3 0.8 multiply_add_fusion.3
  (143 shorter events, 13.5 us)
Async XLA Ops:
  0.6 7.7 %copy-start.8 = (f32[16,5134]{1,0:T(8,128)S(1)}, f32[16,5134]{1,0:T(8,128)}, u32[]{:S(2)}) copy-start(f32[16,5134]{1,0:T(8,128)} %param.16) | copy-start | bytes 985732
  0.7 7.8 %copy-start.5 = (f32[2,16,4096]{2,1,0:T(8,128)S(1)}, f32[2,16,4096]{2,1,0:T(8,128)}, u32[]{:S(2)}) copy-start(f32[2,16,4096]{2,1,0:T(8,128)} %param.20) | copy-start | bytes 1572868
  4.1 10.1 %all-to-all-start = ((f32[4,192,4,15]{1,2,3,0:T(4,128)}), f32[4,192,4,15]{1,2,3,0:T(4,128)S(1)}, u32[]{:S(2)}, u32[]{:S(2)}) async-start(f32[4,192,4,15]{1,2,3,0:T(4,128)} %copy.148), calls=%async_computation | async-start | bytes 491520 | tf_op jit(solution)/shard_map/all_to_all | solution.py:78
  8.3 13.3 %copy-start.11 = (bf16[16,5134]{1,0:T(8,128)(2,1)}, bf16[16,5134]{1,0:T(8,128)(2,1)S(1)}, u32[]{:S(2)}) copy-start(bf16[16,5134]{1,0:T(8,128)(2,1)S(1)} %convert_element_type.87) | copy-start | bytes 492868
  15.1 9.0 %copy-start.24 = (s32[64]{0:T(128)S(1)}, s32[64]{0:T(128)}, u32[]{:S(2)}) copy-start(s32[64]{0:T(128)} %param.15) | copy-start | bytes 772
  15.1 24.3 %all-to-all-start.3 = ((bf16[8,16,2688]{2,1,0:T(8,128)(2,1)}), bf16[8,16,2688]{2,1,0:T(8,128)(2,1)S(1)}, u32[]{:S(2)}, u32[]{:S(2)}) async-start(bf16[8,16,2688]{2,1,0:T(8,128)(2,1)} %broadcast_in_dim.32), calls=%async_computation.3 | async-start | bytes 1376256 | tf_op jit(solution)/shard_map/all_to_all | solution.py:78
  22.3 3.4 %copy-start.13 = (bf16[16,64,64]{2,1,0:T(8,128)(2,1)}, bf16[16,64,64]{2,1,0:T(8,128)(2,1)S(1)}, u32[]{:S(2)}) copy-start(bf16[16,64,64]{2,1,0:T(8,128)(2,1)S(1)} %squeeze.24) | copy-start | bytes 393220
  26.5 18.3 %copy-start.23 = (pred[8]{0:T(512)(128)(4,1)S(1)}, pred[8]{0:T(512)(128)(4,1)}, u32[]{:S(2)}) copy-start(pred[8]{0:T(512)(128)(4,1)} %constant.83.clone.1) | copy-start | bytes 28
  39.4 18.2 %collective-permute-start = (bf16[8,1,16,2688]{3,2,1,0:T(8,128)(2,1)S(1)}, bf16[8,1,16,2688]{3,2,1,0:T(8,128)(2,1)}, u32[]{:S(2)}, u32[]{:S(2)}) collective-permute-start(bf16[8,1,16,2688]{3,2,1,0:T(8,128)(2,1)S(1)} %bitcast.101), channel_id=1, source_target_pairs={{0,2},{1,3},{2,0},{3,1},{4,6},{5,7},{6,4},{7,5},{8,10},{9,11},{10,... | collective-permute-start | bytes 2064392 | tf_op jit(solution)/shard_map/ppermute | solution.py:98
  40.9 20.1 %all-to-all-start.1 = ((f32[32,16,128]{2,1,0:T(8,128)}), f32[32,16,128]{2,1,0:T(8,128)}, u32[]{:S(2)}, u32[]{:S(2)}) async-start(f32[32,16,128]{2,1,0:T(8,128)} %bitcast.5), calls=%async_computation.1 | async-start | bytes 524288 | tf_op jit(solution)/shard_map/all_to_all | solution.py:78
  45.1 13.8 %copy-start.2 = (bf16[768,32]{1,0:T(8,128)(2,1)}, bf16[768,32]{1,0:T(8,128)(2,1)S(1)}, u32[]{:S(2)}) copy-start(bf16[768,32]{1,0:T(8,128)(2,1)S(1)} %copy.160) | copy-start | bytes 147460
  60.1 23.3 %collective-permute-start.1 = (bf16[8,2,16,2688]{3,2,1,0:T(8,128)(2,1)}, bf16[8,2,16,2688]{3,2,1,0:T(8,128)(2,1)}, u32[]{:S(2)}, u32[]{:S(2)}) collective-permute-start(bf16[8,2,16,2688]{3,2,1,0:T(8,128)(2,1)} %pad_maximum_fusion.1), channel_id=1, source_target_pairs={{0,1},{1,0},{2,3},{3,2},{4,5},{5,4},{6,7},{7,6},{8,9},{9,8},{10,11... | collective-permute-start | bytes 4128776 | tf_op jit(solution)/shard_map/ppermute | solution.py:98
  62.2 6.8 %copy-start = (f32[32,16,56]{0,1,2:T(8,128)}, f32[32,16,56]{0,1,2:T(8,128)S(1)}, u32[]{:S(2)}) copy-start(f32[32,16,56]{0,1,2:T(8,128)S(1)} %copy.154) | copy-start | bytes 344068
  66.9 5.2 %copy-start.14 = (bf16[16,64,64]{2,1,0:T(8,128)(2,1)S(1)}, bf16[16,64,64]{2,1,0:T(8,128)(2,1)}, u32[]{:S(2)}) copy-start(bf16[16,64,64]{2,1,0:T(8,128)(2,1)} %copy-done.13) | copy-start | bytes 393220
  74.5 6.0 %copy-start.16 = (bf16[64,768]{0,1:T(8,128)(2,1)S(1)}, bf16[64,768]{0,1:T(8,128)(2,1)}, u32[]{:S(2)}) copy-start(bf16[64,768]{0,1:T(8,128)(2,1)} %pad_bitcast_fusion) | copy-start | bytes 294916
  75.4 22.8 %all-to-all-start.2 = ((bf16[32,80,128]{2,1,0:T(8,128)(2,1)}), bf16[32,80,128]{2,1,0:T(8,128)(2,1)}, u32[]{:S(2)}, u32[]{:S(2)}) async-start(bf16[32,80,128]{2,1,0:T(8,128)(2,1)} %pad_maximum_fusion.2), calls=%async_computation.2 | async-start | bytes 1310720 | tf_op jit(solution)/shard_map/all_to_all | solution.py:78
  151.6 21.4 %all-to-all-start.4 = ((bf16[32,80,128]{2,1,0:T(8,128)(2,1)}), bf16[32,80,128]{2,1,0:T(8,128)(2,1)S(1)}, u32[]{:S(2)}, u32[]{:S(2)}) async-start(bf16[32,80,128]{2,1,0:T(8,128)(2,1)} %get-tuple-element.14), calls=%async_computation.4 | async-start | bytes 1310720 | tf_op jit(solution)/shard_map/all_to_all | solution.py:78
  157.9 15.5 %copy-start.7 = (bf16[16,128,128]{2,1,0:T(8,128)(2,1)S(1)}, bf16[16,128,128]{2,1,0:T(8,128)(2,1)}, u32[]{:S(2)}) copy-start(bf16[16,128,128]{2,1,0:T(8,128)(2,1)} %reshape.127) | copy-start | bytes 1572868
  157.9 27.4 %collective-permute-start.2 = (bf16[8,2,16,2560]{3,2,1,0:T(8,128)(2,1)}, bf16[8,2,16,2560]{3,2,1,0:T(8,128)(2,1)}, u32[]{:S(2)}, u32[]{:S(2)}) collective-permute-start(bf16[8,2,16,2560]{3,2,1,0:T(8,128)(2,1)} %dynamic-slice_bitcast_fusion), channel_id=1, source_target_pairs={{0,1},{1,0},{2,3},{3,2},{4,5},{5,4},{6,7},{7,6},{8,9},{9,8},{10,11... | collective-permute-start | bytes 3932168 | tf_op jit(solution)/shard_map/ppermute | solution.py:113
  173.1 1.0 copy-start.15
  173.1 1.0 copy-start.21
  173.1 1.1 copy-start.22
  175.3 1.3 copy-start.1
  176.6 5.9 %copy-start.6 = (f32[2,16,4096]{2,1,0:T(8,128)S(1)}, f32[2,16,4096]{2,1,0:T(8,128)}, u32[]{:S(2)}) copy-start(f32[2,16,4096]{2,1,0:T(8,128)} %param.20) | copy-start | bytes 1572868
  178.3 27.5 %all-to-all-start.5 = ((f32[32,16,128]{2,1,0:T(8,128)}), f32[32,16,128]{2,1,0:T(8,128)S(1)}, u32[]{:S(2)}, u32[]{:S(2)}) async-start(f32[32,16,128]{2,1,0:T(8,128)} %broadcast_in_dim.74), calls=%async_computation.5 | async-start | bytes 524288 | tf_op jit(solution)/shard_map/all_to_all | solution.py:78
  182.5 2.8 %copy-start.3 = (bf16[512,2560]{1,0:T(8,128)(2,1)S(1)}, bf16[512,2560]{1,0:T(8,128)(2,1)}, u32[]{:S(2)}) copy-start(bf16[512,2560]{1,0:T(8,128)(2,1)} %get-tuple-element.16) | copy-start | bytes 7864324
  185.3 3.9 %copy-start.4 = (f32[2,16,4096]{2,1,0:T(8,128)}, f32[2,16,4096]{2,1,0:T(8,128)S(1)}, u32[]{:S(2)}) copy-start(f32[2,16,4096]{2,1,0:T(8,128)S(1)} %get-tuple-element.20) | copy-start | bytes 1572868
  187.3 1.9 copy-start.17
  187.4 17.3 %collective-permute-start.3 = (bf16[8,1,16,2560]{3,2,1,0:T(8,128)(2,1)S(1)}, bf16[8,1,16,2560]{3,2,1,0:T(8,128)(2,1)S(1)}, u32[]{:S(2)}, u32[]{:S(2)}) collective-permute-start(bf16[8,1,16,2560]{3,2,1,0:T(8,128)(2,1)S(1)} %constant_dynamic-slice_fusion), channel_id=1, source_target_pairs={{0,2},{1,3},{2,0},{3,1},{4,6},{5,7},{6,4},{7,5},{8,10},{9,11},{10,... | collective-permute-start | bytes 1966088 | tf_op jit(solution)/shard_map/ppermute | solution.py:113
  205.7 5.7 %copy-start.12 = (bf16[16,5134]{1,0:T(8,128)(2,1)S(1)}, bf16[16,5134]{1,0:T(8,128)(2,1)}, u32[]{:S(2)}) copy-start(bf16[16,5134]{1,0:T(8,128)(2,1)} %copy-done.11) | copy-start | bytes 492868
  205.7 22.3 %all-to-all-start.6 = ((bf16[8,16,2560]{2,1,0:T(8,128)(2,1)}), bf16[8,16,2560]{2,1,0:T(8,128)(2,1)S(1)}, u32[]{:S(2)}, u32[]{:S(2)}) async-start(bf16[8,16,2560]{2,1,0:T(8,128)(2,1)} %fusion.5), calls=%async_computation.6 | async-start | bytes 1310720 | tf_op jit(solution)/shard_map/all_to_all | solution.py:78
  211.3 16.9 %copy-start.9 = (f32[16,5134]{1,0:T(8,128)S(1)}, f32[16,5134]{1,0:T(8,128)}, u32[]{:S(2)}) copy-start(f32[16,5134]{1,0:T(8,128)} %param.16) | copy-start | bytes 985732
  211.3 16.9 %copy-start.18 = (f32[16,5134]{1,0:T(8,128)S(1)}, f32[16,5134]{1,0:T(8,128)}, u32[]{:S(2)}) copy-start(f32[16,5134]{1,0:T(8,128)} %param.18) | copy-start | bytes 985732
  211.3 16.9 %copy-start.19 = (f32[16,5134]{1,0:T(8,128)S(1)}, f32[16,5134]{1,0:T(8,128)}, u32[]{:S(2)}) copy-start(f32[16,5134]{1,0:T(8,128)} %param.17) | copy-start | bytes 985732
  228.2 1.1 copy-start.20
  229.3 0.8 copy-start.10
where the time goes:
time: 232 us; the launch traced here: 231 us
  waiting for transfers between devices  82.2 us (35%)
  Pallas kernels  53.3 us (23%)
  starting transfers between devices  34.9 us (15%)
  local copies, waits for them, and re-layouts  24.7 us (11%)
  other arithmetic  23.4 us (10%)
  matrix products  8.13 us (4%)
  between operations  4.49 us (2%)
    all_to_all x7, waiting for transfers between devices, exchange(): return lax.all_to_all(x, axes, 0, 0, tiled=True)  55.8 us
    pallas_call x1, Pallas kernels, block(): pl.pallas_call(partial(block_kernel, sizes), out_shape=(jax.ShapeDtypeStr...  53.3 us
    all_to_all x7, starting transfers between devices, exchange(): return lax.all_to_all(x, axes, 0, 0, tiled=True)  32.5 us
    ppermute x2, waiting for transfers between devices, scatter_rows(): other = lax.ppermute(away, 'mode', partners(step))  14.6 us
    ppermute x2, waiting for transfers between devices, gather_rows(): other = lax.ppermute(held, 'mode', partners(step))  11.8 us
    dot_general x6, matrix products, exact(): jnp.einsum(spec, left, right, precision=lax.Precision.HIGHEST, preferred_...  4.89 us
  transfers between devices with their start and end apart: 11, of which 7 were waited for; matrix products, arithmetic and copies ran while one was open for 21% of the time, Pallas kernels for 0%

commit v1 on v0

--- a/solution.py
+++ b/solution.py
@@ -89,6 +89,94 @@
 
 def steps_of_mode():
     return [1 << bit for bit in range(lax.axis_size("mode").bit_length() - 1)]
+
+
+def by_xor(x, axis, step):
+    count = lax.axis_size(axis)
+    return lax.ppermute(x, axis, [(index, index ^ step) for index in range(count)])
+
+
+def assemble_kernel(offsets, n_mode, rows, me_ref, *refs):
+    out_ref = refs[-1]
+    for ref, (data, mode) in zip(refs[:-1], offsets, strict=True):
+        for at, (one, two) in enumerate(zip(data, mode, strict=True)):
+            owner = (me_ref[0] ^ one) * n_mode + (me_ref[1] ^ two)
+            out_ref[pl.ds(pl.multiple_of(owner * rows, rows), rows), :] = ref[at]
+
+
+def gather_tiles(x, me):
+    n_data, n_mode = lax.axis_size("dp"), lax.axis_size("mode")
+    deep = [x] + [by_xor(x, "dp", 2 * step) for step in range(1, n_data // 2)]
+    cut = len(deep) // 2
+    first, second = jnp.stack(deep[:cut]), jnp.stack(deep[cut:])
+    first = jnp.concatenate([first, by_xor(first, "dp", 1)])
+    second = jnp.concatenate([second, by_xor(second, "mode", 2)])
+    pieces = [first, by_xor(first, "mode", 2), second, by_xor(second, "dp", 1)]
+    pieces += [by_xor(piece, "mode", 1) for piece in pieces]
+    low = [2 * step for step in range(cut)]
+    high = [2 * step for step in range(cut, 2 * cut)]
+    ones = lambda data: [index + 1 for index in data]
+    offsets = [
+        (low + ones(low), [0] * 2 * cut),
+        (low + ones(low), [2] * 2 * cut),
+        (high + high, [0] * cut + [2] * cut),
+        (ones(high) + ones(high), [0] * cut + [2] * cut),
+    ]
+    offsets += [(data, [index + 1 for index in mode]) for data, mode in offsets]
+    whole = pl.BlockSpec(memory_space=pltpu.VMEM)
+    return pl.pallas_call(
+        partial(assemble_kernel, offsets, n_mode, x.shape[0]),
+        out_shape=jax.ShapeDtypeStruct((n_data * n_mode * x.shape[0], x.shape[1]), x.dtype),
+        in_specs=[pl.BlockSpec(memory_space=pltpu.SMEM)] + [whole] * len(pieces),
+        out_specs=whole,
+        compiler_params=pltpu.CompilerParams(vmem_limit_bytes=VMEM_BYTES),
+        name="assemble",
+    )(me, *pieces)
+
+
+def tile_order(n_data):
+    cut = n_data // 4
+    low = [2 * step for step in range(cut)]
+    high = [2 * step for step in range(cut, 2 * cut)]
+    groups = [
+        [(data + x, 2) for data in low for x in (0, 1)],
+        [(data + x, 0) for data in low for x in (0, 1)],
+        [(data + 1, 2 * y) for data in high for y in (0, 1)],
+        [(data, 2 * y) for data in high for y in (0, 1)],
+    ]
+    return [[(data, mode + core) for data, mode in group] for core in (1, 0) for group in groups]
+
+
+def together(*values):
+    return lax.optimization_barrier(values)
+
+
+def add(left, right):
+    return (left.astype(F32) + right.astype(F32)).astype(BF)
+
+
+def scatter_tiles_first(away, stay):
+    pairs = lambda x: x.reshape((x.shape[0] // 2, 2) + x.shape[1:])
+    come = by_xor(away, "mode", 1)
+    groups = [add(come[g], stay[g]) for g in range(4)]
+    first = by_xor(groups[0], "mode", 2)
+    second = by_xor(groups[2], "dp", 1)
+    return [pairs(x) for x in (first, groups[1], second, groups[3])]
+
+
+def scatter_tiles_second(one, two, three, four):
+    first_come = by_xor(add(one[:, 1], two[:, 1]), "dp", 1)
+    second_come = by_xor(add(three[:, 1], four[:, 1]), "mode", 2)
+    return [first_come, add(one[:, 0], two[:, 0]), second_come, add(three[:, 0], four[:, 0])]
+
+
+def scatter_tiles_third(one, two, three, four):
+    cut = one.shape[0]
+    total = one[0].astype(F32) + two[0].astype(F32)
+    for step in range(1, 2 * cut):
+        left, right, at = (one, two, step) if step < cut else (three, four, step - cut)
+        total += by_xor(add(left[at], right[at]), "dp", 2 * step).astype(F32)
+    return total
 
 
 def gather_rows(x):
@@ -163,6 +251,53 @@
 
 
 def block_kernel(
+    sizes,
+    count_ref,
+    me_ref,
+    got_ref,
+    w_ref,
+    a_ref,
+    at_ref,
+    rest_ref,
+    rest_t_ref,
+    target_ref,
+    keep_ref,
+    send_ref,
+    stat_ref,
+    *refs,
+):
+    if len(sizes) > 4:
+        away_ref, stay_ref, big_ref, *refs = refs
+    else:
+        big_ref, *refs = refs
+    block_steps(
+        sizes,
+        count_ref,
+        got_ref,
+        w_ref,
+        a_ref,
+        at_ref,
+        rest_ref,
+        rest_t_ref,
+        target_ref,
+        keep_ref,
+        send_ref,
+        big_ref,
+        stat_ref,
+        *refs,
+    )
+    if len(sizes) > 4:
+        n_data, n_mode = sizes[:2]
+        rows = D // n_data // n_mode
+        order = tile_order(n_data)
+        for at, group in enumerate(order):
+            ref = away_ref if at < 4 else stay_ref
+            for index, (data, mode) in enumerate(group):
+                owner = (me_ref[0] ^ data) * n_mode + (me_ref[1] ^ mode)
+                ref[at % 4, index] = big_ref[pl.ds(pl.multiple_of(owner * rows, rows), rows), :]
+
+
+def block_steps(
     sizes,
     count_ref,
     got_ref,
@@ -187,7 +322,7 @@
     zx_ref,
     j_ref,
 ):
-    n_data, n_mode, nb, total = sizes
+    n_data, n_mode, nb, total = sizes[:4]
     n_all = n_data * n_mode
     modes = M // n_mode
     nbm = nb * modes
@@ -386,19 +521,24 @@
         big_ref[:, D + c * 512 : D + (c + 1) * 512] = up_grad.astype(BF)
 
 
-def block(count, got, weights, a, at, rest, rest_t, target, keep, sizes):
-    n_data, n_mode, nb, _ = sizes
+def block(count, me, got, weights, a, at, rest, rest_t, target, keep, sizes):
+    n_data, n_mode, nb = sizes[:3]
     whole = pl.BlockSpec(memory_space=pltpu.VMEM)
+    big = [jax.ShapeDtypeStruct((D, D + FF), BF)]
+    if len(sizes) > 4:
+        half = (4, n_data * n_mode // 8, D // n_data // n_mode, D + FF)
+        big = [jax.ShapeDtypeStruct(half, BF)] * 2
     return pl.pallas_call(
         partial(block_kernel, sizes),
         out_shape=(
             jax.ShapeDtypeStruct(got.shape, BF),
-            jax.ShapeDtypeStruct((D, D + FF), BF),
             jax.ShapeDtypeStruct((8, LANES), F32),
+            *big,
         ),
-        in_specs=[pl.BlockSpec(memory_space=pltpu.SMEM)] + [whole] * 8,
-        out_specs=(whole,) * 3,
-        scratch_shapes=[
+        in_specs=[pl.BlockSpec(memory_space=pltpu.SMEM)] * 2 + [whole] * 8,
+        out_specs=(whole,) * (2 + len(big)),
+        scratch_shapes=([pltpu.VMEM((D, D + FF), BF)] if len(sizes) > 4 else [])
+        + [
             pltpu.VMEM((2 * n_data * E, D), BF),
             pltpu.VMEM((nb * M, n_data * LANES), BF),
             pltpu.VMEM((nb * 2 * M, D), BF),
@@ -412,7 +552,197 @@
         ],
         compiler_params=pltpu.CompilerParams(vmem_limit_bytes=VMEM_BYTES),
         name="block",
-    )(count, got, weights, a, at, rest, rest_t, target, keep)
+    )(count, me, got, weights, a, at, rest, rest_t, target, keep)
+
+
+def at_lane(x, first, width):
+    x = pltpu.roll(x, first, 1) if first else x
+    lane = iota(x.shape, 1)
+    return jnp.where((lane >= first) & (lane < first + width), x, 0.0)
+
+
+def from_lane(x, first, width):
+    base = first // LANES * LANES
+    x = x[:, base : base + LANES]
+    shift = (LANES - (first - base)) % LANES
+    x = pltpu.roll(x, shift, 1) if shift else x
+    return jnp.where(iota(x.shape, 1) < width, x, 0.0)
+
+
+def call(kernel, outs, ins, scratch=(), name=None):
+    whole = pl.BlockSpec(memory_space=pltpu.VMEM)
+    return pl.pallas_call(
+        kernel,
+        out_shape=outs,
+        in_specs=[whole] * len(ins),
+        out_specs=jax.tree.map(lambda _: whole, outs),
+        scratch_shapes=list(scratch),
+        compiler_params=pltpu.CompilerParams(vmem_limit_bytes=VMEM_BYTES),
+        name=name,
+    )(*ins)
+
+
+def spectra_kernel(sizes, x_ref, keep_ref, low_ref, dense_ref, send_ref):
+    n_data, n_mode, nb, _ = sizes
+    n_all = n_data * n_mode
+    modes = M // n_mode
+    wide = D // n_data
+    share = FF // n_all
+    x = x_ref[...].astype(F32)
+    x = jnp.concatenate([x, jnp.zeros_like(x)], axis=1)
+    inner = mm(low_ref[:M, :], x.astype(BF))
+    inner += mm(low_ref[M:, :], pltpu.roll(x, nb * LEAD, 1).astype(BF))
+    thin = dense_ref[:, 2 * D + 2 * FF :]
+    thin = jnp.concatenate([thin, jnp.zeros((thin.shape[0], LANES - 2 * C), F32)], axis=1)
+    thin = at_lane(thin, 0, C) + at_lane(from_lane(thin, C, C), LEAD, C)
+    thin = thin.astype(BF)
+    query = mm(thin, dense_ref[:, :D].astype(BF), TN)[:LEAD]
+    down = mm(thin, dense_ref[:, 2 * D + FF : 2 * D + 2 * FF].astype(BF), TN)[LEAD : 2 * LEAD]
+    count = jnp.sum(keep_ref[...]) * (0.5 / LEAD)
+    row = iota((LEAD, LANES), 0)
+    lane = iota((LEAD, LANES), 1)
+    for i in range(n_data):
+        ours = at_lane(from_lane(query, i * wide, wide), HALF, wide)
+        ours = jnp.where((row == C) & (lane == HALF), count, ours)
+        for j in range(n_mode):
+            d = i * n_mode + j
+            block = inner[j * modes : (j + 1) * modes]
+            if modes < 16:
+                block = jnp.concatenate([block, jnp.zeros((16 - modes, LANES), F32)], axis=0)
+            theirs = at_lane(from_lane(down, d * share, share), HALF, share)
+            send_ref[d] = block + jnp.concatenate([ours, theirs], axis=0)
+
+
+def mix_kernel(sizes, got_ref, mixer_ref, send_ref, spec_ref, thin_ref, wide_ref, out_ref):
+    n_data, n_mode, nb, _ = sizes
+    n_all = n_data * n_mode
+    modes = M // n_mode
+    nbm = nb * modes
+    wide = D // n_data
+    share = FF // n_all
+    got = got_ref[...]
+    thin = jnp.sum(got, axis=0)
+    thin_ref[...] = thin
+    query = from_lane(thin[:LEAD], HALF, wide)
+    query = jnp.where(iota(query.shape, 0) < C, query, 0.0)
+    down = from_lane(thin[LEAD:], HALF, share)
+    high, low = split(down)
+    down = jnp.concatenate([high, low], axis=0).astype(BF)
+    spread = []
+    for part in range(2):
+        block = at_lane(query, part * wide, wide)
+        zero = jnp.zeros_like(block)
+        for k in range(nb):
+            blocks = [block if g == k else zero for g in range(nb)]
+            spread.append(jnp.concatenate(blocks, axis=1))
+    spread = jnp.concatenate(spread, axis=0)
+    inner = got.reshape(n_all * 16, LANES)[:, : 2 * nb * LEAD]
+    spec = lax.dot_general(
+        inner, spread, NN, precision=lax.Precision.HIGHEST, preferred_element_type=F32
+    )
+    for k in range(nb):
+        wide_ref[k] = spec[:, k * LANES : (k + 1) * LANES]
+    for m in range(modes):
+        spec = [wide_ref[k, pl.ds(m, n_all, stride=16), :][:, : 2 * wide] for k in range(nb)]
+        spec = jnp.concatenate(spec, axis=0).astype(BF)
+        spec_ref[m] = spec
+        mixed = mm(spec, mixer_ref[m])
+        for k in range(nb):
+            out_ref[pl.ds(k * modes + m, n_all, stride=nbm), :] = mixed[
+                k * n_all : (k + 1) * n_all
+            ]
+    for d in range(n_all):
+        send_ref[d, :nbm, :] = out_ref[d * nbm : (d + 1) * nbm, :].astype(BF)
+        send_ref[d, nbm:, :] = down
+
+
+def mix_back_kernel(
+    sizes, got_ref, mixer_ref, first_ref, stat_ref, send_ref, grad_ref, thin_ref, in_ref, wide_ref
+):
+    n_data, n_mode, nb, _ = sizes
+    n_all = n_data * n_mode
+    modes = M // n_mode
+    nbm = nb * modes
+    wide = D // n_data
+    share = FF // n_all
+    thin = jnp.zeros((16, LANES), F32)
+    for d in range(n_all):
+        in_ref[d * nbm : (d + 1) * nbm, :] = got_ref[d, :nbm, :].astype(F32)
+        thin += got_ref[d, nbm:, :].astype(F32)
+    thin = thin[:LEAD] + thin[LEAD:]
+    thin_ref[...] = thin
+    if modes < 16:
+        wide_ref[...] = jnp.zeros_like(wide_ref)
+    for m in range(modes):
+        grad = [in_ref[pl.ds(k * modes + m, n_all, stride=nbm), :] for k in range(nb)]
+        grad = jnp.concatenate(grad, axis=0).astype(BF)
+        grad_ref[m] = grad
+        back = mm(grad, mixer_ref[m], NT).astype(BF).astype(F32)
+        if 2 * wide < LANES:
+            back = jnp.concatenate(
+                [back, jnp.zeros((back.shape[0], LANES - 2 * wide), F32)], axis=1
+            )
+        for k in range(nb):
+            wide_ref[k, pl.ds(m, n_all, stride=16), :] = back[k * n_all : (k + 1) * n_all]
+    inner = first_ref[...].reshape(n_all * 16, LANES)
+    inner = jnp.where(iota(inner.shape, 1) < HALF, inner, 0.0)
+    inner = by_halves(fold(inner))
+    total = jnp.zeros((LEAD, LANES), F32)
+    for k in range(nb):
+        query = mm(inner, wide_ref[k].astype(BF), TN)
+        query = query[:HALF] + query[HALF:]
+        for part in range(2):
+            at = (part * nb + k) * LEAD
+            total += from_lane(query[at : at + LEAD], part * wide, wide)
+    block = total + at_lane(from_lane(thin, 0, share), HALF, share)
+    block = jnp.concatenate([block, stat_ref[...]], axis=0)
+    for d in range(n_all):
+        send_ref[d] = block
+
+
+def spectral_kernel(
+    modes,
+    wide,
+    spec_ref,
+    grad_ref,
+    w_ref,
+    m_ref,
+    v_ref,
+    ema_ref,
+    w_out,
+    m_out,
+    v_out,
+    ema_out,
+    low_out,
+    pair_ref,
+    turn_ref,
+):
+    lower = iota((wide, LANES), 1) < HALF
+    half_lower = iota((wide // 2, LANES), 1) < HALF
+    for m in range(modes):
+        slopes = mm(spec_ref[m], grad_ref[m], TN)
+        other = pltpu.roll(slopes[wide:], HALF, 1)
+        pair_ref[m] = jnp.where(lower, slopes[:wide] + other, slopes[:wide] - other)
+        even = pair_ref[m, pl.ds(0, wide // 2, stride=2), :]
+        odd = pair_ref[m, pl.ds(1, wide // 2, stride=2), :]
+        real = jnp.where(half_lower, even, pltpu.roll(odd, HALF, 1))
+        imag = jnp.where(half_lower, pltpu.roll(even, HALF, 1), odd)
+        turn_ref[0, pl.ds(m, wide // 2, stride=modes), :] = real
+        turn_ref[1, pl.ds(m, wide // 2, stride=modes), :] = imag
+    for part in range(2):
+        for at in range(wide // 2):
+            cols = slice(at * LANES, (at + 1) * LANES)
+            grad = turn_ref[part, at * modes : (at + 1) * modes, :]
+            new = adamw(
+                w_ref[part, :, cols],
+                grad,
+                m_ref[part, :, cols],
+                v_ref[part, :, cols],
+                ema_ref[part, :, cols],
+                RATE_SPEC,
+            )
+            for ref, value in zip((w_out, m_out, v_out, ema_out, low_out), new, strict=True):
+                ref[part, :, cols] = value
 
 
 def per_device(
@@ -467,39 +797,23 @@
 
     mine = dense.astype(BF)
     q_rows, o_rows, u_rows, d_rows, e_rows, h_rows = unpack(mine)
-    weights = gather_rows(
-        jnp.concatenate(
-            [o_rows, u_rows, fill(e_rows, LEAD, 1), fill(h_rows, LANES - LEAD, 1)], axis=1
-        )
-    )
-
-    inner = plain("rt,tx->rx", low, x_in.reshape(S, nb * chans))
-    inner = jnp.concatenate([inner[:M], inner[M:]], axis=1).reshape(n_mode, modes, 2 * nb * chans)
-    query_part = plain("rc,re->ce", e_rows, q_rows).reshape(chans, n_data, wide).transpose(1, 0, 2)
-    down_part = plain("rc,rf->cf", h_rows, d_rows).reshape(chans, n_all, share).transpose(1, 0, 2)
-    steps_local = jnp.sum(keep)
-    inner = fill(fill(inner, 64, 2), msg_rows, 1)
-    count = jnp.broadcast_to(steps_local, (n_data, n_mode, 1, 64))
-    thin = jnp.concatenate(
-        [
-            jnp.broadcast_to(fill(query_part, 64, 2)[:, None], (n_data, n_mode, chans, 64)),
-            count,
-            fill(down_part, 64, 2).reshape(n_data, n_mode, chans, 64),
-        ],
-        axis=2,
-    )
-    send = jnp.concatenate(
-        [jnp.broadcast_to(inner[None], (n_data,) + inner.shape), fill(thin, msg_rows, 2)], axis=3
-    ).reshape(n_all, msg_rows, LANES)
-    got = exchange(send, AXES)
-    thin = jnp.sum(got[:, :, 64:], axis=0)
-    query_thin = thin[:chans, :wide]
-    down_slice = thin[8 : 8 + chans, :share]
-    steps_total = thin[7, 0]
-    inner_all = got[:, :modes, : 2 * nb * chans].reshape(n_all, modes, 2, nb, chans)
-
-    spec = exact("dmpkc,cf->mdkpf", inner_all, query_thin).astype(BF)
-    spec = spec.reshape(modes, total, 2 * wide)
+    sizes = (n_data, n_mode, nb, total)
+    tiled = rows % 16 == 0 and n_mode == 4 and n_data >= 4
+    me = jnp.stack([lax.axis_index("dp"), lax.axis_index("mode")]).astype(jnp.int32)
+    weights = jnp.concatenate(
+        [o_rows, u_rows, fill(e_rows, LEAD, 1), fill(h_rows, LANES - LEAD, 1)], axis=1
+    )
+    weights = gather_tiles(weights, me) if tiled else gather_rows(weights)
+
+    shape = jax.ShapeDtypeStruct
+    send = call(
+        partial(spectra_kernel, sizes),
+        shape((n_all, 16, LANES), F32),
+        (x_lanes, keep_lanes, low, dense),
+        name="spectra",
+    )
+    first = exchange(send, AXES)
+
     w_low = spectral.astype(BF).reshape(2, modes, wide, E)
     mixer = jnp.concatenate(
         [
@@ -508,20 +822,27 @@
         ],
         axis=1,
     )
-    mixed = plain("mbi,mio->mbo", spec, mixer).astype(BF)
-    mixed = mixed.reshape(modes, n_all, nb, 2 * E).transpose(1, 2, 0, 3)
-    down_high, down_low = halves(down_slice)
-    thin = jnp.concatenate([fill(down_high, 8, 0), fill(down_low, 8, 0)], axis=0)
-    send = jnp.concatenate(
-        [
-            mixed.reshape(n_all, nb * modes, 2 * E),
-            jnp.broadcast_to(fill(thin, LANES, 1)[None], (n_all, 16, LANES)),
-        ],
-        axis=1,
-    )
+    scratch = [
+        pltpu.VMEM((nb, n_all * 16, LANES), F32),
+        pltpu.VMEM((n_all * nb * modes, LANES), F32),
+    ]
+    send, spec, thin = call(
+        partial(mix_kernel, sizes),
+        (
+            shape((n_all, nb * modes + 16, LANES), BF),
+            shape((modes, total, 2 * wide), BF),
+            shape((16, LANES), F32),
+        ),
+        (first, mixer),
+        scratch,
+        name="mix",
+    )
+    steps_total = thin[7, HALF]
     got = exchange(send, AXES)
-    send, big, stats = block(
+
+    send, stats, *big = block(
         steps_total.reshape(1),
+        me,
         got,
         weights,
         a,
@@ -530,31 +851,40 @@
         rest.T,
         target,
         keep_lanes,
-        (n_data, n_mode, nb, total),
+        sizes + (True,) if tiled else sizes,
     )
     got = exchange(send, AXES)
-    big_sum = scatter_rows(big, rows)
-    thin = jnp.sum(got[:, nb * modes :].astype(F32), axis=0)
-    thin = (thin[:8] + thin[8:])[:chans]
-    down_slice = thin[:, :share]
-    embed_own = thin[:, HALF : HALF + rows].T
-    head_own = thin[:, HALF + rows : HALF + 2 * rows].T
-
-    g_mixed = got[:, : nb * modes].reshape(n_all, nb, modes, 2 * E)
-    g_mixed = g_mixed.transpose(2, 0, 1, 3).reshape(modes, total, 2 * E)
-    g_spec = plain("mbo,mio->mbi", g_mixed, mixer).astype(BF)
-    g_mixer = plain("mbi,mbo->mio", spec, g_mixed)
-    grad_spec = jnp.stack(
+    if tiled:
+        big = scatter_tiles_first(*big)
+        got, *big = together(got, *big)
+        big = scatter_tiles_second(*big)
+    send, grad_mixed, thin = call(
+        partial(mix_back_kernel, sizes),
+        (
+            shape((n_all, 16, LANES), F32),
+            shape((modes, total, LANES), BF),
+            shape((LEAD, LANES), F32),
+        ),
+        (got, mixer, first, stats),
+        scratch[::-1],
+        name="mix_back",
+    )
+    embed_own = thin[:C, HALF : HALF + rows].T
+    head_own = thin[:C, HALF + rows : HALF + 2 * rows].T
+    spec_out = call(
+        partial(spectral_kernel, modes, wide),
+        (shape(spectral.shape, F32),) * 4 + (shape(spectral.shape, BF),),
+        (spec, grad_mixed, spectral, spec_m, fourier_variance_moment, spec_ema),
         [
-            g_mixer[:, :wide, :E] + g_mixer[:, wide:, E:],
-            g_mixer[:, :wide, E:] - g_mixer[:, wide:, :E],
-        ]
-    ).reshape(spectral.shape)
-    g_spec = g_spec.reshape(modes, n_all, nb, 2, wide)
-    query_back = exact("dmpkc,mdkpf->cf", inner_all, g_spec.astype(F32))
-    send = jnp.concatenate([fill(query_back, 64, 1), fill(down_slice, 64, 1)], axis=1)
-    send = jnp.concatenate([fill(send, 8, 0), stats], axis=0)
-    got = exchange(jnp.broadcast_to(send[None], (n_all, 16, LANES)), AXES)
+            pltpu.VMEM((modes, wide, LANES), F32),
+            pltpu.VMEM((2, modes * wide // 2, LANES), F32),
+        ],
+        name="spectral",
+    )
+    if tiled:
+        send, *big = together(send, *big)
+    got = exchange(send, AXES)
+    big_sum = scatter_tiles_third(*big) if tiled else scatter_rows(big[0], rows)
     query_total = jnp.sum(got[:, :chans, :wide].reshape(n_data, n_mode, chans, wide), axis=1)
     query_total = query_total.transpose(1, 0, 2).reshape(chans, D)
     down_total = got[:, :chans, 64 : 64 + share].transpose(1, 0, 2).reshape(chans, FF)
@@ -573,8 +903,7 @@
         axis=1,
     )
     dense_out = adamw(dense, dense_sum, dense_m, dense_v, dense_ema, RATE_DENSE)
-    spec_out = adamw(spectral, grad_spec, spec_m, fourier_variance_moment, spec_ema, RATE_SPEC)
-    return (loss,) + dense_out + spec_out
+    return (loss,) + tuple(dense_out) + tuple(spec_out)
 
 
 def solution(mesh):

time: 232 us -> 196 us (0.84)
  waiting for transfers between devices: 82.2 us -> 43.2 us
  Pallas kernels: 53.3 us -> 68.9 us
  local copies, waits for them, and re-layouts: 24.7 us -> 14.5 us
  starting transfers between devices: 34.9 us -> 43.3 us
  matrix products: 8.13 us -> 0.72 us
  other arithmetic: 23.4 us -> 19.7 us
    all_to_all x7 -> x5, waiting for transfers between devices: 55.8 us -> 30.3 us  [exchange(): return lax.all_to_all(x, axes, 0, 0, tiled=True)]
    ppermute x4 -> x19, starting transfers between devices: 2.47 us -> 23.4 us  [by_xor(): lax.ppermute(x, axis, [(index, index ^ step) for index in range(count)])]
    pallas_call x0 -> x5, Pallas kernels: none -> 15.5 us  [the longest x4 12.2 us: call(): pl.pallas_call(kernel, out_shape=outs, in_specs=[whole] * len(ins), out_s...]
    ppermute x4 -> x19, waiting for transfers between devices: 26.4 us -> 12.9 us  [by_xor(): lax.ppermute(x, axis, [(index, index ^ step) for index in range(count)])]
    all_to_all x7 -> x5, starting transfers between devices: 32.5 us -> 19.9 us  [exchange(): return lax.all_to_all(x, axes, 0, 0, tiled=True)]
    reshape x6 -> x0, local copies, waits for them, and re-layouts: 4.28 us -> none  [the longest x1 3.08 us: per_device(): spec = spec.reshape(modes, total, 2 * wide)]
    dot_general x6 -> x4, matrix products: 4.89 us -> 0.72 us  [exact(): jnp.einsum(spec, left, right, precision=lax.Precision.HIGHEST, preferred_...]
    dot_general x6 -> x0, matrix products: 3.23 us -> none  [plain(): return jnp.einsum(spec, left, right, preferred_element_type=F32)]
  transfers between devices with their start and end apart: 11 -> 24, of which waited for: 7 -> 8; matrix products, arithmetic and copies ran while one was open for 21% -> 13% of each run, Pallas kernels for 0% -> 8%
where the time goes in v1:
time: 196 us; the launch traced here: 195 us
  Pallas kernels  68.9 us (35%)
  starting transfers between devices  43.3 us (22%)
  waiting for transfers between devices  43.2 us (22%)
  other arithmetic  19.7 us (10%)
  local copies, waits for them, and re-layouts  14.5 us (7%)
  between operations  4.27 us (2%)
    pallas_call x1, Pallas kernels, block(): pl.pallas_call(partial(block_kernel, sizes), out_shape=(jax.ShapeDtypeStr...  53.4 us
    all_to_all x5, waiting for transfers between devices, exchange(): return lax.all_to_all(x, axes, 0, 0, tiled=True)  30.3 us
    ppermute x19, starting transfers between devices, by_xor(): lax.ppermute(x, axis, [(index, index ^ step) for index in range(count)])  23.4 us
    all_to_all x5, starting transfers between devices, exchange(): return lax.all_to_all(x, axes, 0, 0, tiled=True)  19.9 us
    ppermute x19, waiting for transfers between devices, by_xor(): lax.ppermute(x, axis, [(index, index ^ step) for index in range(count)])  12.9 us
    pallas_call x4, Pallas kernels, call(): pl.pallas_call(kernel, out_shape=outs, in_specs=[whole] * len(ins), out_s...  12.2 us
    convert_element_type x5, other arithmetic, add(): return (left.astype(F32) + right.astype(F32)).astype(BF)  5.15 us
  transfers between devices with their start and end apart: 24, of which 8 were waited for; matrix products, arithmetic and copies ran while one was open for 13% of the time, Pallas kernels for 8%

profile of v1, /device:TPU:0, one launch (start us, length us, event | category | flops | bytes accessed | tf_op | source)
XLA Modules:
  0.0 194.6 jit_solution(4942992565584515307)
XLA Ops:
  0.7 1.1 convert_element_type.211
  1.9 5.0 %collective-permute-start.4 = (bf16[16,2688]{1,0:T(8,128)(2,1)S(1)}, bf16[16,2688]{1,0:T(8,128)(2,1)S(1)}, u32[]{:S(2)}, u32[]{:S(2)}) collective-permute-start(bf16[16,2688]{1,0:T(8,128)(2,1)S(1)} %concatenate.77), channel_id=1, source_target_pairs={{0,24},{4,28},{8,16},{12,20},{16,8},{20,12},{24,0},{28,4},{1,25},{... | collective-permute-start | bytes 258056 | tf_op jit(solution)/shard_map/ppermute | solution.py:96
  8.3 0.9 reshape.123
  9.2 0.9 concatenate.67
  10.9 3.4 %all-to-all-start = ((f32[4,192,4,15]{1,2,3,0:T(4,128)}), f32[4,192,4,15]{1,2,3,0:T(4,128)S(1)}, u32[]{:S(2)}, u32[]{:S(2)}) async-start(f32[4,192,4,15]{1,2,3,0:T(4,128)} %copy.112), calls=%async_computation | async-start | bytes 491520 | tf_op jit(solution)/shard_map/all_to_all | solution.py:78
  14.4 1.6 fusion.8
  17.3 2.9 %all-to-all-done = f32[4,192,4,15]{1,2,3,0:T(4,128)S(1)} async-done(((f32[4,192,4,15]{1,2,3,0:T(4,128)}), f32[4,192,4,15]{1,2,3,0:T(4,128)S(1)}, u32[]{:S(2)}, u32[]{:S(2)}) %all-to-all-start) | async-done | bytes 184352 | tf_op jit(solution)/shard_map/all_to_all | solution.py:78
  20.9 0.9 copy.116
  21.8 0.9 copy.122
  22.7 1.9 pad_maximum_fusion
  24.7 1.4 spectra.1
  26.1 5.0 %all-to-all-start.1 = ((f32[32,16,128]{2,1,0:T(8,128)}), f32[32,16,128]{2,1,0:T(8,128)S(1)}, u32[]{:S(2)}, u32[]{:S(2)}) async-start(f32[32,16,128]{2,1,0:T(8,128)} %spectra.1), calls=%async_computation.1 | async-start | bytes 524288 | tf_op jit(solution)/shard_map/all_to_all | solution.py:78
  31.1 1.6 pad_maximum_fusion.8
  32.7 1.8 collective-permute-start.1
  35.2 1.5 collective-permute-start.5
  36.6 5.2 %all-to-all-done.1.got_ref.first_ref = f32[32,16,128]{2,1,0:T(8,128)S(1)} async-done(((f32[32,16,128]{2,1,0:T(8,128)}), f32[32,16,128]{2,1,0:T(8,128)S(1)}, u32[]{:S(2)}, u32[]{:S(2)}) %all-to-all-start.1) | async-done | bytes 262176 | tf_op jit(solution)/shard_map/all_to_all | solution.py:78
  41.8 3.1 %mix.1 = (bf16[32,80,128]{2,1,0:T(8,128)(2,1)}, bf16[16,128,128]{2,1,0:T(8,128)(2,1)S(1)}, f32[16,128]{1,0:T(8,128)S(1)}) custom-call(f32[32,16,128]{2,1,0:T(8,128)S(1)} %all-to-all-done.1.got_ref.first_ref, bf16[16,128,128]{2,1,0:T(8,128)(2,1)S(1)} %maximum_maximum_fusion.mixer_ref), custom_call_target="tpu_custom_call" | custom-call | tf_op jit(solution)/shard_map/mix/pallas_call | solution.py:574
  45.7 3.5 %all-to-all-start.2 = ((bf16[32,80,128]{2,1,0:T(8,128)(2,1)}), bf16[32,80,128]{2,1,0:T(8,128)(2,1)}, u32[]{:S(2)}, u32[]{:S(2)}) async-start(bf16[32,80,128]{2,1,0:T(8,128)(2,1)} %get-tuple-element.37), calls=%async_computation.2 | async-start | bytes 1310720 | tf_op jit(solution)/shard_map/all_to_all | solution.py:78
  49.2 1.0 pad_maximum_fusion.6.refs_0_
  50.3 1.5 collective-permute-start.2
  51.8 1.7 pad_maximum_fusion.7.refs_2_
  53.5 1.5 collective-permute-start.6
  55.5 10.7 %collective-permute-done.2.refs_1_ = bf16[4,16,2688]{2,1,0:T(8,128)(2,1)} collective-permute-done((bf16[4,16,2688]{2,1,0:T(8,128)(2,1)S(1)}, bf16[4,16,2688]{2,1,0:T(8,128)(2,1)}, u32[]{:S(2)}, u32[]{:S(2)}) %collective-permute-start.2) | collective-permute-done | bytes 344096 | tf_op jit(solution)/shard_map/ppermute | solution.py:96
  66.2 0.9 collective-permute-done.6.refs_3_
  68.8 1.9 copy.124.at_ref
  71.4 1.5 concatenate.80.a_ref
  73.5 3.3 %assemble.1.w_ref = bf16[512,2688]{1,0:T(8,128)(2,1)} custom-call(s32[2]{0:T(128)S(1)} %pad_add_fusion.me_ref, bf16[4,16,2688]{2,1,0:T(8,128)(2,1)S(1)} %pad_maximum_fusion.6.refs_0_, bf16[4,16,2688]{2,1,0:T(8,128)(2,1)} %collective-permute-done.2.refs_1_, bf16[4,16,2688]{2,1,0:T(8,128)(2,1)} %pad_maximum_fusion.7.refs_2_, ...), custom_call_target="tpu_custom_call" | custom-call | tf_op jit(solution)/shard_map/assemble/pallas_call | solution.py:127
  76.8 1.0 copy-done.2
  77.8 0.9 copy-done.3
  78.7 53.4 %block.1 = (bf16[32,80,128]{2,1,0:T(8,128)(2,1)}, f32[8,128]{1,0:T(8,128)S(1)}, bf16[4,4,16,2560]{3,2,1,0:T(8,128)(2,1)}, bf16[4,4,16,2560]{3,2,1,0:T(8,128)(2,1)}) custom-call(f32[1]{0:T(128)} %bitcast.4.count_ref, s32[2]{0:T(128)S(1)} %pad_add_fusion.me_ref, bf16[32,80,128]{2,1,0:T(8,128)(2,1)} %all-to-all-done.2.got_ref, ...), custom_call_target="tpu_custom_call" | custom-call | tf_op jit(solution)/shard_map/block/pallas_call | solution.py:531
  132.7 4.3 %all-to-all-start.3 = ((bf16[32,80,128]{2,1,0:T(8,128)(2,1)}), bf16[32,80,128]{2,1,0:T(8,128)(2,1)S(1)}, u32[]{:S(2)}, u32[]{:S(2)}) async-start(bf16[32,80,128]{2,1,0:T(8,128)(2,1)} %get-tuple-element.38), calls=%async_computation.3 | async-start | bytes 1310720 | tf_op jit(solution)/shard_map/all_to_all | solution.py:78
  136.9 2.9 %add_convert_fusion = (bf16[1,4,16,2560]{3,2,1,0:T(8,128)(2,1)S(1)}, bf16[4,16,2560]{2,1,0:T(8,128)(2,1)}, bf16[1,4,16,2560]{3,2,1,0:T(8,128)(2,1)S(1)}, bf16[4,16,2560]{2,1,0:T(8,128)(2,1)}) fusion(bf16[4,4,16,2560]{3,2,1,0:T(8,128)(2,1)} %collective-permute-done.11, bf16[4,4,16,2560]{3,2,1,0:T(8,128)(2,1)} %get-tuple-element.40), kind=kLoop, calls=%fused_computation.6 | loop fusion | flops 2621440 | bytes 3932160 | tf_op jit(solution)/shard_map/convert_element_type | solution.py:155
  139.8 1.6 collective-permute-start.13
  141.4 1.5 collective-permute-start.12
  142.9 11.8 %all-to-all-done.3.got_ref = bf16[32,80,128]{2,1,0:T(8,128)(2,1)S(1)} async-done(((bf16[32,80,128]{2,1,0:T(8,128)(2,1)}), bf16[32,80,128]{2,1,0:T(8,128)(2,1)S(1)}, u32[]{:S(2)}, u32[]{:S(2)}) %all-to-all-start.3) | async-done | bytes 655392 | tf_op jit(solution)/shard_map/all_to_all | solution.py:78
  154.9 1.1 fusion.14
  156.0 1.4 collective-permute-start.14
  157.5 1.1 fusion.16
  158.6 1.5 collective-permute-start.15
  160.1 3.3 %mix_back.1 = (f32[32,16,128]{2,1,0:T(8,128)}, bf16[16,128,128]{2,1,0:T(8,128)(2,1)S(1)}, f32[8,128]{1,0:T(8,128)S(1)}) custom-call(bf16[32,80,128]{2,1,0:T(8,128)(2,1)} %copy-done.8, bf16[16,128,128]{2,1,0:T(8,128)(2,1)S(1)} %maximum_maximum_fusion.mixer_ref, f32[32,16,128]{2,1,0:T(8,128)S(1)} %all-to-all-done.1.got_ref.first_ref, ...), custom_call_target="tpu_custom_call" | custom-call | tf_op jit(solution)/shard_map/mix_back/pallas_call | solution.py:574
  163.3 1.0 collective-permute-done.15
  164.3 1.3 collective-permute-start.16
  165.7 2.3 %collective-permute-start.17 = (bf16[16,2560]{1,0:T(8,128)(2,1)S(1)}, bf16[16,2560]{1,0:T(8,128)(2,1)S(1)}, u32[]{:S(2)}, u32[]{:S(2)}) collective-permute-start(bf16[16,2560]{1,0:T(8,128)(2,1)S(1)} %get-tuple-element.79), channel_id=1, source_target_pairs={{0,16},{4,20},{8,24},{12,28},{16,0},{20,4},{24,8},{28,12},{1,17},{... | collective-permute-start | bytes 245768 | tf_op jit(solution)/shard_map/ppermute | solution.py:96
  167.9 0.9 collective-permute-start.18
  168.9 4.4 %spectral.1 = (f32[2,16,4096]{2,1,0:T(8,128)}, f32[2,16,4096]{2,1,0:T(8,128)}, f32[2,16,4096]{2,1,0:T(8,128)}, f32[2,16,4096]{2,1,0:T(8,128)}, bf16[2,16,4096]{2,1,0:T(8,128)(2,1)}) custom-call(bf16[16,128,128]{2,1,0:T(8,128)(2,1)S(1)} %copy-done.5, bf16[16,128,128]{2,1,0:T(8,128)(2,1)S(1)} %get-tuple-element.55.grad_ref, f32[2,16,4096]{2,1,0:T(8,128)S(1)} %copy-done.1, ...), custom_call_target="tpu_custom_call" | custom-call | tf_op jit(solution)/shard_map/spectral/pallas_call | solution.py:574
  173.3 3.7 %all-to-all-start.4 = ((f32[32,16,128]{2,1,0:T(8,128)}), f32[32,16,128]{2,1,0:T(8,128)S(1)}, u32[]{:S(2)}, u32[]{:S(2)}) async-start(f32[32,16,128]{2,1,0:T(8,128)} %get-tuple-element.48), calls=%async_computation.4 | async-start | bytes 524288 | tf_op jit(solution)/shard_map/all_to_all | solution.py:78
  177.1 10.5 %all-to-all-done.4 = f32[32,16,128]{2,1,0:T(8,128)S(1)} async-done(((f32[32,16,128]{2,1,0:T(8,128)}), f32[32,16,128]{2,1,0:T(8,128)S(1)}, u32[]{:S(2)}, u32[]{:S(2)}) %all-to-all-start.4) | async-done | bytes 262176 | tf_op jit(solution)/shard_map/all_to_all | solution.py:78
  191.6 1.1 fusion.28
  (111 shorter events, 13.1 us)
Async XLA Ops:
  0.6 13.7 %copy-start.1 = (f32[2,16,4096]{2,1,0:T(8,128)S(1)}, f32[2,16,4096]{2,1,0:T(8,128)}, u32[]{:S(2)}) copy-start(f32[2,16,4096]{2,1,0:T(8,128)} %w_ref.1) | copy-start | bytes 1572868
  1.7 7.5 %copy-start.10 = (bf16[16,5134]{1,0:T(8,128)(2,1)}, bf16[16,5134]{1,0:T(8,128)(2,1)S(1)}, u32[]{:S(2)}) copy-start(bf16[16,5134]{1,0:T(8,128)(2,1)S(1)} %convert_element_type.211) | copy-start | bytes 492868
  1.9 32.6 %collective-permute-start.4 = (bf16[16,2688]{1,0:T(8,128)(2,1)S(1)}, bf16[16,2688]{1,0:T(8,128)(2,1)S(1)}, u32[]{:S(2)}, u32[]{:S(2)}) collective-permute-start(bf16[16,2688]{1,0:T(8,128)(2,1)S(1)} %concatenate.77), channel_id=1, source_target_pairs={{0,24},{4,28},{8,16},{12,20},{16,8},{20,12},{24,0},{28,4},{1,25},{... | collective-permute-start | bytes 258056 | tf_op jit(solution)/shard_map/ppermute | solution.py:96
  7.0 27.5 %collective-permute-start.3 = (bf16[16,2688]{1,0:T(8,128)(2,1)S(1)}, bf16[16,2688]{1,0:T(8,128)(2,1)S(1)}, u32[]{:S(2)}, u32[]{:S(2)}) collective-permute-start(bf16[16,2688]{1,0:T(8,128)(2,1)S(1)} %concatenate.77), channel_id=1, source_target_pairs={{0,16},{4,20},{8,24},{12,28},{16,0},{20,4},{24,8},{28,12},{1,17},{... | collective-permute-start | bytes 258056 | tf_op jit(solution)/shard_map/ppermute | solution.py:96
  7.0 24.1 %collective-permute-start = (bf16[16,2688]{1,0:T(8,128)(2,1)S(1)}, bf16[16,2688]{1,0:T(8,128)(2,1)}, u32[]{:S(2)}, u32[]{:S(2)}) collective-permute-start(bf16[16,2688]{1,0:T(8,128)(2,1)S(1)} %concatenate.77), channel_id=1, source_target_pairs={{0,8},{4,12},{8,0},{12,4},{16,24},{20,28},{24,16},{28,20},{1,9},{5... | collective-permute-start | bytes 258056 | tf_op jit(solution)/shard_map/ppermute | solution.py:96
  10.1 4.3 %copy-start.17 = (s32[64]{0:T(128)S(1)}, s32[64]{0:T(128)}, u32[]{:S(2)}) copy-start(s32[64]{0:T(128)} %param.15) | copy-start | bytes 772
  10.9 9.2 %all-to-all-start = ((f32[4,192,4,15]{1,2,3,0:T(4,128)}), f32[4,192,4,15]{1,2,3,0:T(4,128)S(1)}, u32[]{:S(2)}, u32[]{:S(2)}) async-start(f32[4,192,4,15]{1,2,3,0:T(4,128)} %copy.112), calls=%async_computation | async-start | bytes 491520 | tf_op jit(solution)/shard_map/all_to_all | solution.py:78
  16.3 51.7 %copy-start.6 = (bf16[128,768]{0,1:T(8,128)(2,1)}, bf16[128,768]{0,1:T(8,128)(2,1)S(1)}, u32[]{:S(2)}) copy-start(bf16[128,768]{0,1:T(8,128)(2,1)S(1)} %get-tuple-element.68) | copy-start | bytes 589828
  17.0 3.5 %copy-start.16 = (pred[8]{0:T(512)(128)(4,1)S(1)}, pred[8]{0:T(512)(128)(4,1)}, u32[]{:S(2)}) copy-start(pred[8]{0:T(512)(128)(4,1)} %constant.16.clone.1) | copy-start | bytes 28
  20.8 15.8 %copy-start.7 = (bf16[768,32]{1,0:T(8,128)(2,1)}, bf16[768,32]{1,0:T(8,128)(2,1)S(1)}, u32[]{:S(2)}) copy-start(bf16[768,32]{1,0:T(8,128)(2,1)S(1)} %copy.115) | copy-start | bytes 147460
  22.7 2.0 %copy-start = (f32[16,5134]{1,0:T(8,128)S(1)}, f32[16,5134]{1,0:T(8,128)}, u32[]{:S(2)}) copy-start(f32[16,5134]{1,0:T(8,128)} %dense_ref.1) | copy-start | bytes 985732
  26.1 15.7 %all-to-all-start.1 = ((f32[32,16,128]{2,1,0:T(8,128)}), f32[32,16,128]{2,1,0:T(8,128)S(1)}, u32[]{:S(2)}, u32[]{:S(2)}) async-start(f32[32,16,128]{2,1,0:T(8,128)} %spectra.1), calls=%async_computation.1 | async-start | bytes 524288 | tf_op jit(solution)/shard_map/all_to_all | solution.py:78
  32.7 16.5 %collective-permute-start.1 = (bf16[2,16,2688]{2,1,0:T(8,128)(2,1)}, bf16[2,16,2688]{2,1,0:T(8,128)(2,1)}, u32[]{:S(2)}, u32[]{:S(2)}) collective-permute-start(bf16[2,16,2688]{2,1,0:T(8,128)(2,1)} %pad_maximum_fusion.8), channel_id=1, source_target_pairs={{0,4},{4,0},{8,12},{12,8},{16,20},{20,16},{24,28},{28,24},{1,5},{5... | collective-permute-start | bytes 516104 | tf_op jit(solution)/shard_map/ppermute | solution.py:96
  34.5 14.7 %copy-start.12 = (bf16[16,2688]{1,0:T(8,128)(2,1)}, bf16[16,2688]{1,0:T(8,128)(2,1)S(1)}, u32[]{:S(2)}) copy-start(bf16[16,2688]{1,0:T(8,128)(2,1)S(1)} %collective-permute-done.3) | copy-start | bytes 258052
  35.2 16.6 %collective-permute-start.5 = (bf16[2,16,2688]{2,1,0:T(8,128)(2,1)}, bf16[2,16,2688]{2,1,0:T(8,128)(2,1)}, u32[]{:S(2)}, u32[]{:S(2)}) collective-permute-start(bf16[2,16,2688]{2,1,0:T(8,128)(2,1)} %pad_maximum_fusion.9), channel_id=1, source_target_pairs={{0,2},{1,3},{2,0},{3,1},{4,6},{5,7},{6,4},{7,5},{8,10},{9,11},{10,... | collective-permute-start | bytes 516104 | tf_op jit(solution)/shard_map/ppermute | solution.py:96
  44.9 0.8 copy-start.4
  45.7 31.1 %all-to-all-start.2 = ((bf16[32,80,128]{2,1,0:T(8,128)(2,1)}), bf16[32,80,128]{2,1,0:T(8,128)(2,1)}, u32[]{:S(2)}, u32[]{:S(2)}) async-start(bf16[32,80,128]{2,1,0:T(8,128)(2,1)} %get-tuple-element.37), calls=%async_computation.2 | async-start | bytes 1310720 | tf_op jit(solution)/shard_map/all_to_all | solution.py:78
  50.3 15.9 %collective-permute-start.2 = (bf16[4,16,2688]{2,1,0:T(8,128)(2,1)S(1)}, bf16[4,16,2688]{2,1,0:T(8,128)(2,1)}, u32[]{:S(2)}, u32[]{:S(2)}) collective-permute-start(bf16[4,16,2688]{2,1,0:T(8,128)(2,1)S(1)} %pad_maximum_fusion.6.refs_0_), channel_id=1, source_target_pairs={{0,2},{1,3},{2,0},{3,1},{4,6},{5,7},{6,4},{7,5},{8,10},{9,11},{10,... | collective-permute-start | bytes 1032200 | tf_op jit(solution)/shard_map/ppermute | solution.py:96
  53.5 13.6 %collective-permute-start.6 = (bf16[4,16,2688]{2,1,0:T(8,128)(2,1)}, bf16[4,16,2688]{2,1,0:T(8,128)(2,1)}, u32[]{:S(2)}, u32[]{:S(2)}) collective-permute-start(bf16[4,16,2688]{2,1,0:T(8,128)(2,1)} %pad_maximum_fusion.7.refs_2_), channel_id=1, source_target_pairs={{0,4},{4,0},{8,12},{12,8},{16,20},{20,16},{24,28},{28,24},{1,5},{5... | collective-permute-start | bytes 1032200 | tf_op jit(solution)/shard_map/ppermute | solution.py:96
  55.0 18.5 %collective-permute-start.7 = (bf16[4,16,2688]{2,1,0:T(8,128)(2,1)S(1)}, bf16[4,16,2688]{2,1,0:T(8,128)(2,1)}, u32[]{:S(2)}, u32[]{:S(2)}) collective-permute-start(bf16[4,16,2688]{2,1,0:T(8,128)(2,1)S(1)} %pad_maximum_fusion.6.refs_0_), channel_id=1, source_target_pairs={{0,1},{1,0},{2,3},{3,2},{4,5},{5,4},{6,7},{7,6},{8,9},{9,8},{10,11... | collective-permute-start | bytes 1032200 | tf_op jit(solution)/shard_map/ppermute | solution.py:96
  55.0 18.5 %collective-permute-start.9 = (bf16[4,16,2688]{2,1,0:T(8,128)(2,1)}, bf16[4,16,2688]{2,1,0:T(8,128)(2,1)}, u32[]{:S(2)}, u32[]{:S(2)}) collective-permute-start(bf16[4,16,2688]{2,1,0:T(8,128)(2,1)} %pad_maximum_fusion.7.refs_2_), channel_id=1, source_target_pairs={{0,1},{1,0},{2,3},{3,2},{4,5},{5,4},{6,7},{7,6},{8,9},{9,8},{10,11... | collective-permute-start | bytes 1032200 | tf_op jit(solution)/shard_map/ppermute | solution.py:96
  66.2 7.3 %collective-permute-start.8 = (bf16[4,16,2688]{2,1,0:T(8,128)(2,1)}, bf16[4,16,2688]{2,1,0:T(8,128)(2,1)}, u32[]{:S(2)}, u32[]{:S(2)}) collective-permute-start(bf16[4,16,2688]{2,1,0:T(8,128)(2,1)} %collective-permute-done.2.refs_1_), channel_id=1, source_target_pairs={{0,1},{1,0},{2,3},{3,2},{4,5},{5,4},{6,7},{7,6},{8,9},{9,8},{10,11... | collective-permute-start | bytes 1032200 | tf_op jit(solution)/shard_map/ppermute | solution.py:96
  67.1 6.4 %collective-permute-start.10 = (bf16[4,16,2688]{2,1,0:T(8,128)(2,1)}, bf16[4,16,2688]{2,1,0:T(8,128)(2,1)}, u32[]{:S(2)}, u32[]{:S(2)}) collective-permute-start(bf16[4,16,2688]{2,1,0:T(8,128)(2,1)} %collective-permute-done.6.refs_3_), channel_id=1, source_target_pairs={{0,1},{1,0},{2,3},{3,2},{4,5},{5,4},{6,7},{7,6},{8,9},{9,8},{10,11... | collective-permute-start | bytes 1032200 | tf_op jit(solution)/shard_map/ppermute | solution.py:96
  76.8 1.0 copy-start.2
  77.8 0.9 copy-start.3
  132.1 4.8 %collective-permute-start.11 = (bf16[4,4,16,2560]{3,2,1,0:T(8,128)(2,1)}, bf16[4,4,16,2560]{3,2,1,0:T(8,128)(2,1)}, u32[]{:S(2)}, u32[]{:S(2)}) collective-permute-start(bf16[4,4,16,2560]{3,2,1,0:T(8,128)(2,1)} %get-tuple-element.39), channel_id=1, source_target_pairs={{0,1},{1,0},{2,3},{3,2},{4,5},{5,4},{6,7},{7,6},{8,9},{9,8},{10,11... | collective-permute-start | bytes 3932168 | tf_op jit(solution)/shard_map/ppermute | solution.py:96
  132.7 22.0 %all-to-all-start.3 = ((bf16[32,80,128]{2,1,0:T(8,128)(2,1)}), bf16[32,80,128]{2,1,0:T(8,128)(2,1)S(1)}, u32[]{:S(2)}, u32[]{:S(2)}) async-start(bf16[32,80,128]{2,1,0:T(8,128)(2,1)} %get-tuple-element.38), calls=%async_computation.3 | async-start | bytes 1310720 | tf_op jit(solution)/shard_map/all_to_all | solution.py:78
  139.8 14.8 %collective-permute-start.13 = (bf16[4,16,2560]{2,1,0:T(8,128)(2,1)}, bf16[4,16,2560]{2,1,0:T(8,128)(2,1)}, u32[]{:S(2)}, u32[]{:S(2)}) collective-permute-start(bf16[4,16,2560]{2,1,0:T(8,128)(2,1)} %get-tuple-element.70), channel_id=1, source_target_pairs={{0,4},{4,0},{8,12},{12,8},{16,20},{20,16},{24,28},{28,24},{1,5},{5... | collective-permute-start | bytes 983048 | tf_op jit(solution)/shard_map/ppermute | solution.py:96
  141.4 13.5 %collective-permute-start.12 = (bf16[4,16,2560]{2,1,0:T(8,128)(2,1)}, bf16[4,16,2560]{2,1,0:T(8,128)(2,1)}, u32[]{:S(2)}, u32[]{:S(2)}) collective-permute-start(bf16[4,16,2560]{2,1,0:T(8,128)(2,1)} %get-tuple-element.72), channel_id=1, source_target_pairs={{0,2},{1,3},{2,0},{3,1},{4,6},{5,7},{6,4},{7,5},{8,10},{9,11},{10,... | collective-permute-start | bytes 983048 | tf_op jit(solution)/shard_map/ppermute | solution.py:96
  154.6 5.4 %copy-start.8 = (bf16[32,80,128]{2,1,0:T(8,128)(2,1)}, bf16[32,80,128]{2,1,0:T(8,128)(2,1)S(1)}, u32[]{:S(2)}) copy-start(bf16[32,80,128]{2,1,0:T(8,128)(2,1)S(1)} %all-to-all-done.3.got_ref) | copy-start | bytes 1966084
  156.0 7.3 %collective-permute-start.14 = (bf16[2,16,2560]{2,1,0:T(8,128)(2,1)S(1)}, bf16[2,16,2560]{2,1,0:T(8,128)(2,1)S(1)}, u32[]{:S(2)}, u32[]{:S(2)}) collective-permute-start(bf16[2,16,2560]{2,1,0:T(8,128)(2,1)S(1)} %get-tuple-element.76), channel_id=1, source_target_pairs={{0,4},{4,0},{8,12},{12,8},{16,20},{20,16},{24,28},{28,24},{1,5},{5... | collective-permute-start | bytes 491528 | tf_op jit(solution)/shard_map/ppermute | solution.py:96
  158.5 10.3 %copy-start.5 = (bf16[16,128,128]{2,1,0:T(8,128)(2,1)S(1)}, bf16[16,128,128]{2,1,0:T(8,128)(2,1)}, u32[]{:S(2)}) copy-start(bf16[16,128,128]{2,1,0:T(8,128)(2,1)} %copy-done.4) | copy-start | bytes 1572868
  158.6 5.7 %collective-permute-start.15 = (bf16[2,16,2560]{2,1,0:T(8,128)(2,1)S(1)}, bf16[2,16,2560]{2,1,0:T(8,128)(2,1)S(1)}, u32[]{:S(2)}, u32[]{:S(2)}) collective-permute-start(bf16[2,16,2560]{2,1,0:T(8,128)(2,1)S(1)} %get-tuple-element.74), channel_id=1, source_target_pairs={{0,2},{1,3},{2,0},{3,1},{4,6},{5,7},{6,4},{7,5},{8,10},{9,11},{10,... | collective-permute-start | bytes 491528 | tf_op jit(solution)/shard_map/ppermute | solution.py:96
  164.3 12.8 %collective-permute-start.16 = (bf16[16,2560]{1,0:T(8,128)(2,1)S(1)}, bf16[16,2560]{1,0:T(8,128)(2,1)S(1)}, u32[]{:S(2)}, u32[]{:S(2)}) collective-permute-start(bf16[16,2560]{1,0:T(8,128)(2,1)S(1)} %fusion.20), channel_id=1, source_target_pairs={{0,8},{4,12},{8,0},{12,4},{16,24},{20,28},{24,16},{28,20},{1,9},{5... | collective-permute-start | bytes 245768 | tf_op jit(solution)/shard_map/ppermute | solution.py:96
  165.7 11.4 %collective-permute-start.17 = (bf16[16,2560]{1,0:T(8,128)(2,1)S(1)}, bf16[16,2560]{1,0:T(8,128)(2,1)S(1)}, u32[]{:S(2)}, u32[]{:S(2)}) collective-permute-start(bf16[16,2560]{1,0:T(8,128)(2,1)S(1)} %get-tuple-element.79), channel_id=1, source_target_pairs={{0,16},{4,20},{8,24},{12,28},{16,0},{20,4},{24,8},{28,12},{1,17},{... | collective-permute-start | bytes 245768 | tf_op jit(solution)/shard_map/ppermute | solution.py:96
  167.9 9.1 %collective-permute-start.18 = (bf16[16,2560]{1,0:T(8,128)(2,1)S(1)}, bf16[16,2560]{1,0:T(8,128)(2,1)S(1)}, u32[]{:S(2)}, u32[]{:S(2)}) collective-permute-start(bf16[16,2560]{1,0:T(8,128)(2,1)S(1)} %get-tuple-element.80), channel_id=1, source_target_pairs={{0,24},{4,28},{8,16},{12,20},{16,8},{20,12},{24,0},{28,4},{1,25},{... | collective-permute-start | bytes 245768 | tf_op jit(solution)/shard_map/ppermute | solution.py:96
  173.3 14.7 %copy-start.11 = (bf16[16,5134]{1,0:T(8,128)(2,1)S(1)}, bf16[16,5134]{1,0:T(8,128)(2,1)}, u32[]{:S(2)}) copy-start(bf16[16,5134]{1,0:T(8,128)(2,1)} %copy-done.10) | copy-start | bytes 492868
  173.3 14.3 %all-to-all-start.4 = ((f32[32,16,128]{2,1,0:T(8,128)}), f32[32,16,128]{2,1,0:T(8,128)S(1)}, u32[]{:S(2)}, u32[]{:S(2)}) async-start(f32[32,16,128]{2,1,0:T(8,128)} %get-tuple-element.48), calls=%async_computation.4 | async-start | bytes 524288 | tf_op jit(solution)/shard_map/all_to_all | solution.py:78
  177.0 14.6 %copy-start.13 = (f32[16,5134]{1,0:T(8,128)S(1)}, f32[16,5134]{1,0:T(8,128)}, u32[]{:S(2)}) copy-start(f32[16,5134]{1,0:T(8,128)} %param.18) | copy-start | bytes 985732
  177.0 14.5 %copy-start.14 = (f32[16,5134]{1,0:T(8,128)S(1)}, f32[16,5134]{1,0:T(8,128)}, u32[]{:S(2)}) copy-start(f32[16,5134]{1,0:T(8,128)} %param.17) | copy-start | bytes 985732
  191.6 1.1 copy-start.15
  192.6 0.8 copy-start.9

commit v2 on v1

--- a/solution.py
+++ b/solution.py
@@ -24,7 +24,9 @@
 F32 = jnp.float32
 AXES = ("dp", "mode")
 SLOPE = jnp.bfloat16
-VMEM_BYTES = 52 * 1024 * 1024
+VMEM_BYTES = 60 * 1024 * 1024
+FULL_BYTES = 60 * 1024 * 1024
+SMALL_BYTES = 16 * 1024 * 1024
 
 
 def plain(spec, left, right):
@@ -96,23 +98,8 @@
     return lax.ppermute(x, axis, [(index, index ^ step) for index in range(count)])
 
 
-def assemble_kernel(offsets, n_mode, rows, me_ref, *refs):
-    out_ref = refs[-1]
-    for ref, (data, mode) in zip(refs[:-1], offsets, strict=True):
-        for at, (one, two) in enumerate(zip(data, mode, strict=True)):
-            owner = (me_ref[0] ^ one) * n_mode + (me_ref[1] ^ two)
-            out_ref[pl.ds(pl.multiple_of(owner * rows, rows), rows), :] = ref[at]
-
-
-def gather_tiles(x, me):
-    n_data, n_mode = lax.axis_size("dp"), lax.axis_size("mode")
-    deep = [x] + [by_xor(x, "dp", 2 * step) for step in range(1, n_data // 2)]
-    cut = len(deep) // 2
-    first, second = jnp.stack(deep[:cut]), jnp.stack(deep[cut:])
-    first = jnp.concatenate([first, by_xor(first, "dp", 1)])
-    second = jnp.concatenate([second, by_xor(second, "mode", 2)])
-    pieces = [first, by_xor(first, "mode", 2), second, by_xor(second, "dp", 1)]
-    pieces += [by_xor(piece, "mode", 1) for piece in pieces]
+def tile_offsets(n_data):
+    cut = n_data // 4
     low = [2 * step for step in range(cut)]
     high = [2 * step for step in range(cut, 2 * cut)]
     ones = lambda data: [index + 1 for index in data]
@@ -122,16 +109,27 @@
         (high + high, [0] * cut + [2] * cut),
         (ones(high) + ones(high), [0] * cut + [2] * cut),
     ]
-    offsets += [(data, [index + 1 for index in mode]) for data, mode in offsets]
-    whole = pl.BlockSpec(memory_space=pltpu.VMEM)
-    return pl.pallas_call(
-        partial(assemble_kernel, offsets, n_mode, x.shape[0]),
-        out_shape=jax.ShapeDtypeStruct((n_data * n_mode * x.shape[0], x.shape[1]), x.dtype),
-        in_specs=[pl.BlockSpec(memory_space=pltpu.SMEM)] + [whole] * len(pieces),
-        out_specs=whole,
-        compiler_params=pltpu.CompilerParams(vmem_limit_bytes=VMEM_BYTES),
-        name="assemble",
-    )(me, *pieces)
+    return offsets + [(data, [index + 1 for index in mode]) for data, mode in offsets]
+
+
+def gather_tiles_first(x):
+    n_data = lax.axis_size("dp")
+    deep = [x] + [by_xor(x, "dp", 2 * step) for step in range(1, n_data // 2)]
+    cut = len(deep) // 2
+    return jnp.stack(deep[:cut]), jnp.stack(deep[cut:])
+
+
+def gather_tiles_second(first, second):
+    first = jnp.concatenate([first, by_xor(first, "dp", 1)])
+    return first, jnp.concatenate([second, by_xor(second, "mode", 2)])
+
+
+def gather_tiles_third(first, second):
+    return [first, by_xor(first, "mode", 2), second, by_xor(second, "dp", 1)]
+
+
+def gather_tiles_last(pieces):
+    return pieces + [by_xor(piece, "mode", 1) for piece in pieces]
 
 
 def tile_order(n_data):
@@ -151,32 +149,35 @@
     return lax.optimization_barrier(values)
 
 
-def add(left, right):
-    return (left.astype(F32) + right.astype(F32)).astype(BF)
+def total_of(terms, pick):
+    return sum(term[pick].astype(F32) for term in terms)
 
 
 def scatter_tiles_first(away, stay):
-    pairs = lambda x: x.reshape((x.shape[0] // 2, 2) + x.shape[1:])
-    come = by_xor(away, "mode", 1)
-    groups = [add(come[g], stay[g]) for g in range(4)]
-    first = by_xor(groups[0], "mode", 2)
-    second = by_xor(groups[2], "dp", 1)
-    return [pairs(x) for x in (first, groups[1], second, groups[3])]
-
-
-def scatter_tiles_second(one, two, three, four):
-    first_come = by_xor(add(one[:, 1], two[:, 1]), "dp", 1)
-    second_come = by_xor(add(three[:, 1], four[:, 1]), "mode", 2)
-    return [first_come, add(one[:, 0], two[:, 0]), second_come, add(three[:, 0], four[:, 0])]
-
-
-def scatter_tiles_third(one, two, three, four):
-    cut = one.shape[0]
-    total = one[0].astype(F32) + two[0].astype(F32)
+    terms = [stay, by_xor(away, "mode", 1)]
+    first = by_xor(total_of(terms, 0).astype(BF), "mode", 2)
+    second = by_xor(total_of(terms, 2).astype(BF), "dp", 1)
+    return [terms[0], terms[1], first, second]
+
+
+def scatter_tiles_second(stay, come, first, second):
+    pairs = lambda terms: [x.reshape((x.shape[0] // 2, 2) + x.shape[1:]) for x in terms]
+    first = pairs([stay[1], come[1], first])
+    second = pairs([stay[3], come[3], second])
+    halves = (slice(None), 1)
+    return [
+        [x[:, 0] for x in first] + [by_xor(total_of(first, halves).astype(BF), "dp", 1)],
+        [x[:, 0] for x in second] + [by_xor(total_of(second, halves).astype(BF), "mode", 2)],
+    ]
+
+
+def scatter_tiles_third(first, second):
+    cut = first[0].shape[0]
+    come = []
     for step in range(1, 2 * cut):
-        left, right, at = (one, two, step) if step < cut else (three, four, step - cut)
-        total += by_xor(add(left[at], right[at]), "dp", 2 * step).astype(F32)
-    return total
+        terms, at = (first, step) if step < cut else (second, step - cut)
+        come.append(by_xor(total_of(terms, at).astype(BF), "dp", 2 * step))
+    return [total_of(first, 0)] + come
 
 
 def gather_rows(x):
@@ -209,7 +210,8 @@
 TN = (((0,), (0,)), ((), ()))
 FIRST = 2.0 * math.sqrt(2.0 / math.pi)
 THIRD = FIRST * 0.044715
-GATES = 256
+GATES = 512
+UNROLL = 4
 LEAD = 8
 HALF = 64
 
@@ -250,12 +252,57 @@
     return sum(x[at : at + LEAD] for at in range(0, x.shape[0], LEAD))
 
 
-def block_kernel(
+def block_kernel(sizes, count_ref, me_ref, *refs):
+    if len(sizes) == 4:
+        block_steps(sizes, lambda what: None, count_ref, *refs)
+        return
+    n_data, n_mode = sizes[:2]
+    rows = D // n_data // n_mode
+    offsets = tile_offsets(n_data)
+    n_pieces = len(offsets)
+    pieces, got_ref, sources, refs = refs[:n_pieces], refs[n_pieces], refs[n_pieces + 1 : n_pieces + 7], refs[n_pieces + 7 :]
+    send_ref, stat_ref, away_ref, stay_ref, row_sems, sems, w_ref = refs[:7]
+    places, scratch = refs[7:13], refs[13:]
+    act_ref = scratch[5]
+
+    def rows_of(data, mode):
+        owner = (me_ref[0] ^ data) * n_mode + (me_ref[1] ^ mode)
+        return pl.ds(pl.multiple_of(owner * rows, rows), rows)
+
+    row_copies = []
+    for ref, (data, mode) in zip(pieces, offsets, strict=True):
+        for at, (one, two) in enumerate(zip(data, mode, strict=True)):
+            place = w_ref.at[rows_of(one, two), :]
+            row_copies.append(
+                pltpu.make_async_copy(ref.at[at], place, row_sems.at[len(row_copies)])
+            )
+            row_copies[-1].start()
+    copies = [
+        pltpu.make_async_copy(source, place, sems.at[at])
+        for at, (source, place) in enumerate(zip(sources, places, strict=True))
+    ]
+    for copy in copies:
+        copy.start()
+    waits = {"rows": row_copies, "a": copies[:1], "rest": copies[1:]}
+
+    def ready(what):
+        for copy in waits[what]:
+            copy.wait()
+
+    block_steps(sizes, ready, count_ref, w_ref, got_ref, *places, send_ref, stat_ref, None, *scratch)
+    for at, group in enumerate(tile_order(n_data)):
+        ref = away_ref if at < 4 else stay_ref
+        for index, (data, mode) in enumerate(group):
+            ref[at % 4, index, :, :D] = act_ref[1, rows_of(data, mode), :D]
+            ref[at % 4, index, :, D:] = act_ref[0, rows_of(data, mode), :]
+
+
+def block_steps(
     sizes,
+    ready,
     count_ref,
-    me_ref,
+    w_ref,
     got_ref,
-    w_ref,
     a_ref,
     at_ref,
     rest_ref,
@@ -264,53 +311,7 @@
     keep_ref,
     send_ref,
     stat_ref,
-    *refs,
-):
-    if len(sizes) > 4:
-        away_ref, stay_ref, big_ref, *refs = refs
-    else:
-        big_ref, *refs = refs
-    block_steps(
-        sizes,
-        count_ref,
-        got_ref,
-        w_ref,
-        a_ref,
-        at_ref,
-        rest_ref,
-        rest_t_ref,
-        target_ref,
-        keep_ref,
-        send_ref,
-        big_ref,
-        stat_ref,
-        *refs,
-    )
-    if len(sizes) > 4:
-        n_data, n_mode = sizes[:2]
-        rows = D // n_data // n_mode
-        order = tile_order(n_data)
-        for at, group in enumerate(order):
-            ref = away_ref if at < 4 else stay_ref
-            for index, (data, mode) in enumerate(group):
-                owner = (me_ref[0] ^ data) * n_mode + (me_ref[1] ^ mode)
-                ref[at % 4, index] = big_ref[pl.ds(pl.multiple_of(owner * rows, rows), rows), :]
-
-
-def block_steps(
-    sizes,
-    count_ref,
-    got_ref,
-    w_ref,
-    a_ref,
-    at_ref,
-    rest_ref,
-    rest_t_ref,
-    target_ref,
-    keep_ref,
-    send_ref,
     big_ref,
-    stat_ref,
     wdup_ref,
     x_ref,
     v_ref,
@@ -333,17 +334,31 @@
     chunks = FF // GATES
 
     for i in range(n_data):
-        head = i * H // n_data
-        block = w_ref[head * E : (head + 1) * E, :D]
-        wdup_ref[2 * i * E : (2 * i + 1) * E, :] = block
-        wdup_ref[(2 * i + 1) * E : (2 * i + 2) * E, :] = block
-    for i in range(n_data):
         blocks = [got_ref[i * n_mode + j, :nbm, :].astype(F32) for j in range(n_mode)]
         for k in range(nb):
             column = [block[k * modes : (k + 1) * modes] for block in blocks]
             x_ref[k * M : (k + 1) * M, i * LANES : (i + 1) * LANES] = jnp.concatenate(
                 column, axis=0
             ).astype(BF)
+
+    per = LANES // share
+    for at in range(FF // LANES):
+        block = jnp.zeros((16, LANES), F32)
+        for q in range(per):
+            piece = got_ref[at * per + q, nbm : nbm + 16, :].astype(F32)
+            piece = pltpu.roll(piece, q * share, 1) if q else piece
+            block = jnp.where(iota(block.shape, 1) // share == q, piece, block)
+        spread = [
+            rows_at(jnp.concatenate([half] * nb, axis=0), 0, HALF)
+            for half in (block[:LEAD], block[LEAD:])
+        ]
+        wd_ref[:, at * LANES : (at + 1) * LANES] = jnp.concatenate(spread, axis=0).astype(BF)
+    ready("rows")
+    for i in range(n_data):
+        head = i * H // n_data
+        block = w_ref[head * E : (head + 1) * E, :D]
+        wdup_ref[2 * i * E : (2 * i + 1) * E, :] = block
+        wdup_ref[(2 * i + 1) * E : (2 * i + 2) * E, :] = block
     x_all = x_ref[...]
     real_lane = iota(x_all.shape, 1) % LANES < HALF
     zero = jnp.zeros_like(x_all)
@@ -363,20 +378,6 @@
     head_all = jnp.concatenate([head_t] * nb + pad, axis=0).astype(BF)
     head_twice = jnp.concatenate([head_all, head_all], axis=0)
     embed_twice = jnp.concatenate([embed_t, embed_t], axis=0).astype(BF)
-
-    per = LANES // share
-    for at in range(FF // LANES):
-        block = jnp.zeros((16, LANES), F32)
-        for q in range(per):
-            piece = got_ref[at * per + q, nbm : nbm + 16, :].astype(F32)
-            piece = pltpu.roll(piece, q * share, 1) if q else piece
-            block = jnp.where(iota(block.shape, 1) // share == q, piece, block)
-        for k in range(nb):
-            spread = jnp.concatenate(
-                [rows_at(block[:LEAD], k * LEAD, HALF), rows_at(block[LEAD:], k * LEAD, HALF)],
-                axis=0,
-            )
-            wd_ref[k, :, at * LANES : (at + 1) * LANES] = spread.astype(BF)
 
     for c in range(FF // 512):
         cols = slice(c * 512, (c + 1) * 512)
@@ -396,7 +397,10 @@
     cross = jnp.where(iota(cross.shape, 0) // LEAD == iota(cross.shape, 1) // LEAD, cross, 0.0)
     high, low = split(jnp.concatenate([by_head, cross], axis=1))
     by_head = jnp.concatenate([high, low], axis=0).astype(BF)
+    ready("a")
     fc_ref[...] = mm(a_ref[...], by_head, NT)
+
+    own_lane = iota((S, LANES), 1) % HALF // LEAD
 
     def forward(step, carry):
         k = step // chunks
@@ -409,11 +413,12 @@
         act_ref[k, :, cols] = low
         slope = sig + act * (1.0 - sig) * (square * (3.0 * THIRD) + FIRST)
         slope_ref[k, :, cols] = slope.astype(slope_ref.dtype)
-        fc_ref[...] += mm(low, wd_ref[k, :, cols], NT)
+        fc_ref[...] += jnp.where(own_lane == k, mm(low, wd_ref[:, cols], NT), 0.0)
         return carry
 
-    lax.fori_loop(0, nb * chunks, forward, 0)
-
+    lax.fori_loop(0, nb * chunks, forward, 0, unroll=UNROLL)
+
+    ready("rest")
     keep = keep_ref[...]
     masked = keep * (fold(fc_ref[...]) - target_ref[...])
     two = by_halves(masked)
@@ -431,14 +436,13 @@
     g_fc = keep * ((2.0 / count_ref[0]) * masked + (2.0 * norm) * back)
     g_low = g_fc.astype(BF)
     g_turn = g_fc.T[:HALF].astype(BF)
-    fc_ref[...] = g_fc
     zx_ref[...] = jnp.zeros_like(zx_ref)
     j_ref[...] = jnp.zeros_like(j_ref)
 
     def backward(step, carry):
         k = step // chunks
         cols = pl.ds(pl.multiple_of(step % chunks * GATES, GATES), GATES)
-        fed = mm(g_low, wd_ref[k, :, cols])
+        fed = mm(jnp.where(own_lane == k, g_fc, 0.0).astype(BF), wd_ref[:, cols])
         g_gate = (fed * slope_ref[k, :, cols].astype(F32)).astype(BF)
         turned = mm(at_ref[...], g_gate)
         r_ref[k, : 2 * M, cols] = turned[: 2 * M].astype(BF)
@@ -447,7 +451,7 @@
         j_ref[:, cols] += jnp.where(own, mm(g_turn, act_ref[k, :, cols]), 0.0)
         return carry
 
-    lax.fori_loop(0, nb * chunks, backward, 0)
+    lax.fori_loop(0, nb * chunks, backward, 0, unroll=UNROLL)
 
     back_fc = by_halves(mm(at_ref[...], g_low))
     lane_of = iota((2 * M, LANES), 1) % HALF // LEAD
@@ -514,36 +518,52 @@
         block = 0.0
         for i in range(head * each, (head + 1) * each):
             block += out_grad[2 * i * E : (2 * i + 1) * E] + out_grad[(2 * i + 1) * E : (2 * i + 2) * E]
-        big_ref[head * E : (head + 1) * E, :D] = block.astype(BF)
+        out = act_ref.at[1] if big_ref is None else big_ref
+        out[head * E : (head + 1) * E, :D] = block.astype(BF)
     for c in range(FF // 512):
         cols = slice(c * 512, (c + 1) * 512)
         up_grad = mm(v_all, z_all[:, cols], TN) + mm(embed_twice, zx[:, cols], TN)
-        big_ref[:, D + c * 512 : D + (c + 1) * 512] = up_grad.astype(BF)
-
-
-def block(count, me, got, weights, a, at, rest, rest_t, target, keep, sizes):
+        if big_ref is None:
+            act_ref[0, :D, cols] = up_grad.astype(BF)
+        else:
+            big_ref[:, D + c * 512 : D + (c + 1) * 512] = up_grad.astype(BF)
+
+
+def block(count, me, weights, ins, sizes):
     n_data, n_mode, nb = sizes[:3]
+    tiled = len(sizes) > 4
     whole = pl.BlockSpec(memory_space=pltpu.VMEM)
+    far = pl.BlockSpec(memory_space=pl.ANY if tiled else pltpu.VMEM)
     big = [jax.ShapeDtypeStruct((D, D + FF), BF)]
-    if len(sizes) > 4:
+    scratch = []
+    if tiled:
         half = (4, n_data * n_mode // 8, D // n_data // n_mode, D + FF)
         big = [jax.ShapeDtypeStruct(half, BF)] * 2
+        scratch = [
+            pltpu.SemaphoreType.DMA((n_data * n_mode,)),
+            pltpu.SemaphoreType.DMA((6,)),
+            pltpu.VMEM((D, D + FF + LANES), BF),
+        ]
+        scratch += [pltpu.VMEM(x.shape, x.dtype) for x in ins[1:]]
     return pl.pallas_call(
         partial(block_kernel, sizes),
         out_shape=(
-            jax.ShapeDtypeStruct(got.shape, BF),
+            jax.ShapeDtypeStruct(ins[0].shape, BF),
             jax.ShapeDtypeStruct((8, LANES), F32),
             *big,
         ),
-        in_specs=[pl.BlockSpec(memory_space=pltpu.SMEM)] * 2 + [whole] * 8,
+        in_specs=[pl.BlockSpec(memory_space=pltpu.SMEM)] * 2
+        + [far] * len(weights)
+        + [whole]
+        + [far] * (len(ins) - 1),
         out_specs=(whole,) * (2 + len(big)),
-        scratch_shapes=([pltpu.VMEM((D, D + FF), BF)] if len(sizes) > 4 else [])
+        scratch_shapes=scratch
         + [
             pltpu.VMEM((2 * n_data * E, D), BF),
             pltpu.VMEM((nb * M, n_data * LANES), BF),
             pltpu.VMEM((nb * 2 * M, D), BF),
             pltpu.VMEM((nb, 4 * M, FF), BF),
-            pltpu.VMEM((nb, LANES, FF), BF),
+            pltpu.VMEM((LANES, FF), BF),
             pltpu.VMEM((nb, S, FF), BF),
             pltpu.VMEM((nb, S, FF), SLOPE),
             pltpu.VMEM((S, LANES), F32),
@@ -552,7 +572,7 @@
         ],
         compiler_params=pltpu.CompilerParams(vmem_limit_bytes=VMEM_BYTES),
         name="block",
-    )(count, me, got, weights, a, at, rest, rest_t, target, keep)
+    )(count, me, *weights, *ins)
 
 
 def at_lane(x, first, width):
@@ -569,36 +589,96 @@
     return jnp.where(iota(x.shape, 1) < width, x, 0.0)
 
 
-def call(kernel, outs, ins, scratch=(), name=None):
+def staged(kernel, ahead, *refs):
+    sems = refs[-1]
+    n_held = len(refs) - 1 - len(ahead)
+    held = list(refs[:n_held])
+    copies = []
+    for at, (index, place) in enumerate(zip(ahead, refs[n_held:-1], strict=True)):
+        copies.append(pltpu.make_async_copy(refs[index], place, sems.at[at]))
+        copies[-1].start()
+        held[index] = place
+
+    def ready():
+        for copy in copies:
+            copy.wait()
+
+    kernel(ready, *held)
+
+
+def call(kernel, outs, ins, scratch=(), name=None, cost=0, ahead=()):
     whole = pl.BlockSpec(memory_space=pltpu.VMEM)
+    in_specs = [whole] * len(ins)
+    scratch = list(scratch)
+    if ahead:
+        kernel = partial(staged, kernel, ahead)
+        for index in ahead:
+            in_specs[index] = pl.BlockSpec(memory_space=pl.ANY)
+            scratch.append(pltpu.VMEM(ins[index].shape, ins[index].dtype))
+        scratch.append(pltpu.SemaphoreType.DMA((len(ahead),)))
     return pl.pallas_call(
         kernel,
         out_shape=outs,
-        in_specs=[whole] * len(ins),
+        in_specs=in_specs,
         out_specs=jax.tree.map(lambda _: whole, outs),
-        scratch_shapes=list(scratch),
-        compiler_params=pltpu.CompilerParams(vmem_limit_bytes=VMEM_BYTES),
+        scratch_shapes=scratch,
+        compiler_params=pltpu.CompilerParams(vmem_limit_bytes=FULL_BYTES if ahead else SMALL_BYTES),
         name=name,
+        cost_estimate=pl.CostEstimate(flops=cost, bytes_accessed=cost // 10, transcendentals=0)
+        if cost
+        else None,
     )(*ins)
 
 
-def spectra_kernel(sizes, x_ref, keep_ref, low_ref, dense_ref, send_ref):
+def thin_rows(dense_ref):
+    thin = dense_ref[:, 2 * D + 2 * FF :]
+    thin = jnp.concatenate([thin, jnp.zeros((thin.shape[0], LANES - 2 * C), F32)], axis=1)
+    return at_lane(thin, 0, C) + at_lane(from_lane(thin, C, C), LEAD, C)
+
+
+def pack_kernel(sizes, ready, series_ref, future_ref, mask_ref, dense_ref, send_ref, rows_ref, one_ref, two_ref):
+    n_mode, nb = sizes[1:3]
+    ready()
+    one_ref[...] = series_ref[...].astype(F32)
+    two_ref[...] = mask_ref[...].astype(F32)
+    for j in range(n_mode):
+        for k in range(nb):
+            b = j * nb + k
+            for c in range(C):
+                send_ref[j, k * LEAD + c, :] = one_ref[c, b, :]
+                send_ref[j, (nb + k) * LEAD + c, :] = future_ref[c, b, :]
+            send_ref[j, k * LEAD + C, :] = two_ref[b, :]
+            send_ref[j, (nb + k) * LEAD + C, :] = jnp.zeros_like(two_ref[b, :])
+    rows_ref[:, : D + FF] = dense_ref[:, D : 2 * D + FF].astype(BF)
+    rows_ref[:, D + FF :] = thin_rows(dense_ref).astype(BF)
+
+
+def own_rows(got_ref, all_ref):
+    steps = got_ref.shape[2]
+    for j in range(got_ref.shape[0]):
+        all_ref[:, j * steps : (j + 1) * steps] = got_ref[j]
+    half = all_ref.shape[0] // 2
+    inputs = all_ref[:half, :]
+    mask = inputs
+    inputs = jnp.where(iota(inputs.shape, 0) % LEAD == C, 0.0, inputs)
+    return inputs, mask, all_ref[half:, :]
+
+
+def spectra_kernel(sizes, got_ref, cos_ref, sin_ref, dense_ref, send_ref, all_ref):
     n_data, n_mode, nb, _ = sizes
     n_all = n_data * n_mode
     modes = M // n_mode
     wide = D // n_data
     share = FF // n_all
-    x = x_ref[...].astype(F32)
-    x = jnp.concatenate([x, jnp.zeros_like(x)], axis=1)
-    inner = mm(low_ref[:M, :], x.astype(BF))
-    inner += mm(low_ref[M:, :], pltpu.roll(x, nb * LEAD, 1).astype(BF))
-    thin = dense_ref[:, 2 * D + 2 * FF :]
-    thin = jnp.concatenate([thin, jnp.zeros((thin.shape[0], LANES - 2 * C), F32)], axis=1)
-    thin = at_lane(thin, 0, C) + at_lane(from_lane(thin, C, C), LEAD, C)
-    thin = thin.astype(BF)
+    x, mask, _ = own_rows(got_ref, all_ref)
+    count = jnp.sum(jnp.where(iota(mask.shape, 0) % LEAD == C, mask, 0.0))
+    low = cos_ref[...].astype(BF)
+    inner = mm(low, rows_at(x, 0, LANES).astype(BF), NT)
+    low = (-sin_ref[...]).astype(BF)
+    inner += mm(low, rows_at(x, nb * LEAD, LANES).astype(BF), NT)
+    thin = thin_rows(dense_ref).astype(BF)
     query = mm(thin, dense_ref[:, :D].astype(BF), TN)[:LEAD]
     down = mm(thin, dense_ref[:, 2 * D + FF : 2 * D + 2 * FF].astype(BF), TN)[LEAD : 2 * LEAD]
-    count = jnp.sum(keep_ref[...]) * (0.5 / LEAD)
     row = iota((LEAD, LANES), 0)
     lane = iota((LEAD, LANES), 1)
     for i in range(n_data):
@@ -611,6 +691,30 @@
                 block = jnp.concatenate([block, jnp.zeros((16 - modes, LANES), F32)], axis=0)
             theirs = at_lane(from_lane(down, d * share, share), HALF, share)
             send_ref[d] = block + jnp.concatenate([ours, theirs], axis=0)
+
+
+def tables_kernel(
+    got_ref, cos_ref, sin_ref, a_ref, at_ref, rest_ref, rest_t_ref, target_ref, keep_ref, all_ref
+):
+    x, mask, target = own_rows(got_ref, all_ref)
+    count = x.shape[0]
+    keep = [
+        jnp.broadcast_to(mask[at + C : at + LEAD], (LEAD, S)) for at in range(0, count, LEAD)
+    ]
+    keep = jnp.concatenate(keep, axis=0)
+    twice = lambda rows: jnp.concatenate([rows_at(rows, 0, HALF)] * 2, axis=0).T
+    a_ref[:, 2 * M :] = twice(x).astype(BF)
+    at_ref[2 * M :, :] = rows_at(x, 0, HALF).astype(BF)
+    target_ref[...] = twice(target)
+    keep_ref[...] = twice(keep)
+    basis = jnp.concatenate([cos_ref[...], -sin_ref[...]], axis=0)
+    low = basis.astype(BF)
+    at_ref[: 2 * M, :] = low
+    rest_ref[...] = (basis - low.astype(F32)).astype(BF)
+    turned = basis.T
+    low = turned.astype(BF)
+    a_ref[:, : 2 * M] = low
+    rest_t_ref[...] = (turned - low.astype(F32)).astype(BF)
 
 
 def mix_kernel(sizes, got_ref, mixer_ref, send_ref, spec_ref, thin_ref, wide_ref, out_ref):
@@ -703,6 +807,7 @@
 def spectral_kernel(
     modes,
     wide,
+    ready,
     spec_ref,
     grad_ref,
     w_ref,
@@ -717,6 +822,7 @@
     pair_ref,
     turn_ref,
 ):
+    ready()
     lower = iota((wide, LANES), 1) < HALF
     half_lower = iota((wide // 2, LANES), 1) < HALF
     for m in range(modes):
@@ -745,6 +851,75 @@
                 ref[part, :, cols] = value
 
 
+def rows_kernel(
+    sizes,
+    n_big,
+    got_ref,
+    thin_ref,
+    steps_ref,
+    w_ref,
+    m_ref,
+    v_ref,
+    ema_ref,
+    *refs,
+):
+    big_refs, (loss_ref, w_out, m_out, v_out, ema_out, low_out) = refs[:n_big], refs[n_big:]
+    n_data, n_mode, _, total = sizes
+    n_all = n_data * n_mode
+    wide = D // n_data
+    share = FF // n_all
+    rows = w_ref.shape[0]
+    query = []
+    for at in range(D // LANES):
+        block = jnp.zeros((LEAD, LANES), F32)
+        for i in range(at * LANES // wide, (at + 1) * LANES // wide):
+            part = sum(got_ref[i * n_mode + j, :LEAD, :] for j in range(n_mode))
+            block += at_lane(part, i * wide % LANES, wide)
+        query.append(block)
+    query = jnp.concatenate(query, axis=1)
+    down = []
+    for at in range(FF // LANES):
+        block = jnp.zeros((LEAD, LANES), F32)
+        for d in range(at * LANES // share, (at + 1) * LANES // share):
+            block += at_lane(from_lane(got_ref[d, :LEAD, :], HALF, share), d * share % LANES, share)
+        down.append(block)
+    down = jnp.concatenate(down, axis=1)
+    norm = SPECTRAL_WEIGHT / (total * M * S)
+    stats = sum(got_ref[d, LEAD:, :] for d in range(n_all))
+    loss_ref[...] = stats[:1, :1] / steps_ref[C : C + 1, HALF : HALF + 1] + norm * stats[1:2, :1]
+
+    keep = iota((LEAD, D), 0) < C
+    query = jnp.where(keep, query, 0.0)
+    query = jnp.concatenate(split(query), axis=0).astype(BF)
+    down = jnp.concatenate(split(down), axis=0).astype(BF)
+    thin = thin_rows(w_ref)
+    embed = at_lane(thin, 0, C) + at_lane(from_lane(thin, 0, C), LEAD, C)
+    head = from_lane(thin, LEAD, C)
+    head = at_lane(head, 0, C) + at_lane(head, LEAD, C)
+
+    def back(weights, sums):
+        sums = jnp.concatenate([sums, jnp.zeros((LANES - 16, sums.shape[1]), BF)], axis=0)
+        out = mm(weights.astype(BF), sums, NT)
+        return from_lane(out, 0, LEAD) + from_lane(out, LEAD, LEAD)
+
+    own = jnp.concatenate([thin_ref[...], jnp.zeros((LANES - LEAD, LANES), F32)], axis=0).T
+    embed_grad = own[HALF : HALF + rows] + back(w_ref[:, :D], query)
+    head_grad = own[HALF + rows : HALF + 2 * rows] + back(
+        w_ref[:, 2 * D + FF : 2 * D + 2 * FF], down
+    )
+    last = at_lane(embed_grad, 0, C) + at_lane(head_grad, C, C)
+
+    def update(grad, cols):
+        new = adamw(w_ref[:, cols], grad, m_ref[:, cols], v_ref[:, cols], ema_ref[:, cols], RATE_DENSE)
+        for ref, value in zip((w_out, m_out, v_out, ema_out, low_out), new, strict=True):
+            ref[:, cols] = value
+
+    update(mm(embed[:, :16].astype(BF), query), slice(0, D))
+    update(sum(ref[...].astype(F32) for ref in big_refs), slice(D, 2 * D + FF))
+    update(mm(head[:, :16].astype(BF), down), slice(2 * D + FF, 2 * D + 2 * FF))
+    update(last[:, : 2 * C], slice(2 * D + 2 * FF, 2 * D + 2 * FF + 2 * C))
+
+
 def per_device(
     series,
     future_values,
@@ -767,52 +942,54 @@
     total = batch * n_data
     modes = M // n_mode
     wide = D // n_data
-    share = FF // n_all
     rows = dense.shape[0]
-    msg_rows = max(modes, 16)
-
-    packed = jnp.concatenate(
-        [series.astype(F32), future_values, step_mask.astype(F32)[..., None]], axis=2
-    )
-    packed = packed.reshape(time_rows, n_mode, nb, 2 * chans + 1).transpose(1, 0, 2, 3)
-    packed = exchange(packed, "mode").reshape(S, nb, 2 * chans + 1)
-    x_in = packed[..., :chans].astype(BF)
-    target = packed[..., chans : 2 * chans]
-    keep = packed[..., 2 * chans :]
-
-    cosv, sinv = tables(mode_index)
-    basis = jnp.concatenate([cosv, -sinv], axis=0)
-    low = basis.astype(BF)
-    rest = (basis - low.astype(F32)).astype(BF)
-
-    def lanes(x):
-        return fill(fill(x, LEAD, 2).reshape(S, nb * LEAD), HALF, 1)
-
-    x_lanes = lanes(x_in)
-    a = jnp.concatenate([low.T, x_lanes, x_lanes], axis=1)
-    a_turn = jnp.concatenate([low, x_lanes.T], axis=0)
-    target = jnp.concatenate([lanes(target)] * 2, axis=1)
-    keep_lanes = lanes(jnp.broadcast_to(keep, (S, nb, LEAD)))
-    keep_lanes = jnp.concatenate([keep_lanes] * 2, axis=1)
-
-    mine = dense.astype(BF)
-    q_rows, o_rows, u_rows, d_rows, e_rows, h_rows = unpack(mine)
+    shape = jax.ShapeDtypeStruct
     sizes = (n_data, n_mode, nb, total)
     tiled = rows % 16 == 0 and n_mode == 4 and n_data >= 4
+
+    send, weights = call(
+        partial(pack_kernel, sizes),
+        (shape((n_mode, 2 * nb * LEAD, time_rows), F32), shape((rows, D + FF + LANES), BF)),
+        (series.transpose(2, 1, 0), future_values.transpose(2, 1, 0), step_mask.T, dense),
+        [pltpu.VMEM((chans, batch, time_rows), F32), pltpu.VMEM((batch, time_rows), F32)],
+        name="pack",
+        ahead=(0, 1, 2, 3),
+    )
     me = jnp.stack([lax.axis_index("dp"), lax.axis_index("mode")]).astype(jnp.int32)
-    weights = jnp.concatenate(
-        [o_rows, u_rows, fill(e_rows, LEAD, 1), fill(h_rows, LANES - LEAD, 1)], axis=1
-    )
-    weights = gather_tiles(weights, me) if tiled else gather_rows(weights)
-
-    shape = jax.ShapeDtypeStruct
+    own = exchange(send, "mode")
+    cosv, sinv = tables(mode_index)
+    weights = [gather_rows(weights)] if not tiled else gather_tiles_first(weights)
+    if tiled:
+        own, *weights = together(own, *weights)
+        weights = gather_tiles_second(*weights)
+
+    whole_rows = [pltpu.VMEM((2 * nb * LEAD, S), F32)]
     send = call(
         partial(spectra_kernel, sizes),
         shape((n_all, 16, LANES), F32),
-        (x_lanes, keep_lanes, low, dense),
+        (own, cosv, sinv, dense),
+        whole_rows,
         name="spectra",
     )
     first = exchange(send, AXES)
+    ins = call(
+        tables_kernel,
+        (
+            shape((S, 4 * M), BF),
+            shape((3 * M, S), BF),
+            shape((2 * M, S), BF),
+            shape((S, 2 * M), BF),
+            shape((S, LANES), F32),
+            shape((S, LANES), F32),
+        ),
+        (own, cosv, sinv),
+        whole_rows,
+        name="tables",
+        cost=10**10,
+    )
+    first, *ins = together(first, *ins)
+    if tiled:
+        weights = gather_tiles_third(*weights)
 
     w_low = spectral.astype(BF).reshape(2, modes, wide, E)
     mixer = jnp.concatenate(
@@ -837,20 +1014,17 @@
         scratch,
         name="mix",
     )
-    steps_total = thin[7, HALF]
+    if tiled:
+        send, *weights = together(send, *weights)
+        weights = gather_tiles_last(weights)
     got = exchange(send, AXES)
+    steps = thin
 
     send, stats, *big = block(
-        steps_total.reshape(1),
+        steps[C, HALF].reshape(1),
         me,
-        got,
         weights,
-        a,
-        a_turn,
-        rest,
-        rest.T,
-        target,
-        keep_lanes,
+        (got, *ins),
         sizes + (True,) if tiled else sizes,
     )
     got = exchange(send, AXES)
@@ -868,9 +1042,10 @@
         (got, mixer, first, stats),
         scratch[::-1],
         name="mix_back",
-    )
-    embed_own = thin[:C, HALF : HALF + rows].T
-    head_own = thin[:C, HALF + rows : HALF + 2 * rows].T
+        cost=10**10,
+    )
+    if tiled:
+        grad_mixed, big = together(grad_mixed, big)
     spec_out = call(
         partial(spectral_kernel, modes, wide),
         (shape(spectral.shape, F32),) * 4 + (shape(spectral.shape, BF),),
@@ -880,30 +1055,18 @@
             pltpu.VMEM((2, modes * wide // 2, LANES), F32),
         ],
         name="spectral",
-    )
-    if tiled:
-        send, *big = together(send, *big)
+        ahead=(0, 1, 2, 3, 4, 5),
+        cost=10**10,
+    )
     got = exchange(send, AXES)
-    big_sum = scatter_tiles_third(*big) if tiled else scatter_rows(big[0], rows)
-    query_total = jnp.sum(got[:, :chans, :wide].reshape(n_data, n_mode, chans, wide), axis=1)
-    query_total = query_total.transpose(1, 0, 2).reshape(chans, D)
-    down_total = got[:, :chans, 64 : 64 + share].transpose(1, 0, 2).reshape(chans, FF)
-    spec_norm = SPECTRAL_WEIGHT / (total * M * S)
-    loss = jnp.sum(got[:, 8, 0]) / steps_total + spec_norm * jnp.sum(got[:, 9, 0])
-
-    up = lambda x: x.astype(F32)
-    dense_sum = jnp.concatenate(
-        [
-            exact("rc,ce->re", up(e_rows), query_total),
-            big_sum,
-            exact("rc,cf->rf", up(h_rows), down_total),
-            embed_own + exact("re,ce->rc", up(q_rows), query_total),
-            head_own + exact("rf,cf->rc", up(d_rows), down_total),
-        ],
-        axis=1,
-    )
-    dense_out = adamw(dense, dense_sum, dense_m, dense_v, dense_ema, RATE_DENSE)
-    return (loss,) + tuple(dense_out) + tuple(spec_out)
+    big = scatter_tiles_third(*big) if tiled else [scatter_rows(big[0], rows)]
+    loss, *dense_out = call(
+        partial(rows_kernel, sizes, len(big)),
+        (shape((1, 1), F32),) + (shape(dense.shape, F32),) * 4 + (shape(dense.shape, BF),),
+        (got, thin, steps, dense, dense_m, dense_v, dense_ema, *big),
+        name="rows",
+    )
+    return (loss.reshape(()),) + tuple(dense_out) + tuple(spec_out)
 
 
 def solution(mesh):

time: 196 us -> 154 us (0.79)
  Pallas kernels: 68.9 us -> 54.1 us
  other arithmetic: 19.7 us -> 5.16 us
  local copies, waits for them, and re-layouts: 14.5 us -> 10.1 us
  between operations: 4.27 us -> 1.07 us
    pallas_call x1, Pallas kernels: 53.4 us -> 38 us  [block(): pl.pallas_call(partial(block_kernel, sizes), out_shape=(jax.ShapeDtypeStr...]
    concatenate x5 -> x0, other arithmetic: 5.56 us -> none  [the longest x1 1.88 us: per_device(): target = jnp.concatenate([lanes(target)] * 2, axis=1)]
    concatenate x8 -> x2, local copies, waits for them, and re-layouts: 5.33 us -> 0.04 us  [the longest x1 0.02 us: gather_tiles_second(): return (first, jnp.concatenate([second, by_xor(second, 'mode', 2)]))]
    convert_element_type x9 -> x3, other arithmetic: 8.19 us -> 3.12 us  [the longest x1 2.06 us: scatter_tiles_first(): second = by_xor(total_of(terms, 2).astype(BF), 'dp', 1)]
    unnamed x37 -> x48, local copies, waits for them, and re-layouts: 2.78 us -> 6.81 us
    ppermute x19, waiting for transfers between devices: 12.9 us -> 9.37 us  [by_xor(): lax.ppermute(x, axis, [(index, index ^ step) for index in range(count)])]
    reshape x8 -> x0, local copies, waits for them, and re-layouts: 2.41 us -> none  [the longest x5 2.01 us: lanes(): return fill(fill(x, LEAD, 2).reshape(S, nb * LEAD), HALF, 1)]
    another operation x2, other arithmetic: 2.27 us -> 0.05 us  [gather_tiles_first(): return (jnp.stack(deep[:cut]), jnp.stack(deep[cut:]))]
  transfers between devices with their start and end apart: 24 -> 24, of which waited for: 8 -> 10; matrix products, arithmetic and copies ran while one was open for 13% -> 3% of each run, Pallas kernels for 8% -> 8%
where the time goes in v2:
time: 154 us
  Pallas kernels  54.1 us (35%)
  starting transfers between devices  41.9 us (27%)
  waiting for transfers between devices  41.3 us (27%)
  local copies, waits for them, and re-layouts  10.1 us (7%)
  other arithmetic  5.16 us (3%)
    pallas_call x1, Pallas kernels, block(): pl.pallas_call(partial(block_kernel, sizes), out_shape=(jax.ShapeDtypeStr...  38 us
    all_to_all x5, waiting for transfers between devices, exchange(): return lax.all_to_all(x, axes, 0, 0, tiled=True)  32 us
    ppermute x19, starting transfers between devices, by_xor(): lax.ppermute(x, axis, [(index, index ^ step) for index in range(count)])  22.9 us
    all_to_all x5, starting transfers between devices, exchange(): return lax.all_to_all(x, axes, 0, 0, tiled=True)  18.9 us
    pallas_call x7, Pallas kernels, call(): pl.pallas_call(kernel, out_shape=outs, in_specs=in_specs, out_specs=jax.t...  16 us
    ppermute x19, waiting for transfers between devices, by_xor(): lax.ppermute(x, axis, [(index, index ^ step) for index in range(count)])  9.37 us
    unnamed x48, local copies, waits for them, and re-layouts  6.81 us
  transfers between devices with their start and end apart: 24, of which 10 were waited for; matrix products, arithmetic and copies ran while one was open for 3% of the time, Pallas kernels for 8%

profile of v2, /device:TPU:0, one launch (start us, length us, event | category | flops | bytes accessed | tf_op | source)
XLA Modules:
  0.0 153.6 jit_solution(15233000001328820436)
XLA Ops:
  0.7 2.0 %pack.1 = (f32[4,64,192]{2,1,0:T(8,128)}, bf16[16,2688]{1,0:T(8,128)(2,1)}) custom-call(bf16[7,16,192]{2,1,0:T(8,128)(2,1)} %bitcast.96, f32[7,16,192]{2,1,0:T(8,128)} %bitcast.91, s32[16,192]{1,0:T(8,128)} %bitcast.97, f32[16,5134]{1,0:T(8,128)} %w_ref.1), custom_call_target="tpu_custom_call" | custom-call | tf_op jit(solution)/shard_map/pack/pallas_call | solution.py:619
  2.7 5.1 %collective-permute-start.2 = (bf16[16,2688]{1,0:T(8,128)(2,1)}, bf16[16,2688]{1,0:T(8,128)(2,1)S(1)}, u32[]{:S(2)}, u32[]{:S(2)}) collective-permute-start(bf16[16,2688]{1,0:T(8,128)(2,1)} %get-tuple-element.70), channel_id=1, source_target_pairs={{0,24},{4,28},{8,16},{12,20},{16,8},{20,12},{24,0},{28,4},{1,25},{... | collective-permute-start | bytes 258056 | tf_op jit(solution)/shard_map/ppermute | solution.py:98
  7.8 0.6 collective-permute-start
  8.5 3.4 %all-to-all-start = ((f32[4,64,192]{2,1,0:T(8,128)}), f32[4,64,192]{2,1,0:T(8,128)S(1)}, u32[]{:S(2)}, u32[]{:S(2)}) async-start(f32[4,64,192]{2,1,0:T(8,128)} %get-tuple-element.69), calls=%async_computation | async-start | bytes 524288 | tf_op jit(solution)/shard_map/all_to_all | solution.py:80
  12.6 0.9 fusion.6
  13.7 1.5 collective-permute-done.1
  15.3 2.6 %all-to-all-done.got_ref = f32[4,64,192]{2,1,0:T(8,128)S(1)} async-done(((f32[4,64,192]{2,1,0:T(8,128)}), f32[4,64,192]{2,1,0:T(8,128)S(1)}, u32[]{:S(2)}, u32[]{:S(2)}) %all-to-all-start) | async-done | bytes 196640 | tf_op jit(solution)/shard_map/all_to_all | solution.py:80
  17.9 1.6 %collective-permute-start.3 = (bf16[2,16,2688]{2,1,0:T(8,128)(2,1)S(1)}, bf16[2,16,2688]{2,1,0:T(8,128)(2,1)S(1)}, u32[]{:S(2)}, u32[]{:S(2)}) collective-permute-start(bf16[2,16,2688]{2,1,0:T(8,128)(2,1)S(1)} %pad_maximum_fusion), channel_id=1, source_target_pairs={{0,4},{4,0},{8,12},{12,8},{16,20},{20,16},{24,28},{28,24},{1,5},{5... | collective-permute-start | bytes 516104 | tf_op jit(solution)/shard_map/ppermute | solution.py:98
  20.0 1.4 spectra.1
  21.4 5.1 %all-to-all-start.1 = ((f32[32,16,128]{2,1,0:T(8,128)}), f32[32,16,128]{2,1,0:T(8,128)S(1)}, u32[]{:S(2)}, u32[]{:S(2)}) async-start(f32[32,16,128]{2,1,0:T(8,128)} %spectra.1), calls=%async_computation.1 | async-start | bytes 524288 | tf_op jit(solution)/shard_map/all_to_all | solution.py:80
  26.5 1.8 %collective-permute-start.6 = (bf16[4,16,2688]{2,1,0:T(8,128)(2,1)S(1)}, bf16[4,16,2688]{2,1,0:T(8,128)(2,1)S(1)}, u32[]{:S(2)}, u32[]{:S(2)}) collective-permute-start(bf16[4,16,2688]{2,1,0:T(8,128)(2,1)S(1)} %constant_dynamic-update-slice_fusion.2.refs_2_), channel_id=1, source_target_pairs={{0,4},{4,0},{8,12},{12,8},{16,20},{20,16},{24,28},{28,24},{1,5},{5... | collective-permute-start | bytes 1032200 | tf_op jit(solution)/shard_map/ppermute | solution.py:98
  28.4 1.5 collective-permute-start.4
  29.9 0.5 tables.1
  30.4 0.7 copy-done.1
  31.2 0.7 copy-done.2
  31.9 0.7 copy-done.3
  32.7 0.7 copy-done.7
  33.4 0.7 copy-done.8
  34.1 0.7 copy-done.9
  34.7 2.4 %all-to-all-done.1.got_ref.first_ref = f32[32,16,128]{2,1,0:T(8,128)S(1)} async-done(((f32[32,16,128]{2,1,0:T(8,128)}), f32[32,16,128]{2,1,0:T(8,128)S(1)}, u32[]{:S(2)}, u32[]{:S(2)}) %all-to-all-start.1) | async-done | bytes 262176 | tf_op jit(solution)/shard_map/all_to_all | solution.py:80
  37.1 3.1 %mix.1 = (bf16[32,80,128]{2,1,0:T(8,128)(2,1)}, bf16[16,128,128]{2,1,0:T(8,128)(2,1)S(1)}, f32[16,128]{1,0:T(8,128)S(1)}) custom-call(f32[32,16,128]{2,1,0:T(8,128)S(1)} %all-to-all-done.1.got_ref.first_ref, bf16[16,128,128]{2,1,0:T(8,128)(2,1)S(1)} %maximum_maximum_fusion.mixer_ref), custom_call_target="tpu_custom_call" | custom-call | tf_op jit(solution)/shard_map/mix/pallas_call | solution.py:619
  40.2 0.8 copy-done.10
  41.0 3.3 %all-to-all-start.2 = ((bf16[32,80,128]{2,1,0:T(8,128)(2,1)}), bf16[32,80,128]{2,1,0:T(8,128)(2,1)S(1)}, u32[]{:S(2)}, u32[]{:S(2)}) async-start(bf16[32,80,128]{2,1,0:T(8,128)(2,1)} %get-tuple-element.87), calls=%async_computation.2 | async-start | bytes 1310720 | tf_op jit(solution)/shard_map/all_to_all | solution.py:80
  45.5 0.6 pad_add_fusion.me_ref
  46.1 0.6 slice.123
  46.7 0.5 collective-permute-done.9.refs_6_
  47.7 14.4 %all-to-all-done.2.refs_8_ = bf16[32,80,128]{2,1,0:T(8,128)(2,1)S(1)} async-done(((bf16[32,80,128]{2,1,0:T(8,128)(2,1)}), bf16[32,80,128]{2,1,0:T(8,128)(2,1)S(1)}, u32[]{:S(2)}, u32[]{:S(2)}) %all-to-all-start.2) | async-done | bytes 655392 | tf_op jit(solution)/shard_map/all_to_all | solution.py:80
  62.1 0.8 copy-done.13
  62.9 38.0 %block.1 = (bf16[32,80,128]{2,1,0:T(8,128)(2,1)}, f32[8,128]{1,0:T(8,128)}, bf16[4,4,16,2560]{3,2,1,0:T(8,128)(2,1)}, bf16[4,4,16,2560]{3,2,1,0:T(8,128)(2,1)}) custom-call(f32[1]{0:T(128)} %bitcast.7.count_ref, s32[2]{0:T(128)} %pad_add_fusion.me_ref, bf16[4,16,2688]{2,1,0:T(8,128)(2,1)} %copy-done.15, bf16[4,16,2688]{2,1,0:T(8,128)(2,1)} %copy-done.19, ...), custom_call_target="tpu_custom_call" | custom-call | tf_op jit(solution)/shard_map/block/pallas_call | solution.py:548
  101.1 3.6 %all-to-all-start.3 = ((bf16[32,80,128]{2,1,0:T(8,128)(2,1)}), bf16[32,80,128]{2,1,0:T(8,128)(2,1)S(1)}, u32[]{:S(2)}, u32[]{:S(2)}) async-start(bf16[32,80,128]{2,1,0:T(8,128)(2,1)} %get-tuple-element.94), calls=%async_computation.3 | async-start | bytes 1310720 | tf_op jit(solution)/shard_map/all_to_all | solution.py:80
  104.7 2.1 %fusion.1 = (bf16[4,16,2560]{2,1,0:T(8,128)(2,1)}, bf16[4,16,2560]{2,1,0:T(8,128)(2,1)}) fusion(bf16[4,4,16,2560]{3,2,1,0:T(8,128)(2,1)} %collective-permute-done.11, bf16[4,4,16,2560]{3,2,1,0:T(8,128)(2,1)S(1)} %copy-done.14), kind=kLoop, calls=%fused_computation.4 | loop fusion | flops 1310720 | bytes 1966080 | tf_op jit(solution)/shard_map/convert_element_type | solution.py:159
  106.8 1.8 %collective-permute-start.13 = (bf16[4,16,2560]{2,1,0:T(8,128)(2,1)}, bf16[4,16,2560]{2,1,0:T(8,128)(2,1)S(1)}, u32[]{:S(2)}, u32[]{:S(2)}) collective-permute-start(bf16[4,16,2560]{2,1,0:T(8,128)(2,1)} %get-tuple-element.127), channel_id=1, source_target_pairs={{0,4},{4,0},{8,12},{12,8},{16,20},{20,16},{24,28},{28,24},{1,5},{5... | collective-permute-start | bytes 983048 | tf_op jit(solution)/shard_map/ppermute | solution.py:98
  108.5 1.5 collective-permute-start.12
  110.0 12.6 %all-to-all-done.3.got_ref = bf16[32,80,128]{2,1,0:T(8,128)(2,1)S(1)} async-done(((bf16[32,80,128]{2,1,0:T(8,128)(2,1)}), bf16[32,80,128]{2,1,0:T(8,128)(2,1)S(1)}, u32[]{:S(2)}, u32[]{:S(2)}) %all-to-all-start.3) | async-done | bytes 655392 | tf_op jit(solution)/shard_map/all_to_all | solution.py:80
  122.6 1.2 fusion.14
  123.9 0.9 slice_bitcast_fusion.3
  124.9 1.0 fusion.9
  125.9 1.5 collective-permute-start.14
  127.4 1.4 collective-permute-start.15
  128.8 2.2 %mix_back.1 = (f32[32,16,128]{2,1,0:T(8,128)}, bf16[16,128,128]{2,1,0:T(8,128)(2,1)S(1)}, f32[8,128]{1,0:T(8,128)S(1)}) custom-call(bf16[32,80,128]{2,1,0:T(8,128)(2,1)S(1)} %all-to-all-done.3.got_ref, bf16[16,128,128]{2,1,0:T(8,128)(2,1)S(1)} %maximum_maximum_fusion.mixer_ref, f32[32,16,128]{2,1,0:T(8,128)S(1)} %all-to-all-done.1.got_ref.first_ref, ...), custom_call_target="tpu_custom_call" | custom-call | flops 10000000000 | bytes 1000000000 | tf_op jit(solution)/shard_map/mix_back/pallas_call | solution.py:619
  131.0 0.8 copy-done.12
  131.8 3.6 %all-to-all-start.4 = ((f32[32,16,128]{2,1,0:T(8,128)}), f32[32,16,128]{2,1,0:T(8,128)S(1)}, u32[]{:S(2)}, u32[]{:S(2)}) async-start(f32[32,16,128]{2,1,0:T(8,128)} %get-tuple-element.99), calls=%async_computation.4 | async-start | bytes 524288 | tf_op jit(solution)/shard_map/all_to_all | solution.py:80
  135.5 1.8 %collective-permute-start.16 = (bf16[16,2560]{1,0:T(8,128)(2,1)S(1)}, bf16[16,2560]{1,0:T(8,128)(2,1)S(1)}, u32[]{:S(2)}, u32[]{:S(2)}) collective-permute-start(bf16[16,2560]{1,0:T(8,128)(2,1)S(1)} %get-tuple-element.135), channel_id=1, source_target_pairs={{0,8},{4,12},{8,0},{12,4},{16,24},{20,28},{24,16},{28,20},{1,9},{5... | collective-permute-start | bytes 245768 | tf_op jit(solution)/shard_map/ppermute | solution.py:98
  137.4 2.4 %collective-permute-start.18 = (bf16[16,2560]{1,0:T(8,128)(2,1)S(1)}, bf16[16,2560]{1,0:T(8,128)(2,1)S(1)}, u32[]{:S(2)}, u32[]{:S(2)}) collective-permute-start(bf16[16,2560]{1,0:T(8,128)(2,1)S(1)} %get-tuple-element.133), channel_id=1, source_target_pairs={{0,24},{4,28},{8,16},{12,20},{16,8},{20,12},{24,0},{28,4},{1,25},{... | collective-permute-start | bytes 245768 | tf_op jit(solution)/shard_map/ppermute | solution.py:98
  140.0 5.0 %spectral.1 = (f32[2,16,4096]{2,1,0:T(8,128)}, f32[2,16,4096]{2,1,0:T(8,128)}, f32[2,16,4096]{2,1,0:T(8,128)}, f32[2,16,4096]{2,1,0:T(8,128)}, bf16[2,16,4096]{2,1,0:T(8,128)(2,1)}) custom-call(bf16[16,128,128]{2,1,0:T(8,128)(2,1)} %copy-done.10, bf16[16,128,128]{2,1,0:T(8,128)(2,1)} %copy-done.12, f32[2,16,4096]{2,1,0:T(8,128)} %refs_2_.1, ...), custom_call_target="tpu_custom_call" | custom-call | flops 10000000000 | bytes 1000000000 | tf_op jit(solution)/shard_map/spectral/pallas_call | solution.py:619
  145.0 3.4 %collective-permute-done.18.refs_3_ = bf16[16,2560]{1,0:T(8,128)(2,1)S(1)} collective-permute-done((bf16[16,2560]{1,0:T(8,128)(2,1)S(1)}, bf16[16,2560]{1,0:T(8,128)(2,1)S(1)}, u32[]{:S(2)}, u32[]{:S(2)}) %collective-permute-start.18) | collective-permute-done | bytes 81952 | tf_op jit(solution)/shard_map/ppermute | solution.py:98
  148.4 3.4 %collective-permute-done.17.refs_2_ = bf16[16,2560]{1,0:T(8,128)(2,1)S(1)} collective-permute-done((bf16[16,2560]{1,0:T(8,128)(2,1)S(1)}, bf16[16,2560]{1,0:T(8,128)(2,1)S(1)}, u32[]{:S(2)}, u32[]{:S(2)}) %collective-permute-start.17) | collective-permute-done | bytes 81952 | tf_op jit(solution)/shard_map/ppermute | solution.py:98
  151.8 1.8 %rows.1 = (f32[1,1]{1,0:T(1,128)}, f32[16,5134]{1,0:T(8,128)}, f32[16,5134]{1,0:T(8,128)}, f32[16,5134]{1,0:T(8,128)}, f32[16,5134]{1,0:T(8,128)}, /*index=5*/bf16[16,5134]{1,0:T(8,128)(2,1)}) custom-call(f32[32,16,128]{2,1,0:T(8,128)S(1)} %all-to-all-done.4.got_ref, f32[8,128]{1,0:T(8,128)S(1)} %get-tuple-element.100.thin_ref, ...), custom_call_target="tpu_custom_call" | custom-call | tf_op jit(solution)/shard_map/rows/pallas_call | solution.py:619
  (80 shorter events, 3.7 us)
Async XLA Ops:
  0.6 11.2 %copy-start.17 = (f32[2,16,4096]{2,1,0:T(8,128)S(1)}, f32[2,16,4096]{2,1,0:T(8,128)}, u32[]{:S(2)}) copy-start(f32[2,16,4096]{2,1,0:T(8,128)} %refs_2_.1) | copy-start | bytes 1572868
  2.7 11.0 %collective-permute-start.2 = (bf16[16,2688]{1,0:T(8,128)(2,1)}, bf16[16,2688]{1,0:T(8,128)(2,1)S(1)}, u32[]{:S(2)}, u32[]{:S(2)}) collective-permute-start(bf16[16,2688]{1,0:T(8,128)(2,1)} %get-tuple-element.70), channel_id=1, source_target_pairs={{0,24},{4,28},{8,16},{12,20},{16,8},{20,12},{24,0},{28,4},{1,25},{... | collective-permute-start | bytes 258056 | tf_op jit(solution)/shard_map/ppermute | solution.py:98
  7.8 7.4 %collective-permute-start.1 = (bf16[16,2688]{1,0:T(8,128)(2,1)}, bf16[16,2688]{1,0:T(8,128)(2,1)S(1)}, u32[]{:S(2)}, u32[]{:S(2)}) collective-permute-start(bf16[16,2688]{1,0:T(8,128)(2,1)} %get-tuple-element.70), channel_id=1, source_target_pairs={{0,16},{4,20},{8,24},{12,28},{16,0},{20,4},{24,8},{28,12},{1,17},{... | collective-permute-start | bytes 258056 | tf_op jit(solution)/shard_map/ppermute | solution.py:98
  7.8 7.4 %collective-permute-start = (bf16[16,2688]{1,0:T(8,128)(2,1)}, bf16[16,2688]{1,0:T(8,128)(2,1)S(1)}, u32[]{:S(2)}, u32[]{:S(2)}) collective-permute-start(bf16[16,2688]{1,0:T(8,128)(2,1)} %get-tuple-element.70), channel_id=1, source_target_pairs={{0,8},{4,12},{8,0},{12,4},{16,24},{20,28},{24,16},{28,20},{1,9},{5... | collective-permute-start | bytes 258056 | tf_op jit(solution)/shard_map/ppermute | solution.py:98
  8.5 9.4 %all-to-all-start = ((f32[4,64,192]{2,1,0:T(8,128)}), f32[4,64,192]{2,1,0:T(8,128)S(1)}, u32[]{:S(2)}, u32[]{:S(2)}) async-start(f32[4,64,192]{2,1,0:T(8,128)} %get-tuple-element.69), calls=%async_computation | async-start | bytes 524288 | tf_op jit(solution)/shard_map/all_to_all | solution.py:80
  11.9 0.7 copy-start.22
  12.3 3.0 %copy-start.21 = (bf16[16,2688]{1,0:T(8,128)(2,1)S(1)}, bf16[16,2688]{1,0:T(8,128)(2,1)}, u32[]{:S(2)}) copy-start(bf16[16,2688]{1,0:T(8,128)(2,1)} %get-tuple-element.70) | copy-start | bytes 258052
  12.5 7.4 %copy-start = (f32[16,5134]{1,0:T(8,128)S(1)}, f32[16,5134]{1,0:T(8,128)}, u32[]{:S(2)}) copy-start(f32[16,5134]{1,0:T(8,128)} %w_ref.1) | copy-start | bytes 985732
  17.9 10.5 %collective-permute-start.3 = (bf16[2,16,2688]{2,1,0:T(8,128)(2,1)S(1)}, bf16[2,16,2688]{2,1,0:T(8,128)(2,1)S(1)}, u32[]{:S(2)}, u32[]{:S(2)}) collective-permute-start(bf16[2,16,2688]{2,1,0:T(8,128)(2,1)S(1)} %pad_maximum_fusion), channel_id=1, source_target_pairs={{0,4},{4,0},{8,12},{12,8},{16,20},{20,16},{24,28},{28,24},{1,5},{5... | collective-permute-start | bytes 516104 | tf_op jit(solution)/shard_map/ppermute | solution.py:98
  19.5 6.9 %collective-permute-start.5 = (bf16[2,16,2688]{2,1,0:T(8,128)(2,1)S(1)}, bf16[2,16,2688]{2,1,0:T(8,128)(2,1)S(1)}, u32[]{:S(2)}, u32[]{:S(2)}) collective-permute-start(bf16[2,16,2688]{2,1,0:T(8,128)(2,1)S(1)} %pad_maximum_fusion.1), channel_id=1, source_target_pairs={{0,2},{1,3},{2,0},{3,1},{4,6},{5,7},{6,4},{7,5},{8,10},{9,11},{10,... | collective-permute-start | bytes 516104 | tf_op jit(solution)/shard_map/ppermute | solution.py:98
  21.4 15.8 %all-to-all-start.1 = ((f32[32,16,128]{2,1,0:T(8,128)}), f32[32,16,128]{2,1,0:T(8,128)S(1)}, u32[]{:S(2)}, u32[]{:S(2)}) async-start(f32[32,16,128]{2,1,0:T(8,128)} %spectra.1), calls=%async_computation.1 | async-start | bytes 524288 | tf_op jit(solution)/shard_map/all_to_all | solution.py:80
  26.5 18.5 %copy-start.16 = (bf16[4,16,2688]{2,1,0:T(8,128)(2,1)}, bf16[4,16,2688]{2,1,0:T(8,128)(2,1)S(1)}, u32[]{:S(2)}) copy-start(bf16[4,16,2688]{2,1,0:T(8,128)(2,1)S(1)} %constant_dynamic-update-slice_fusion.2.refs_2_) | copy-start | bytes 1032196
  26.5 14.5 %collective-permute-start.6 = (bf16[4,16,2688]{2,1,0:T(8,128)(2,1)S(1)}, bf16[4,16,2688]{2,1,0:T(8,128)(2,1)S(1)}, u32[]{:S(2)}, u32[]{:S(2)}) collective-permute-start(bf16[4,16,2688]{2,1,0:T(8,128)(2,1)S(1)} %constant_dynamic-update-slice_fusion.2.refs_2_), channel_id=1, source_target_pairs={{0,4},{4,0},{8,12},{12,8},{16,20},{20,16},{24,28},{28,24},{1,5},{5... | collective-permute-start | bytes 1032200 | tf_op jit(solution)/shard_map/ppermute | solution.py:98
  28.4 16.0 %copy-start.15 = (bf16[4,16,2688]{2,1,0:T(8,128)(2,1)}, bf16[4,16,2688]{2,1,0:T(8,128)(2,1)S(1)}, u32[]{:S(2)}) copy-start(bf16[4,16,2688]{2,1,0:T(8,128)(2,1)S(1)} %constant_dynamic-update-slice_fusion.refs_0_) | copy-start | bytes 1032196
  28.4 12.7 %collective-permute-start.4 = (bf16[4,16,2688]{2,1,0:T(8,128)(2,1)S(1)}, bf16[4,16,2688]{2,1,0:T(8,128)(2,1)S(1)}, u32[]{:S(2)}, u32[]{:S(2)}) collective-permute-start(bf16[4,16,2688]{2,1,0:T(8,128)(2,1)S(1)} %constant_dynamic-update-slice_fusion.refs_0_), channel_id=1, source_target_pairs={{0,2},{1,3},{2,0},{3,1},{4,6},{5,7},{6,4},{7,5},{8,10},{9,11},{10,... | collective-permute-start | bytes 1032200 | tf_op jit(solution)/shard_map/ppermute | solution.py:98
  30.4 0.7 copy-start.1
  31.2 0.7 copy-start.2
  31.9 0.7 copy-start.3
  32.7 0.7 copy-start.7
  33.4 0.7 copy-start.8
  34.1 0.7 copy-start.9
  40.2 0.8 copy-start.10
  41.0 21.1 %copy-start.18 = (bf16[4,16,2688]{2,1,0:T(8,128)(2,1)}, bf16[4,16,2688]{2,1,0:T(8,128)(2,1)S(1)}, u32[]{:S(2)}) copy-start(bf16[4,16,2688]{2,1,0:T(8,128)(2,1)S(1)} %collective-permute-done.6.refs_3_) | copy-start | bytes 1032196
  41.0 21.1 %copy-start.19 = (bf16[4,16,2688]{2,1,0:T(8,128)(2,1)}, bf16[4,16,2688]{2,1,0:T(8,128)(2,1)S(1)}, u32[]{:S(2)}) copy-start(bf16[4,16,2688]{2,1,0:T(8,128)(2,1)S(1)} %collective-permute-done.4.refs_1_) | copy-start | bytes 1032196
  41.0 21.1 %all-to-all-start.2 = ((bf16[32,80,128]{2,1,0:T(8,128)(2,1)}), bf16[32,80,128]{2,1,0:T(8,128)(2,1)S(1)}, u32[]{:S(2)}, u32[]{:S(2)}) async-start(bf16[32,80,128]{2,1,0:T(8,128)(2,1)} %get-tuple-element.87), calls=%async_computation.2 | async-start | bytes 1310720 | tf_op jit(solution)/shard_map/all_to_all | solution.py:80
  44.4 2.3 %collective-permute-start.7 = (bf16[4,16,2688]{2,1,0:T(8,128)(2,1)S(1)}, bf16[4,16,2688]{2,1,0:T(8,128)(2,1)S(1)}, u32[]{:S(2)}, u32[]{:S(2)}) collective-permute-start(bf16[4,16,2688]{2,1,0:T(8,128)(2,1)S(1)} %constant_dynamic-update-slice_fusion.refs_0_), channel_id=1, source_target_pairs={{0,1},{1,0},{2,3},{3,2},{4,5},{5,4},{6,7},{7,6},{8,9},{9,8},{10,11... | collective-permute-start | bytes 1032200 | tf_op jit(solution)/shard_map/ppermute | solution.py:98
  44.5 2.2 %collective-permute-start.8 = (bf16[4,16,2688]{2,1,0:T(8,128)(2,1)S(1)}, bf16[4,16,2688]{2,1,0:T(8,128)(2,1)}, u32[]{:S(2)}, u32[]{:S(2)}) collective-permute-start(bf16[4,16,2688]{2,1,0:T(8,128)(2,1)S(1)} %collective-permute-done.4.refs_1_), channel_id=1, source_target_pairs={{0,1},{1,0},{2,3},{3,2},{4,5},{5,4},{6,7},{7,6},{8,9},{9,8},{10,11... | collective-permute-start | bytes 1032200 | tf_op jit(solution)/shard_map/ppermute | solution.py:98
  45.0 2.3 %collective-permute-start.9 = (bf16[4,16,2688]{2,1,0:T(8,128)(2,1)S(1)}, bf16[4,16,2688]{2,1,0:T(8,128)(2,1)}, u32[]{:S(2)}, u32[]{:S(2)}) collective-permute-start(bf16[4,16,2688]{2,1,0:T(8,128)(2,1)S(1)} %constant_dynamic-update-slice_fusion.2.refs_2_), channel_id=1, source_target_pairs={{0,1},{1,0},{2,3},{3,2},{4,5},{5,4},{6,7},{7,6},{8,9},{9,8},{10,11... | collective-permute-start | bytes 1032200 | tf_op jit(solution)/shard_map/ppermute | solution.py:98
  45.0 2.7 %collective-permute-start.10 = (bf16[4,16,2688]{2,1,0:T(8,128)(2,1)S(1)}, bf16[4,16,2688]{2,1,0:T(8,128)(2,1)}, u32[]{:S(2)}, u32[]{:S(2)}) collective-permute-start(bf16[4,16,2688]{2,1,0:T(8,128)(2,1)S(1)} %collective-permute-done.6.refs_3_), channel_id=1, source_target_pairs={{0,1},{1,0},{2,3},{3,2},{4,5},{5,4},{6,7},{7,6},{8,9},{9,8},{10,11... | collective-permute-start | bytes 1032200 | tf_op jit(solution)/shard_map/ppermute | solution.py:98
  46.6 15.5 %copy-start.20 = (bf16[4,16,2688]{2,1,0:T(8,128)(2,1)}, bf16[4,16,2688]{2,1,0:T(8,128)(2,1)S(1)}, u32[]{:S(2)}) copy-start(bf16[4,16,2688]{2,1,0:T(8,128)(2,1)S(1)} %collective-permute-done.7.refs_4_) | copy-start | bytes 1032196
  62.1 0.8 copy-start.13
  101.0 3.7 %copy-start.14 = (bf16[4,4,16,2560]{3,2,1,0:T(8,128)(2,1)S(1)}, bf16[4,4,16,2560]{3,2,1,0:T(8,128)(2,1)}, u32[]{:S(2)}) copy-start(bf16[4,4,16,2560]{3,2,1,0:T(8,128)(2,1)} %get-tuple-element.102) | copy-start | bytes 3932164
  101.0 3.7 %collective-permute-start.11 = (bf16[4,4,16,2560]{3,2,1,0:T(8,128)(2,1)}, bf16[4,4,16,2560]{3,2,1,0:T(8,128)(2,1)}, u32[]{:S(2)}, u32[]{:S(2)}) collective-permute-start(bf16[4,4,16,2560]{3,2,1,0:T(8,128)(2,1)} %get-tuple-element.96), channel_id=1, source_target_pairs={{0,1},{1,0},{2,3},{3,2},{4,5},{5,4},{6,7},{7,6},{8,9},{9,8},{10,11... | collective-permute-start | bytes 3932168 | tf_op jit(solution)/shard_map/ppermute | solution.py:98
  101.1 21.5 %all-to-all-start.3 = ((bf16[32,80,128]{2,1,0:T(8,128)(2,1)}), bf16[32,80,128]{2,1,0:T(8,128)(2,1)S(1)}, u32[]{:S(2)}, u32[]{:S(2)}) async-start(bf16[32,80,128]{2,1,0:T(8,128)(2,1)} %get-tuple-element.94), calls=%async_computation.3 | async-start | bytes 1310720 | tf_op jit(solution)/shard_map/all_to_all | solution.py:80
  106.8 15.8 %collective-permute-start.13 = (bf16[4,16,2560]{2,1,0:T(8,128)(2,1)}, bf16[4,16,2560]{2,1,0:T(8,128)(2,1)S(1)}, u32[]{:S(2)}, u32[]{:S(2)}) collective-permute-start(bf16[4,16,2560]{2,1,0:T(8,128)(2,1)} %get-tuple-element.127), channel_id=1, source_target_pairs={{0,4},{4,0},{8,12},{12,8},{16,20},{20,16},{24,28},{28,24},{1,5},{5... | collective-permute-start | bytes 983048 | tf_op jit(solution)/shard_map/ppermute | solution.py:98
  108.5 14.1 %collective-permute-start.12 = (bf16[4,16,2560]{2,1,0:T(8,128)(2,1)}, bf16[4,16,2560]{2,1,0:T(8,128)(2,1)}, u32[]{:S(2)}, u32[]{:S(2)}) collective-permute-start(bf16[4,16,2560]{2,1,0:T(8,128)(2,1)} %get-tuple-element.128), channel_id=1, source_target_pairs={{0,2},{1,3},{2,0},{3,1},{4,6},{5,7},{6,4},{7,5},{8,10},{9,11},{10,... | collective-permute-start | bytes 983048 | tf_op jit(solution)/shard_map/ppermute | solution.py:98
  123.8 5.0 %copy-start.11 = (f32[8,128]{1,0:T(8,128)S(1)}, f32[8,128]{1,0:T(8,128)}, u32[]{:S(2)}) copy-start(f32[8,128]{1,0:T(8,128)} %get-tuple-element.98.stat_ref) | copy-start | bytes 12292
  125.9 9.5 %collective-permute-start.14 = (bf16[2,16,2560]{2,1,0:T(8,128)(2,1)S(1)}, bf16[2,16,2560]{2,1,0:T(8,128)(2,1)S(1)}, u32[]{:S(2)}, u32[]{:S(2)}) collective-permute-start(bf16[2,16,2560]{2,1,0:T(8,128)(2,1)S(1)} %fusion.9), channel_id=1, source_target_pairs={{0,4},{4,0},{8,12},{12,8},{16,20},{20,16},{24,28},{28,24},{1,5},{5... | collective-permute-start | bytes 491528 | tf_op jit(solution)/shard_map/ppermute | solution.py:98
  127.4 8.0 %collective-permute-start.15 = (bf16[2,16,2560]{2,1,0:T(8,128)(2,1)S(1)}, bf16[2,16,2560]{2,1,0:T(8,128)(2,1)S(1)}, u32[]{:S(2)}, u32[]{:S(2)}) collective-permute-start(bf16[2,16,2560]{2,1,0:T(8,128)(2,1)S(1)} %fusion.10), channel_id=1, source_target_pairs={{0,2},{1,3},{2,0},{3,1},{4,6},{5,7},{6,4},{7,5},{8,10},{9,11},{10,... | collective-permute-start | bytes 491528 | tf_op jit(solution)/shard_map/ppermute | solution.py:98
  131.0 0.8 copy-start.12
  131.8 20.0 %all-to-all-start.4 = ((f32[32,16,128]{2,1,0:T(8,128)}), f32[32,16,128]{2,1,0:T(8,128)S(1)}, u32[]{:S(2)}, u32[]{:S(2)}) async-start(f32[32,16,128]{2,1,0:T(8,128)} %get-tuple-element.99), calls=%async_computation.4 | async-start | bytes 524288 | tf_op jit(solution)/shard_map/all_to_all | solution.py:80
  135.5 9.5 %collective-permute-start.16 = (bf16[16,2560]{1,0:T(8,128)(2,1)S(1)}, bf16[16,2560]{1,0:T(8,128)(2,1)S(1)}, u32[]{:S(2)}, u32[]{:S(2)}) collective-permute-start(bf16[16,2560]{1,0:T(8,128)(2,1)S(1)} %get-tuple-element.135), channel_id=1, source_target_pairs={{0,8},{4,12},{8,0},{12,4},{16,24},{20,28},{24,16},{28,20},{1,9},{5... | collective-permute-start | bytes 245768 | tf_op jit(solution)/shard_map/ppermute | solution.py:98
  137.4 11.0 %collective-permute-start.18 = (bf16[16,2560]{1,0:T(8,128)(2,1)S(1)}, bf16[16,2560]{1,0:T(8,128)(2,1)S(1)}, u32[]{:S(2)}, u32[]{:S(2)}) collective-permute-start(bf16[16,2560]{1,0:T(8,128)(2,1)S(1)} %get-tuple-element.133), channel_id=1, source_target_pairs={{0,24},{4,28},{8,16},{12,20},{16,8},{20,12},{24,0},{28,4},{1,25},{... | collective-permute-start | bytes 245768 | tf_op jit(solution)/shard_map/ppermute | solution.py:98
  139.9 11.9 %collective-permute-start.17 = (bf16[16,2560]{1,0:T(8,128)(2,1)S(1)}, bf16[16,2560]{1,0:T(8,128)(2,1)S(1)}, u32[]{:S(2)}, u32[]{:S(2)}) collective-permute-start(bf16[16,2560]{1,0:T(8,128)(2,1)S(1)} %get-tuple-element.134), channel_id=1, source_target_pairs={{0,16},{4,20},{8,24},{12,28},{16,0},{20,4},{24,8},{28,12},{1,17},{... | collective-permute-start | bytes 245768 | tf_op jit(solution)/shard_map/ppermute | solution.py:98
  140.0 11.8 %copy-start.4 = (f32[16,5134]{1,0:T(8,128)S(1)}, f32[16,5134]{1,0:T(8,128)}, u32[]{:S(2)}) copy-start(f32[16,5134]{1,0:T(8,128)} %m_ref.1) | copy-start | bytes 985732
  140.0 11.8 %copy-start.5 = (f32[16,5134]{1,0:T(8,128)S(1)}, f32[16,5134]{1,0:T(8,128)}, u32[]{:S(2)}) copy-start(f32[16,5134]{1,0:T(8,128)} %v_ref.1) | copy-start | bytes 985732
  140.0 11.8 %copy-start.6 = (f32[16,5134]{1,0:T(8,128)S(1)}, f32[16,5134]{1,0:T(8,128)}, u32[]{:S(2)}) copy-start(f32[16,5134]{1,0:T(8,128)} %ema_ref.1) | copy-start | bytes 985732

commit v3 on v2

--- a/solution.py
+++ b/solution.py
@@ -154,21 +154,18 @@
 
 
 def scatter_tiles_first(away, stay):
-    terms = [stay, by_xor(away, "mode", 1)]
-    first = by_xor(total_of(terms, 0).astype(BF), "mode", 2)
-    second = by_xor(total_of(terms, 2).astype(BF), "dp", 1)
-    return [terms[0], terms[1], first, second]
-
-
-def scatter_tiles_second(stay, come, first, second):
     pairs = lambda terms: [x.reshape((x.shape[0] // 2, 2) + x.shape[1:]) for x in terms]
+    come = by_xor(away, "mode", 1)
+    first = by_xor(total_of([stay, come], 0).astype(BF), "mode", 2)
+    second = by_xor(total_of([stay, come], 2).astype(BF), "dp", 1)
     first = pairs([stay[1], come[1], first])
     second = pairs([stay[3], come[3], second])
-    halves = (slice(None), 1)
-    return [
-        [x[:, 0] for x in first] + [by_xor(total_of(first, halves).astype(BF), "dp", 1)],
-        [x[:, 0] for x in second] + [by_xor(total_of(second, halves).astype(BF), "mode", 2)],
-    ]
+    away = [total_of(terms, (slice(None), 1)).astype(BF) for terms in (first, second)]
+    return away + [[x[:, 0] for x in terms] for terms in (first, second)]
+
+
+def scatter_tiles_second(first_away, second_away, first, second):
+    return [first + [by_xor(first_away, "dp", 1)], second + [by_xor(second_away, "mode", 2)]]
 
 
 def scatter_tiles_third(first, second):
@@ -799,7 +796,9 @@
             at = (part * nb + k) * LEAD
             total += from_lane(query[at : at + LEAD], part * wide, wide)
     block = total + at_lane(from_lane(thin, 0, share), HALF, share)
-    block = jnp.concatenate([block, stat_ref[...]], axis=0)
+    row, lane = iota(block.shape, 0), iota(block.shape, 1)
+    stats = jnp.where(lane < HALF, stat_ref[:1, :], stat_ref[1:2, :])
+    block = jnp.where(row == C, stats, block)
     for d in range(n_all):
         send_ref[d] = block
 
@@ -883,10 +882,11 @@
         for d in range(at * LANES // share, (at + 1) * LANES // share):
             block += at_lane(from_lane(got_ref[d, :LEAD, :], HALF, share), d * share % LANES, share)
         down.append(block)
-    down = jnp.concatenate(down, axis=1)
+    down = jnp.where(iota((LEAD, FF), 0) < C, jnp.concatenate(down, axis=1), 0.0)
     norm = SPECTRAL_WEIGHT / (total * M * S)
-    stats = sum(got_ref[d, LEAD:, :] for d in range(n_all))
-    loss_ref[...] = stats[:1, :1] / steps_ref[C : C + 1, HALF : HALF + 1] + norm * stats[1:2, :1]
+    stats = sum(got_ref[d, C : C + 1, :] for d in range(n_all))
+    steps = steps_ref[C : C + 1, HALF : HALF + 1]
+    loss_ref[...] = stats[:, :1] / steps + norm * stats[:, HALF : HALF + 1]
 
     keep = iota((LEAD, D), 0) < C
     query = jnp.where(keep, query, 0.0)
@@ -960,7 +960,6 @@
     cosv, sinv = tables(mode_index)
     weights = [gather_rows(weights)] if not tiled else gather_tiles_first(weights)
     if tiled:
-        own, *weights = together(own, *weights)
         weights = gather_tiles_second(*weights)
 
     whole_rows = [pltpu.VMEM((2 * nb * LEAD, S), F32)]
@@ -1035,7 +1034,7 @@
     send, grad_mixed, thin = call(
         partial(mix_back_kernel, sizes),
         (
-            shape((n_all, 16, LANES), F32),
+            shape((n_all, LEAD, LANES), F32),
             shape((modes, total, LANES), BF),
             shape((LEAD, LANES), F32),
         ),

time: 154 us -> 146 us (0.948)
  waiting for transfers between devices: 41.3 us -> 34.1 us
  starting transfers between devices: 41.9 us -> 44.7 us
  local copies, waits for them, and re-layouts: 10.1 us -> 8.29 us
  other arithmetic: 5.16 us -> 3.5 us
    all_to_all x5, waiting for transfers between devices: 32 us -> 17.3 us  [exchange(): return lax.all_to_all(x, axes, 0, 0, tiled=True)]
    ppermute x19, waiting for transfers between devices: 9.37 us -> 16.8 us  [by_xor(): lax.ppermute(x, axis, [(index, index ^ step) for index in range(count)])]
    convert_element_type x3, other arithmetic: 3.12 us -> 1.38 us  [the longest x1 1.25 us: scatter_tiles_first(): second = by_xor(total_of([stay, come], 2).astype(BF), 'dp', 1)]
    ppermute x19, starting transfers between devices: 22.9 us -> 24.6 us  [by_xor(): lax.ppermute(x, axis, [(index, index ^ step) for index in range(count)])]
    unnamed x48 -> x40, local copies, waits for them, and re-layouts: 6.81 us -> 5.99 us
  transfers between devices with their start and end apart: 24 -> 24, of which waited for: 10 -> 11; matrix products, arithmetic and copies ran while one was open for 3% -> 4% of each run, Pallas kernels for 8% -> 8%
where the time goes in v3:
time: 146 us
  Pallas kernels  54.1 us (37%)
  starting transfers between devices  44.7 us (31%)
  waiting for transfers between devices  34.1 us (23%)
  local copies, waits for them, and re-layouts  8.29 us (6%)
  other arithmetic  3.5 us (2%)
    pallas_call x1, Pallas kernels, block(): pl.pallas_call(partial(block_kernel, sizes), out_shape=(jax.ShapeDtypeStr...  38 us
    ppermute x19, starting transfers between devices, by_xor(): lax.ppermute(x, axis, [(index, index ^ step) for index in range(count)])  24.6 us
    all_to_all x5, starting transfers between devices, exchange(): return lax.all_to_all(x, axes, 0, 0, tiled=True)  20.1 us
    all_to_all x5, waiting for transfers between devices, exchange(): return lax.all_to_all(x, axes, 0, 0, tiled=True)  17.3 us
    ppermute x19, waiting for transfers between devices, by_xor(): lax.ppermute(x, axis, [(index, index ^ step) for index in range(count)])  16.8 us
    pallas_call x7, Pallas kernels, call(): pl.pallas_call(kernel, out_shape=outs, in_specs=in_specs, out_specs=jax.t...  16 us
    unnamed x40, local copies, waits for them, and re-layouts  5.99 us
  transfers between devices with their start and end apart: 24, of which 11 were waited for; matrix products, arithmetic and copies ran while one was open for 4% of the time, Pallas kernels for 8%

profile of v3, /device:TPU:0, one launch (start us, length us, event | category | flops | bytes accessed | tf_op | source)
XLA Modules:
  0.0 145.7 jit_solution(16002811765130723419)
XLA Ops:
  0.7 2.0 %pack.1 = (f32[4,64,192]{2,1,0:T(8,128)}, bf16[16,2688]{1,0:T(8,128)(2,1)}) custom-call(bf16[7,16,192]{2,1,0:T(8,128)(2,1)} %bitcast.102, f32[7,16,192]{2,1,0:T(8,128)} %bitcast.101, s32[16,192]{1,0:T(8,128)} %bitcast.103, f32[16,5134]{1,0:T(8,128)} %w_ref.1), custom_call_target="tpu_custom_call" | custom-call | tf_op jit(solution)/shard_map/pack/pallas_call | solution.py:616
  2.7 5.1 %collective-permute-start.4 = (bf16[16,2688]{1,0:T(8,128)(2,1)}, bf16[16,2688]{1,0:T(8,128)(2,1)S(1)}, u32[]{:S(2)}, u32[]{:S(2)}) collective-permute-start(bf16[16,2688]{1,0:T(8,128)(2,1)} %get-tuple-element.80), channel_id=1, source_target_pairs={{0,24},{4,28},{8,16},{12,20},{16,8},{20,12},{24,0},{28,4},{1,25},{... | collective-permute-start | bytes 258056 | tf_op jit(solution)/shard_map/ppermute | solution.py:98
  7.8 0.6 collective-permute-start
  8.5 3.4 %all-to-all-start = ((f32[4,64,192]{2,1,0:T(8,128)}), f32[4,64,192]{2,1,0:T(8,128)S(1)}, u32[]{:S(2)}, u32[]{:S(2)}) async-start(f32[4,64,192]{2,1,0:T(8,128)} %get-tuple-element.70), calls=%async_computation | async-start | bytes 524288 | tf_op jit(solution)/shard_map/all_to_all | solution.py:80
  12.6 0.9 fusion.6
  13.8 1.7 %collective-permute-start.1 = (bf16[2,16,2688]{2,1,0:T(8,128)(2,1)S(1)}, bf16[2,16,2688]{2,1,0:T(8,128)(2,1)S(1)}, u32[]{:S(2)}, u32[]{:S(2)}) collective-permute-start(bf16[2,16,2688]{2,1,0:T(8,128)(2,1)S(1)} %pad_maximum_fusion.2), channel_id=1, source_target_pairs={{0,4},{4,0},{8,12},{12,8},{16,20},{20,16},{24,28},{28,24},{1,5},{5... | collective-permute-start | bytes 516104 | tf_op jit(solution)/shard_map/ppermute | solution.py:98
  15.5 2.0 %collective-permute-start.5 = (bf16[2,16,2688]{2,1,0:T(8,128)(2,1)S(1)}, bf16[2,16,2688]{2,1,0:T(8,128)(2,1)S(1)}, u32[]{:S(2)}, u32[]{:S(2)}) collective-permute-start(bf16[2,16,2688]{2,1,0:T(8,128)(2,1)S(1)} %pad_maximum_fusion.3), channel_id=1, source_target_pairs={{0,2},{1,3},{2,0},{3,1},{4,6},{5,7},{6,4},{7,5},{8,10},{9,11},{10,... | collective-permute-start | bytes 516104 | tf_op jit(solution)/shard_map/ppermute | solution.py:98
  17.9 1.4 spectra.1
  19.3 5.5 %all-to-all-start.1 = ((f32[32,16,128]{2,1,0:T(8,128)}), f32[32,16,128]{2,1,0:T(8,128)S(1)}, u32[]{:S(2)}, u32[]{:S(2)}) async-start(f32[32,16,128]{2,1,0:T(8,128)} %spectra.1), calls=%async_computation.1 | async-start | bytes 524288 | tf_op jit(solution)/shard_map/all_to_all | solution.py:80
  24.9 1.8 %collective-permute-start.2 = (bf16[4,16,2688]{2,1,0:T(8,128)(2,1)S(1)}, bf16[4,16,2688]{2,1,0:T(8,128)(2,1)}, u32[]{:S(2)}, u32[]{:S(2)}) collective-permute-start(bf16[4,16,2688]{2,1,0:T(8,128)(2,1)S(1)} %pad_maximum_fusion.refs_0_), channel_id=1, source_target_pairs={{0,2},{1,3},{2,0},{3,1},{4,6},{5,7},{6,4},{7,5},{8,10},{9,11},{10,... | collective-permute-start | bytes 1032200 | tf_op jit(solution)/shard_map/ppermute | solution.py:98
  26.8 1.5 %collective-permute-start.6 = (bf16[4,16,2688]{2,1,0:T(8,128)(2,1)S(1)}, bf16[4,16,2688]{2,1,0:T(8,128)(2,1)}, u32[]{:S(2)}, u32[]{:S(2)}) collective-permute-start(bf16[4,16,2688]{2,1,0:T(8,128)(2,1)S(1)} %pad_maximum_fusion.1.refs_2_), channel_id=1, source_target_pairs={{0,4},{4,0},{8,12},{12,8},{16,20},{20,16},{24,28},{28,24},{1,5},{5... | collective-permute-start | bytes 1032200 | tf_op jit(solution)/shard_map/ppermute | solution.py:98
  28.3 0.5 tables.1
  28.8 0.7 copy-done.1
  29.6 0.7 copy-done.2
  30.3 0.7 copy-done.3
  31.1 0.7 copy-done.7
  31.8 0.7 copy-done.8
  32.5 0.7 copy-done.9
  33.1 2.4 %all-to-all-done.1.got_ref.first_ref = f32[32,16,128]{2,1,0:T(8,128)S(1)} async-done(((f32[32,16,128]{2,1,0:T(8,128)}), f32[32,16,128]{2,1,0:T(8,128)S(1)}, u32[]{:S(2)}, u32[]{:S(2)}) %all-to-all-start.1) | async-done | bytes 262176 | tf_op jit(solution)/shard_map/all_to_all | solution.py:80
  35.5 3.1 %mix.1 = (bf16[32,80,128]{2,1,0:T(8,128)(2,1)}, bf16[16,128,128]{2,1,0:T(8,128)(2,1)S(1)}, f32[16,128]{1,0:T(8,128)S(1)}) custom-call(f32[32,16,128]{2,1,0:T(8,128)S(1)} %all-to-all-done.1.got_ref.first_ref, bf16[16,128,128]{2,1,0:T(8,128)(2,1)S(1)} %maximum_maximum_fusion.mixer_ref), custom_call_target="tpu_custom_call" | custom-call | tf_op jit(solution)/shard_map/mix/pallas_call | solution.py:616
  38.6 4.1 %all-to-all-start.2 = ((bf16[32,80,128]{2,1,0:T(8,128)(2,1)}), bf16[32,80,128]{2,1,0:T(8,128)(2,1)S(1)}, u32[]{:S(2)}, u32[]{:S(2)}) async-start(bf16[32,80,128]{2,1,0:T(8,128)(2,1)} %get-tuple-element.85), calls=%async_computation.2 | async-start | bytes 1310720 | tf_op jit(solution)/shard_map/all_to_all | solution.py:80
  42.9 0.4 collective-permute-start.8
  43.4 0.4 collective-permute-start.10
  43.9 0.6 pad_add_fusion.me_ref
  44.5 0.6 slice.123
  45.3 0.8 collective-permute-done.9.refs_6_
  46.3 14.2 %all-to-all-done.2.refs_8_ = bf16[32,80,128]{2,1,0:T(8,128)(2,1)S(1)} async-done(((bf16[32,80,128]{2,1,0:T(8,128)(2,1)}), bf16[32,80,128]{2,1,0:T(8,128)(2,1)S(1)}, u32[]{:S(2)}, u32[]{:S(2)}) %all-to-all-start.2) | async-done | bytes 655392 | tf_op jit(solution)/shard_map/all_to_all | solution.py:80
  60.5 0.8 copy-done.13
  61.3 38.0 %block.1 = (bf16[32,80,128]{2,1,0:T(8,128)(2,1)}, f32[8,128]{1,0:T(8,128)}, bf16[4,4,16,2560]{3,2,1,0:T(8,128)(2,1)}, bf16[4,4,16,2560]{3,2,1,0:T(8,128)(2,1)}) custom-call(f32[1]{0:T(128)} %bitcast.3.count_ref, s32[2]{0:T(128)} %pad_add_fusion.me_ref, bf16[4,16,2688]{2,1,0:T(8,128)(2,1)} %copy-done.14, bf16[4,16,2688]{2,1,0:T(8,128)(2,1)} %collective-permute-done.2.refs_1_, ...), custom_call_target="tpu_custom_call" | custom-call | tf_op jit(solution)/shard_map/block/pallas_call | solution.py:545
  99.5 3.6 %all-to-all-start.3 = ((bf16[32,80,128]{2,1,0:T(8,128)(2,1)}), bf16[32,80,128]{2,1,0:T(8,128)(2,1)S(1)}, u32[]{:S(2)}, u32[]{:S(2)}) async-start(bf16[32,80,128]{2,1,0:T(8,128)(2,1)} %get-tuple-element.92), calls=%async_computation.3 | async-start | bytes 1310720 | tf_op jit(solution)/shard_map/all_to_all | solution.py:80
  103.2 1.3 fusion.1
  104.4 1.8 %collective-permute-start.13 = (bf16[4,16,2560]{2,1,0:T(8,128)(2,1)S(1)}, bf16[4,16,2560]{2,1,0:T(8,128)(2,1)S(1)}, u32[]{:S(2)}, u32[]{:S(2)}) collective-permute-start(bf16[4,16,2560]{2,1,0:T(8,128)(2,1)S(1)} %get-tuple-element.129), channel_id=1, source_target_pairs={{0,4},{4,0},{8,12},{12,8},{16,20},{20,16},{24,28},{28,24},{1,5},{5... | collective-permute-start | bytes 983048 | tf_op jit(solution)/shard_map/ppermute | solution.py:98
  106.3 1.5 %collective-permute-start.12 = (bf16[4,16,2560]{2,1,0:T(8,128)(2,1)S(1)}, bf16[4,16,2560]{2,1,0:T(8,128)(2,1)S(1)}, u32[]{:S(2)}, u32[]{:S(2)}) collective-permute-start(bf16[4,16,2560]{2,1,0:T(8,128)(2,1)S(1)} %get-tuple-element.130), channel_id=1, source_target_pairs={{0,2},{1,3},{2,0},{3,1},{4,6},{5,7},{6,4},{7,5},{8,10},{9,11},{10,... | collective-permute-start | bytes 983048 | tf_op jit(solution)/shard_map/ppermute | solution.py:98
  107.7 1.1 fusion.15
  108.9 10.6 %collective-permute-done.13 = bf16[4,16,2560]{2,1,0:T(8,128)(2,1)S(1)} collective-permute-done((bf16[4,16,2560]{2,1,0:T(8,128)(2,1)S(1)}, bf16[4,16,2560]{2,1,0:T(8,128)(2,1)S(1)}, u32[]{:S(2)}, u32[]{:S(2)}) %collective-permute-start.13) | collective-permute-done | bytes 327712 | tf_op jit(solution)/shard_map/ppermute | solution.py:98
  119.6 1.0 collective-permute-done.12
  120.6 0.4 all-to-all-done.3.got_ref
  121.0 1.4 collective-permute-start.14
  122.4 1.4 collective-permute-start.15
  123.9 2.1 %mix_back.1 = (f32[32,8,128]{2,1,0:T(8,128)}, bf16[16,128,128]{2,1,0:T(8,128)(2,1)S(1)}, f32[8,128]{1,0:T(8,128)S(1)}) custom-call(bf16[32,80,128]{2,1,0:T(8,128)(2,1)S(1)} %all-to-all-done.3.got_ref, bf16[16,128,128]{2,1,0:T(8,128)(2,1)S(1)} %maximum_maximum_fusion.mixer_ref, f32[32,16,128]{2,1,0:T(8,128)S(1)} %all-to-all-done.1.got_ref.first_ref, ...), custom_call_target="tpu_custom_call" | custom-call | flops 10000000000 | bytes 1000000000 | tf_op jit(solution)/shard_map/mix_back/pallas_call | solution.py:616
  126.0 0.8 copy-done.12
  126.8 3.5 %all-to-all-start.4 = ((f32[32,8,128]{2,1,0:T(8,128)}), f32[32,8,128]{2,1,0:T(8,128)S(1)}, u32[]{:S(2)}, u32[]{:S(2)}) async-start(f32[32,8,128]{2,1,0:T(8,128)} %get-tuple-element.97), calls=%async_computation.4 | async-start | bytes 262144 | tf_op jit(solution)/shard_map/all_to_all | solution.py:80
  130.4 1.8 %collective-permute-start.16 = (bf16[16,2560]{1,0:T(8,128)(2,1)S(1)}, bf16[16,2560]{1,0:T(8,128)(2,1)S(1)}, u32[]{:S(2)}, u32[]{:S(2)}) collective-permute-start(bf16[16,2560]{1,0:T(8,128)(2,1)S(1)} %get-tuple-element.137), channel_id=1, source_target_pairs={{0,8},{4,12},{8,0},{12,4},{16,24},{20,28},{24,16},{28,20},{1,9},{5... | collective-permute-start | bytes 245768 | tf_op jit(solution)/shard_map/ppermute | solution.py:98
  132.3 2.4 %collective-permute-start.18 = (bf16[16,2560]{1,0:T(8,128)(2,1)S(1)}, bf16[16,2560]{1,0:T(8,128)(2,1)S(1)}, u32[]{:S(2)}, u32[]{:S(2)}) collective-permute-start(bf16[16,2560]{1,0:T(8,128)(2,1)S(1)} %get-tuple-element.135), channel_id=1, source_target_pairs={{0,24},{4,28},{8,16},{12,20},{16,8},{20,12},{24,0},{28,4},{1,25},{... | collective-permute-start | bytes 245768 | tf_op jit(solution)/shard_map/ppermute | solution.py:98
  134.9 5.0 %spectral.1 = (f32[2,16,4096]{2,1,0:T(8,128)}, f32[2,16,4096]{2,1,0:T(8,128)}, f32[2,16,4096]{2,1,0:T(8,128)}, f32[2,16,4096]{2,1,0:T(8,128)}, bf16[2,16,4096]{2,1,0:T(8,128)(2,1)}) custom-call(bf16[16,128,128]{2,1,0:T(8,128)(2,1)} %copy-done.10, bf16[16,128,128]{2,1,0:T(8,128)(2,1)} %copy-done.12, f32[2,16,4096]{2,1,0:T(8,128)} %refs_2_.1, ...), custom_call_target="tpu_custom_call" | custom-call | flops 10000000000 | bytes 1000000000 | tf_op jit(solution)/shard_map/spectral/pallas_call | solution.py:616
  139.9 1.2 collective-permute-done.18.refs_3_
  141.2 2.7 %collective-permute-done.17.refs_2_ = bf16[16,2560]{1,0:T(8,128)(2,1)S(1)} collective-permute-done((bf16[16,2560]{1,0:T(8,128)(2,1)S(1)}, bf16[16,2560]{1,0:T(8,128)(2,1)S(1)}, u32[]{:S(2)}, u32[]{:S(2)}) %collective-permute-start.17) | collective-permute-done | bytes 81952 | tf_op jit(solution)/shard_map/ppermute | solution.py:98
  143.9 1.8 %rows.1 = (f32[1,1]{1,0:T(1,128)}, f32[16,5134]{1,0:T(8,128)}, f32[16,5134]{1,0:T(8,128)}, f32[16,5134]{1,0:T(8,128)}, f32[16,5134]{1,0:T(8,128)}, /*index=5*/bf16[16,5134]{1,0:T(8,128)(2,1)}) custom-call(f32[32,8,128]{2,1,0:T(8,128)S(1)} %all-to-all-done.4.got_ref, f32[8,128]{1,0:T(8,128)S(1)} %get-tuple-element.98.thin_ref, ...), custom_call_target="tpu_custom_call" | custom-call | tf_op jit(solution)/shard_map/rows/pallas_call | solution.py:616
  (72 shorter events, 2.9 us)
Async XLA Ops:
  0.6 11.2 %copy-start.17 = (f32[2,16,4096]{2,1,0:T(8,128)S(1)}, f32[2,16,4096]{2,1,0:T(8,128)}, u32[]{:S(2)}) copy-start(f32[2,16,4096]{2,1,0:T(8,128)} %refs_2_.1) | copy-start | bytes 1572868
  2.7 12.8 %collective-permute-start.4 = (bf16[16,2688]{1,0:T(8,128)(2,1)}, bf16[16,2688]{1,0:T(8,128)(2,1)S(1)}, u32[]{:S(2)}, u32[]{:S(2)}) collective-permute-start(bf16[16,2688]{1,0:T(8,128)(2,1)} %get-tuple-element.80), channel_id=1, source_target_pairs={{0,24},{4,28},{8,16},{12,20},{16,8},{20,12},{24,0},{28,4},{1,25},{... | collective-permute-start | bytes 258056 | tf_op jit(solution)/shard_map/ppermute | solution.py:98
  7.8 7.7 %collective-permute-start.3 = (bf16[16,2688]{1,0:T(8,128)(2,1)}, bf16[16,2688]{1,0:T(8,128)(2,1)S(1)}, u32[]{:S(2)}, u32[]{:S(2)}) collective-permute-start(bf16[16,2688]{1,0:T(8,128)(2,1)} %get-tuple-element.80), channel_id=1, source_target_pairs={{0,16},{4,20},{8,24},{12,28},{16,0},{20,4},{24,8},{28,12},{1,17},{... | collective-permute-start | bytes 258056 | tf_op jit(solution)/shard_map/ppermute | solution.py:98
  7.8 5.9 %collective-permute-start = (bf16[16,2688]{1,0:T(8,128)(2,1)}, bf16[16,2688]{1,0:T(8,128)(2,1)S(1)}, u32[]{:S(2)}, u32[]{:S(2)}) collective-permute-start(bf16[16,2688]{1,0:T(8,128)(2,1)} %get-tuple-element.80), channel_id=1, source_target_pairs={{0,8},{4,12},{8,0},{12,4},{16,24},{20,28},{24,16},{28,20},{1,9},{5... | collective-permute-start | bytes 258056 | tf_op jit(solution)/shard_map/ppermute | solution.py:98
  8.5 9.4 %all-to-all-start = ((f32[4,64,192]{2,1,0:T(8,128)}), f32[4,64,192]{2,1,0:T(8,128)S(1)}, u32[]{:S(2)}, u32[]{:S(2)}) async-start(f32[4,64,192]{2,1,0:T(8,128)} %get-tuple-element.70), calls=%async_computation | async-start | bytes 524288 | tf_op jit(solution)/shard_map/all_to_all | solution.py:80
  11.9 0.7 copy-start.19
  12.2 1.5 %copy-start.18 = (bf16[16,2688]{1,0:T(8,128)(2,1)S(1)}, bf16[16,2688]{1,0:T(8,128)(2,1)}, u32[]{:S(2)}) copy-start(bf16[16,2688]{1,0:T(8,128)(2,1)} %get-tuple-element.80) | copy-start | bytes 258052
  12.3 5.6 %copy-start = (f32[16,5134]{1,0:T(8,128)S(1)}, f32[16,5134]{1,0:T(8,128)}, u32[]{:S(2)}) copy-start(f32[16,5134]{1,0:T(8,128)} %w_ref.1) | copy-start | bytes 985732
  13.8 11.0 %collective-permute-start.1 = (bf16[2,16,2688]{2,1,0:T(8,128)(2,1)S(1)}, bf16[2,16,2688]{2,1,0:T(8,128)(2,1)S(1)}, u32[]{:S(2)}, u32[]{:S(2)}) collective-permute-start(bf16[2,16,2688]{2,1,0:T(8,128)(2,1)S(1)} %pad_maximum_fusion.2), channel_id=1, source_target_pairs={{0,4},{4,0},{8,12},{12,8},{16,20},{20,16},{24,28},{28,24},{1,5},{5... | collective-permute-start | bytes 516104 | tf_op jit(solution)/shard_map/ppermute | solution.py:98
  15.5 11.2 %collective-permute-start.5 = (bf16[2,16,2688]{2,1,0:T(8,128)(2,1)S(1)}, bf16[2,16,2688]{2,1,0:T(8,128)(2,1)S(1)}, u32[]{:S(2)}, u32[]{:S(2)}) collective-permute-start(bf16[2,16,2688]{2,1,0:T(8,128)(2,1)S(1)} %pad_maximum_fusion.3), channel_id=1, source_target_pairs={{0,2},{1,3},{2,0},{3,1},{4,6},{5,7},{6,4},{7,5},{8,10},{9,11},{10,... | collective-permute-start | bytes 516104 | tf_op jit(solution)/shard_map/ppermute | solution.py:98
  19.3 16.2 %all-to-all-start.1 = ((f32[32,16,128]{2,1,0:T(8,128)}), f32[32,16,128]{2,1,0:T(8,128)S(1)}, u32[]{:S(2)}, u32[]{:S(2)}) async-start(f32[32,16,128]{2,1,0:T(8,128)} %spectra.1), calls=%async_computation.1 | async-start | bytes 524288 | tf_op jit(solution)/shard_map/all_to_all | solution.py:80
  24.9 17.9 %copy-start.14 = (bf16[4,16,2688]{2,1,0:T(8,128)(2,1)}, bf16[4,16,2688]{2,1,0:T(8,128)(2,1)S(1)}, u32[]{:S(2)}) copy-start(bf16[4,16,2688]{2,1,0:T(8,128)(2,1)S(1)} %pad_maximum_fusion.refs_0_) | copy-start | bytes 1032196
  24.9 13.7 %collective-permute-start.2 = (bf16[4,16,2688]{2,1,0:T(8,128)(2,1)S(1)}, bf16[4,16,2688]{2,1,0:T(8,128)(2,1)}, u32[]{:S(2)}, u32[]{:S(2)}) collective-permute-start(bf16[4,16,2688]{2,1,0:T(8,128)(2,1)S(1)} %pad_maximum_fusion.refs_0_), channel_id=1, source_target_pairs={{0,2},{1,3},{2,0},{3,1},{4,6},{5,7},{6,4},{7,5},{8,10},{9,11},{10,... | collective-permute-start | bytes 1032200 | tf_op jit(solution)/shard_map/ppermute | solution.py:98
  26.8 16.6 %copy-start.15 = (bf16[4,16,2688]{2,1,0:T(8,128)(2,1)}, bf16[4,16,2688]{2,1,0:T(8,128)(2,1)S(1)}, u32[]{:S(2)}) copy-start(bf16[4,16,2688]{2,1,0:T(8,128)(2,1)S(1)} %pad_maximum_fusion.1.refs_2_) | copy-start | bytes 1032196
  26.8 11.8 %collective-permute-start.6 = (bf16[4,16,2688]{2,1,0:T(8,128)(2,1)S(1)}, bf16[4,16,2688]{2,1,0:T(8,128)(2,1)}, u32[]{:S(2)}, u32[]{:S(2)}) collective-permute-start(bf16[4,16,2688]{2,1,0:T(8,128)(2,1)S(1)} %pad_maximum_fusion.1.refs_2_), channel_id=1, source_target_pairs={{0,4},{4,0},{8,12},{12,8},{16,20},{20,16},{24,28},{28,24},{1,5},{5... | collective-permute-start | bytes 1032200 | tf_op jit(solution)/shard_map/ppermute | solution.py:98
  28.8 0.7 copy-start.1
  29.6 0.7 copy-start.2
  30.3 0.7 copy-start.3
  31.1 0.7 copy-start.7
  31.8 0.7 copy-start.8
  32.5 0.7 copy-start.9
  38.6 60.8 %copy-start.10 = (bf16[16,128,128]{2,1,0:T(8,128)(2,1)}, bf16[16,128,128]{2,1,0:T(8,128)(2,1)S(1)}, u32[]{:S(2)}) copy-start(bf16[16,128,128]{2,1,0:T(8,128)(2,1)S(1)} %get-tuple-element.122.refs_0_) | copy-start | bytes 1572868
  38.6 21.9 %all-to-all-start.2 = ((bf16[32,80,128]{2,1,0:T(8,128)(2,1)}), bf16[32,80,128]{2,1,0:T(8,128)(2,1)S(1)}, u32[]{:S(2)}, u32[]{:S(2)}) async-start(bf16[32,80,128]{2,1,0:T(8,128)(2,1)} %get-tuple-element.85), calls=%async_computation.2 | async-start | bytes 1310720 | tf_op jit(solution)/shard_map/all_to_all | solution.py:80
  42.8 2.3 %collective-permute-start.7 = (bf16[4,16,2688]{2,1,0:T(8,128)(2,1)S(1)}, bf16[4,16,2688]{2,1,0:T(8,128)(2,1)}, u32[]{:S(2)}, u32[]{:S(2)}) collective-permute-start(bf16[4,16,2688]{2,1,0:T(8,128)(2,1)S(1)} %pad_maximum_fusion.refs_0_), channel_id=1, source_target_pairs={{0,1},{1,0},{2,3},{3,2},{4,5},{5,4},{6,7},{7,6},{8,9},{9,8},{10,11... | collective-permute-start | bytes 1032200 | tf_op jit(solution)/shard_map/ppermute | solution.py:98
  42.9 2.4 %collective-permute-start.8 = (bf16[4,16,2688]{2,1,0:T(8,128)(2,1)}, bf16[4,16,2688]{2,1,0:T(8,128)(2,1)}, u32[]{:S(2)}, u32[]{:S(2)}) collective-permute-start(bf16[4,16,2688]{2,1,0:T(8,128)(2,1)} %collective-permute-done.2.refs_1_), channel_id=1, source_target_pairs={{0,1},{1,0},{2,3},{3,2},{4,5},{5,4},{6,7},{7,6},{8,9},{9,8},{10,11... | collective-permute-start | bytes 1032200 | tf_op jit(solution)/shard_map/ppermute | solution.py:98
  43.4 2.7 %collective-permute-start.9 = (bf16[4,16,2688]{2,1,0:T(8,128)(2,1)S(1)}, bf16[4,16,2688]{2,1,0:T(8,128)(2,1)}, u32[]{:S(2)}, u32[]{:S(2)}) collective-permute-start(bf16[4,16,2688]{2,1,0:T(8,128)(2,1)S(1)} %pad_maximum_fusion.1.refs_2_), channel_id=1, source_target_pairs={{0,1},{1,0},{2,3},{3,2},{4,5},{5,4},{6,7},{7,6},{8,9},{9,8},{10,11... | collective-permute-start | bytes 1032200 | tf_op jit(solution)/shard_map/ppermute | solution.py:98
  43.4 2.9 %collective-permute-start.10 = (bf16[4,16,2688]{2,1,0:T(8,128)(2,1)}, bf16[4,16,2688]{2,1,0:T(8,128)(2,1)}, u32[]{:S(2)}, u32[]{:S(2)}) collective-permute-start(bf16[4,16,2688]{2,1,0:T(8,128)(2,1)} %collective-permute-done.6.refs_3_), channel_id=1, source_target_pairs={{0,1},{1,0},{2,3},{3,2},{4,5},{5,4},{6,7},{7,6},{8,9},{9,8},{10,11... | collective-permute-start | bytes 1032200 | tf_op jit(solution)/shard_map/ppermute | solution.py:98
  60.5 0.8 copy-start.13
  99.4 3.7 %copy-start.16 = (bf16[4,4,16,2560]{3,2,1,0:T(8,128)(2,1)S(1)}, bf16[4,4,16,2560]{3,2,1,0:T(8,128)(2,1)}, u32[]{:S(2)}) copy-start(bf16[4,4,16,2560]{3,2,1,0:T(8,128)(2,1)} %get-tuple-element.93) | copy-start | bytes 3932164
  99.4 3.8 %collective-permute-start.11 = (bf16[4,4,16,2560]{3,2,1,0:T(8,128)(2,1)}, bf16[4,4,16,2560]{3,2,1,0:T(8,128)(2,1)}, u32[]{:S(2)}, u32[]{:S(2)}) collective-permute-start(bf16[4,4,16,2560]{3,2,1,0:T(8,128)(2,1)} %get-tuple-element.94), channel_id=1, source_target_pairs={{0,1},{1,0},{2,3},{3,2},{4,5},{5,4},{6,7},{7,6},{8,9},{9,8},{10,11... | collective-permute-start | bytes 3932168 | tf_op jit(solution)/shard_map/ppermute | solution.py:98
  99.5 21.5 %all-to-all-start.3 = ((bf16[32,80,128]{2,1,0:T(8,128)(2,1)}), bf16[32,80,128]{2,1,0:T(8,128)(2,1)S(1)}, u32[]{:S(2)}, u32[]{:S(2)}) async-start(bf16[32,80,128]{2,1,0:T(8,128)(2,1)} %get-tuple-element.92), calls=%async_computation.3 | async-start | bytes 1310720 | tf_op jit(solution)/shard_map/all_to_all | solution.py:80
  104.4 15.0 %collective-permute-start.13 = (bf16[4,16,2560]{2,1,0:T(8,128)(2,1)S(1)}, bf16[4,16,2560]{2,1,0:T(8,128)(2,1)S(1)}, u32[]{:S(2)}, u32[]{:S(2)}) collective-permute-start(bf16[4,16,2560]{2,1,0:T(8,128)(2,1)S(1)} %get-tuple-element.129), channel_id=1, source_target_pairs={{0,4},{4,0},{8,12},{12,8},{16,20},{20,16},{24,28},{28,24},{1,5},{5... | collective-permute-start | bytes 983048 | tf_op jit(solution)/shard_map/ppermute | solution.py:98
  106.3 14.2 %collective-permute-start.12 = (bf16[4,16,2560]{2,1,0:T(8,128)(2,1)S(1)}, bf16[4,16,2560]{2,1,0:T(8,128)(2,1)S(1)}, u32[]{:S(2)}, u32[]{:S(2)}) collective-permute-start(bf16[4,16,2560]{2,1,0:T(8,128)(2,1)S(1)} %get-tuple-element.130), channel_id=1, source_target_pairs={{0,2},{1,3},{2,0},{3,1},{4,6},{5,7},{6,4},{7,5},{8,10},{9,11},{10,... | collective-permute-start | bytes 983048 | tf_op jit(solution)/shard_map/ppermute | solution.py:98
  108.9 15.0 %copy-start.11 = (f32[8,128]{1,0:T(8,128)S(1)}, f32[8,128]{1,0:T(8,128)}, u32[]{:S(2)}) copy-start(f32[8,128]{1,0:T(8,128)} %get-tuple-element.96.stat_ref) | copy-start | bytes 12292
  121.0 9.3 %collective-permute-start.14 = (bf16[2,16,2560]{2,1,0:T(8,128)(2,1)S(1)}, bf16[2,16,2560]{2,1,0:T(8,128)(2,1)S(1)}, u32[]{:S(2)}, u32[]{:S(2)}) collective-permute-start(bf16[2,16,2560]{2,1,0:T(8,128)(2,1)S(1)} %fusion.9), channel_id=1, source_target_pairs={{0,4},{4,0},{8,12},{12,8},{16,20},{20,16},{24,28},{28,24},{1,5},{5... | collective-permute-start | bytes 491528 | tf_op jit(solution)/shard_map/ppermute | solution.py:98
  122.4 7.9 %collective-permute-start.15 = (bf16[2,16,2560]{2,1,0:T(8,128)(2,1)S(1)}, bf16[2,16,2560]{2,1,0:T(8,128)(2,1)S(1)}, u32[]{:S(2)}, u32[]{:S(2)}) collective-permute-start(bf16[2,16,2560]{2,1,0:T(8,128)(2,1)S(1)} %fusion.10), channel_id=1, source_target_pairs={{0,2},{1,3},{2,0},{3,1},{4,6},{5,7},{6,4},{7,5},{8,10},{9,11},{10,... | collective-permute-start | bytes 491528 | tf_op jit(solution)/shard_map/ppermute | solution.py:98
  126.0 0.8 copy-start.12
  126.8 17.1 %all-to-all-start.4 = ((f32[32,8,128]{2,1,0:T(8,128)}), f32[32,8,128]{2,1,0:T(8,128)S(1)}, u32[]{:S(2)}, u32[]{:S(2)}) async-start(f32[32,8,128]{2,1,0:T(8,128)} %get-tuple-element.97), calls=%async_computation.4 | async-start | bytes 262144 | tf_op jit(solution)/shard_map/all_to_all | solution.py:80
  130.4 9.5 %collective-permute-start.16 = (bf16[16,2560]{1,0:T(8,128)(2,1)S(1)}, bf16[16,2560]{1,0:T(8,128)(2,1)S(1)}, u32[]{:S(2)}, u32[]{:S(2)}) collective-permute-start(bf16[16,2560]{1,0:T(8,128)(2,1)S(1)} %get-tuple-element.137), channel_id=1, source_target_pairs={{0,8},{4,12},{8,0},{12,4},{16,24},{20,28},{24,16},{28,20},{1,9},{5... | collective-permute-start | bytes 245768 | tf_op jit(solution)/shard_map/ppermute | solution.py:98
  132.3 8.9 %collective-permute-start.18 = (bf16[16,2560]{1,0:T(8,128)(2,1)S(1)}, bf16[16,2560]{1,0:T(8,128)(2,1)S(1)}, u32[]{:S(2)}, u32[]{:S(2)}) collective-permute-start(bf16[16,2560]{1,0:T(8,128)(2,1)S(1)} %get-tuple-element.135), channel_id=1, source_target_pairs={{0,24},{4,28},{8,16},{12,20},{16,8},{20,12},{24,0},{28,4},{1,25},{... | collective-permute-start | bytes 245768 | tf_op jit(solution)/shard_map/ppermute | solution.py:98
  134.7 9.1 %collective-permute-start.17 = (bf16[16,2560]{1,0:T(8,128)(2,1)S(1)}, bf16[16,2560]{1,0:T(8,128)(2,1)S(1)}, u32[]{:S(2)}, u32[]{:S(2)}) collective-permute-start(bf16[16,2560]{1,0:T(8,128)(2,1)S(1)} %get-tuple-element.136), channel_id=1, source_target_pairs={{0,16},{4,20},{8,24},{12,28},{16,0},{20,4},{24,8},{28,12},{1,17},{... | collective-permute-start | bytes 245768 | tf_op jit(solution)/shard_map/ppermute | solution.py:98
  134.9 9.0 %copy-start.4 = (f32[16,5134]{1,0:T(8,128)S(1)}, f32[16,5134]{1,0:T(8,128)}, u32[]{:S(2)}) copy-start(f32[16,5134]{1,0:T(8,128)} %m_ref.1) | copy-start | bytes 985732
  134.9 9.0 %copy-start.5 = (f32[16,5134]{1,0:T(8,128)S(1)}, f32[16,5134]{1,0:T(8,128)}, u32[]{:S(2)}) copy-start(f32[16,5134]{1,0:T(8,128)} %v_ref.1) | copy-start | bytes 985732
  134.9 9.0 %copy-start.6 = (f32[16,5134]{1,0:T(8,128)S(1)}, f32[16,5134]{1,0:T(8,128)}, u32[]{:S(2)}) copy-start(f32[16,5134]{1,0:T(8,128)} %ema_ref.1) | copy-start | bytes 985732

commit v4 on v3

--- a/solution.py
+++ b/solution.py
@@ -207,7 +207,7 @@
 TN = (((0,), (0,)), ((), ()))
 FIRST = 2.0 * math.sqrt(2.0 / math.pi)
 THIRD = FIRST * 0.044715
-GATES = 512
+GATES = 1024
 UNROLL = 4
 LEAD = 8
 HALF = 64
@@ -737,10 +737,11 @@
             blocks = [block if g == k else zero for g in range(nb)]
             spread.append(jnp.concatenate(blocks, axis=1))
     spread = jnp.concatenate(spread, axis=0)
-    inner = got.reshape(n_all * 16, LANES)[:, : 2 * nb * LEAD]
-    spec = lax.dot_general(
-        inner, spread, NN, precision=lax.Precision.HIGHEST, preferred_element_type=F32
-    )
+    inner = got.reshape(n_all * 16, LANES)
+    inner = by_halves(fold(jnp.where(iota(inner.shape, 1) < HALF, inner, 0.0)))
+    high, low = split(rows_at(spread, 0, HALF))
+    spec = mm(inner, jnp.concatenate([high, high], axis=0).astype(BF))
+    spec += mm(inner, jnp.concatenate([low, jnp.zeros_like(low)], axis=0).astype(BF))
     for k in range(nb):
         wide_ref[k] = spec[:, k * LANES : (k + 1) * LANES]
     for m in range(modes):

time: 146 us -> 145 us (level)
  Pallas kernels: 54.1 us -> 52.2 us
  transfers between devices with their start and end apart: 24 -> 24, of which waited for: 11 -> 12; matrix products, arithmetic and copies ran while one was open for 4% -> 4% of each run, Pallas kernels for 8% -> 8%
where the time goes in v4:
time: 145 us; the launch traced here: 144 us
  Pallas kernels  52.2 us (36%)
  starting transfers between devices  44.7 us (31%)
  waiting for transfers between devices  34.6 us (24%)
  local copies, waits for them, and re-layouts  8.29 us (6%)
  other arithmetic  3.5 us (2%)
    pallas_call x1, Pallas kernels, block(): pl.pallas_call(partial(block_kernel, sizes), out_shape=(jax.ShapeDtypeStr...  36.7 us
    ppermute x19, starting transfers between devices, by_xor(): lax.ppermute(x, axis, [(index, index ^ step) for index in range(count)])  24.6 us
    all_to_all x5, starting transfers between devices, exchange(): return lax.all_to_all(x, axes, 0, 0, tiled=True)  20.1 us
    all_to_all x5, waiting for transfers between devices, exchange(): return lax.all_to_all(x, axes, 0, 0, tiled=True)  17.3 us
    ppermute x19, waiting for transfers between devices, by_xor(): lax.ppermute(x, axis, [(index, index ^ step) for index in range(count)])  17.3 us
    pallas_call x7, Pallas kernels, call(): pl.pallas_call(kernel, out_shape=outs, in_specs=in_specs, out_specs=jax.t...  15.5 us
    unnamed x40, local copies, waits for them, and re-layouts  5.99 us
  transfers between devices with their start and end apart: 24, of which 12 were waited for; matrix products, arithmetic and copies ran while one was open for 4% of the time, Pallas kernels for 8%

profile of v4, /device:TPU:0, one launch (start us, length us, event | category | flops | bytes accessed | tf_op | source)
XLA Modules:
  0.0 144.3 jit_solution(9420869315209190493)
XLA Ops:
  0.7 2.0 %pack.1 = (f32[4,64,192]{2,1,0:T(8,128)}, bf16[16,2688]{1,0:T(8,128)(2,1)}) custom-call(bf16[7,16,192]{2,1,0:T(8,128)(2,1)} %bitcast.102, f32[7,16,192]{2,1,0:T(8,128)} %bitcast.101, s32[16,192]{1,0:T(8,128)} %bitcast.103, f32[16,5134]{1,0:T(8,128)} %w_ref.1), custom_call_target="tpu_custom_call" | custom-call | tf_op jit(solution)/shard_map/pack/pallas_call | solution.py:616
  2.7 5.1 %collective-permute-start.4 = (bf16[16,2688]{1,0:T(8,128)(2,1)}, bf16[16,2688]{1,0:T(8,128)(2,1)S(1)}, u32[]{:S(2)}, u32[]{:S(2)}) collective-permute-start(bf16[16,2688]{1,0:T(8,128)(2,1)} %get-tuple-element.80), channel_id=1, source_target_pairs={{0,24},{4,28},{8,16},{12,20},{16,8},{20,12},{24,0},{28,4},{1,25},{... | collective-permute-start | bytes 258056 | tf_op jit(solution)/shard_map/ppermute | solution.py:98
  7.8 0.6 collective-permute-start
  8.5 3.4 %all-to-all-start = ((f32[4,64,192]{2,1,0:T(8,128)}), f32[4,64,192]{2,1,0:T(8,128)S(1)}, u32[]{:S(2)}, u32[]{:S(2)}) async-start(f32[4,64,192]{2,1,0:T(8,128)} %get-tuple-element.70), calls=%async_computation | async-start | bytes 524288 | tf_op jit(solution)/shard_map/all_to_all | solution.py:80
  12.6 0.9 fusion.6
  13.8 1.7 %collective-permute-start.1 = (bf16[2,16,2688]{2,1,0:T(8,128)(2,1)S(1)}, bf16[2,16,2688]{2,1,0:T(8,128)(2,1)S(1)}, u32[]{:S(2)}, u32[]{:S(2)}) collective-permute-start(bf16[2,16,2688]{2,1,0:T(8,128)(2,1)S(1)} %pad_maximum_fusion.2), channel_id=1, source_target_pairs={{0,4},{4,0},{8,12},{12,8},{16,20},{20,16},{24,28},{28,24},{1,5},{5... | collective-permute-start | bytes 516104 | tf_op jit(solution)/shard_map/ppermute | solution.py:98
  15.5 2.0 %collective-permute-start.5 = (bf16[2,16,2688]{2,1,0:T(8,128)(2,1)S(1)}, bf16[2,16,2688]{2,1,0:T(8,128)(2,1)S(1)}, u32[]{:S(2)}, u32[]{:S(2)}) collective-permute-start(bf16[2,16,2688]{2,1,0:T(8,128)(2,1)S(1)} %pad_maximum_fusion.3), channel_id=1, source_target_pairs={{0,2},{1,3},{2,0},{3,1},{4,6},{5,7},{6,4},{7,5},{8,10},{9,11},{10,... | collective-permute-start | bytes 516104 | tf_op jit(solution)/shard_map/ppermute | solution.py:98
  17.9 1.4 spectra.1
  19.3 5.5 %all-to-all-start.1 = ((f32[32,16,128]{2,1,0:T(8,128)}), f32[32,16,128]{2,1,0:T(8,128)S(1)}, u32[]{:S(2)}, u32[]{:S(2)}) async-start(f32[32,16,128]{2,1,0:T(8,128)} %spectra.1), calls=%async_computation.1 | async-start | bytes 524288 | tf_op jit(solution)/shard_map/all_to_all | solution.py:80
  24.9 1.8 %collective-permute-start.2 = (bf16[4,16,2688]{2,1,0:T(8,128)(2,1)S(1)}, bf16[4,16,2688]{2,1,0:T(8,128)(2,1)}, u32[]{:S(2)}, u32[]{:S(2)}) collective-permute-start(bf16[4,16,2688]{2,1,0:T(8,128)(2,1)S(1)} %pad_maximum_fusion.refs_0_), channel_id=1, source_target_pairs={{0,2},{1,3},{2,0},{3,1},{4,6},{5,7},{6,4},{7,5},{8,10},{9,11},{10,... | collective-permute-start | bytes 1032200 | tf_op jit(solution)/shard_map/ppermute | solution.py:98
  26.8 1.5 %collective-permute-start.6 = (bf16[4,16,2688]{2,1,0:T(8,128)(2,1)S(1)}, bf16[4,16,2688]{2,1,0:T(8,128)(2,1)}, u32[]{:S(2)}, u32[]{:S(2)}) collective-permute-start(bf16[4,16,2688]{2,1,0:T(8,128)(2,1)S(1)} %pad_maximum_fusion.1.refs_2_), channel_id=1, source_target_pairs={{0,4},{4,0},{8,12},{12,8},{16,20},{20,16},{24,28},{28,24},{1,5},{5... | collective-permute-start | bytes 1032200 | tf_op jit(solution)/shard_map/ppermute | solution.py:98
  28.3 0.5 tables.1
  28.8 0.7 copy-done.1
  29.6 0.7 copy-done.2
  30.3 0.7 copy-done.3
  31.1 0.7 copy-done.7
  31.8 0.7 copy-done.8
  32.5 0.7 copy-done.9
  33.1 2.4 %all-to-all-done.1.got_ref.first_ref = f32[32,16,128]{2,1,0:T(8,128)S(1)} async-done(((f32[32,16,128]{2,1,0:T(8,128)}), f32[32,16,128]{2,1,0:T(8,128)S(1)}, u32[]{:S(2)}, u32[]{:S(2)}) %all-to-all-start.1) | async-done | bytes 262176 | tf_op jit(solution)/shard_map/all_to_all | solution.py:80
  35.5 2.6 %mix.1 = (bf16[32,80,128]{2,1,0:T(8,128)(2,1)}, bf16[16,128,128]{2,1,0:T(8,128)(2,1)S(1)}, f32[16,128]{1,0:T(8,128)S(1)}) custom-call(f32[32,16,128]{2,1,0:T(8,128)S(1)} %all-to-all-done.1.got_ref.first_ref, bf16[16,128,128]{2,1,0:T(8,128)(2,1)S(1)} %maximum_maximum_fusion.mixer_ref), custom_call_target="tpu_custom_call" | custom-call | tf_op jit(solution)/shard_map/mix/pallas_call | solution.py:616
  38.1 0.6 collective-permute-done.6.refs_3_
  38.6 4.1 %all-to-all-start.2 = ((bf16[32,80,128]{2,1,0:T(8,128)(2,1)}), bf16[32,80,128]{2,1,0:T(8,128)(2,1)S(1)}, u32[]{:S(2)}, u32[]{:S(2)}) async-start(bf16[32,80,128]{2,1,0:T(8,128)(2,1)} %get-tuple-element.85), calls=%async_computation.2 | async-start | bytes 1310720 | tf_op jit(solution)/shard_map/all_to_all | solution.py:80
  42.9 0.4 collective-permute-start.8
  43.4 0.4 collective-permute-start.10
  43.9 0.6 pad_add_fusion.me_ref
  44.5 0.6 slice.123
  45.3 0.8 collective-permute-done.9.refs_6_
  46.3 14.2 %all-to-all-done.2.refs_8_ = bf16[32,80,128]{2,1,0:T(8,128)(2,1)S(1)} async-done(((bf16[32,80,128]{2,1,0:T(8,128)(2,1)}), bf16[32,80,128]{2,1,0:T(8,128)(2,1)S(1)}, u32[]{:S(2)}, u32[]{:S(2)}) %all-to-all-start.2) | async-done | bytes 655392 | tf_op jit(solution)/shard_map/all_to_all | solution.py:80
  60.5 0.8 copy-done.13
  61.3 36.7 %block.1 = (bf16[32,80,128]{2,1,0:T(8,128)(2,1)}, f32[8,128]{1,0:T(8,128)}, bf16[4,4,16,2560]{3,2,1,0:T(8,128)(2,1)}, bf16[4,4,16,2560]{3,2,1,0:T(8,128)(2,1)}) custom-call(f32[1]{0:T(128)} %bitcast.3.count_ref, s32[2]{0:T(128)} %pad_add_fusion.me_ref, bf16[4,16,2688]{2,1,0:T(8,128)(2,1)} %copy-done.14, bf16[4,16,2688]{2,1,0:T(8,128)(2,1)} %collective-permute-done.2.refs_1_, ...), custom_call_target="tpu_custom_call" | custom-call | tf_op jit(solution)/shard_map/block/pallas_call | solution.py:545
  98.2 3.6 %all-to-all-start.3 = ((bf16[32,80,128]{2,1,0:T(8,128)(2,1)}), bf16[32,80,128]{2,1,0:T(8,128)(2,1)S(1)}, u32[]{:S(2)}, u32[]{:S(2)}) async-start(bf16[32,80,128]{2,1,0:T(8,128)(2,1)} %get-tuple-element.92), calls=%async_computation.3 | async-start | bytes 1310720 | tf_op jit(solution)/shard_map/all_to_all | solution.py:80
  101.8 1.3 fusion.1
  103.1 1.8 %collective-permute-start.13 = (bf16[4,16,2560]{2,1,0:T(8,128)(2,1)S(1)}, bf16[4,16,2560]{2,1,0:T(8,128)(2,1)S(1)}, u32[]{:S(2)}, u32[]{:S(2)}) collective-permute-start(bf16[4,16,2560]{2,1,0:T(8,128)(2,1)S(1)} %get-tuple-element.129), channel_id=1, source_target_pairs={{0,4},{4,0},{8,12},{12,8},{16,20},{20,16},{24,28},{28,24},{1,5},{5... | collective-permute-start | bytes 983048 | tf_op jit(solution)/shard_map/ppermute | solution.py:98
  104.9 1.5 %collective-permute-start.12 = (bf16[4,16,2560]{2,1,0:T(8,128)(2,1)S(1)}, bf16[4,16,2560]{2,1,0:T(8,128)(2,1)S(1)}, u32[]{:S(2)}, u32[]{:S(2)}) collective-permute-start(bf16[4,16,2560]{2,1,0:T(8,128)(2,1)S(1)} %get-tuple-element.130), channel_id=1, source_target_pairs={{0,2},{1,3},{2,0},{3,1},{4,6},{5,7},{6,4},{7,5},{8,10},{9,11},{10,... | collective-permute-start | bytes 983048 | tf_op jit(solution)/shard_map/ppermute | solution.py:98
  106.4 1.1 fusion.15
  107.6 10.6 %collective-permute-done.13 = bf16[4,16,2560]{2,1,0:T(8,128)(2,1)S(1)} collective-permute-done((bf16[4,16,2560]{2,1,0:T(8,128)(2,1)S(1)}, bf16[4,16,2560]{2,1,0:T(8,128)(2,1)S(1)}, u32[]{:S(2)}, u32[]{:S(2)}) %collective-permute-start.13) | collective-permute-done | bytes 327712 | tf_op jit(solution)/shard_map/ppermute | solution.py:98
  118.2 1.0 collective-permute-done.12
  119.7 1.4 collective-permute-start.14
  121.1 1.4 collective-permute-start.15
  122.5 2.1 %mix_back.1 = (f32[32,8,128]{2,1,0:T(8,128)}, bf16[16,128,128]{2,1,0:T(8,128)(2,1)S(1)}, f32[8,128]{1,0:T(8,128)S(1)}) custom-call(bf16[32,80,128]{2,1,0:T(8,128)(2,1)S(1)} %all-to-all-done.3.got_ref, bf16[16,128,128]{2,1,0:T(8,128)(2,1)S(1)} %maximum_maximum_fusion.mixer_ref, f32[32,16,128]{2,1,0:T(8,128)S(1)} %all-to-all-done.1.got_ref.first_ref, ...), custom_call_target="tpu_custom_call" | custom-call | flops 10000000000 | bytes 1000000000 | tf_op jit(solution)/shard_map/mix_back/pallas_call | solution.py:616
  124.7 0.8 copy-done.12
  125.5 3.5 %all-to-all-start.4 = ((f32[32,8,128]{2,1,0:T(8,128)}), f32[32,8,128]{2,1,0:T(8,128)S(1)}, u32[]{:S(2)}, u32[]{:S(2)}) async-start(f32[32,8,128]{2,1,0:T(8,128)} %get-tuple-element.97), calls=%async_computation.4 | async-start | bytes 262144 | tf_op jit(solution)/shard_map/all_to_all | solution.py:80
  129.0 1.8 %collective-permute-start.16 = (bf16[16,2560]{1,0:T(8,128)(2,1)S(1)}, bf16[16,2560]{1,0:T(8,128)(2,1)S(1)}, u32[]{:S(2)}, u32[]{:S(2)}) collective-permute-start(bf16[16,2560]{1,0:T(8,128)(2,1)S(1)} %get-tuple-element.137), channel_id=1, source_target_pairs={{0,8},{4,12},{8,0},{12,4},{16,24},{20,28},{24,16},{28,20},{1,9},{5... | collective-permute-start | bytes 245768 | tf_op jit(solution)/shard_map/ppermute | solution.py:98
  131.0 2.4 %collective-permute-start.18 = (bf16[16,2560]{1,0:T(8,128)(2,1)S(1)}, bf16[16,2560]{1,0:T(8,128)(2,1)S(1)}, u32[]{:S(2)}, u32[]{:S(2)}) collective-permute-start(bf16[16,2560]{1,0:T(8,128)(2,1)S(1)} %get-tuple-element.135), channel_id=1, source_target_pairs={{0,24},{4,28},{8,16},{12,20},{16,8},{20,12},{24,0},{28,4},{1,25},{... | collective-permute-start | bytes 245768 | tf_op jit(solution)/shard_map/ppermute | solution.py:98
  133.5 5.0 %spectral.1 = (f32[2,16,4096]{2,1,0:T(8,128)}, f32[2,16,4096]{2,1,0:T(8,128)}, f32[2,16,4096]{2,1,0:T(8,128)}, f32[2,16,4096]{2,1,0:T(8,128)}, bf16[2,16,4096]{2,1,0:T(8,128)(2,1)}) custom-call(bf16[16,128,128]{2,1,0:T(8,128)(2,1)} %copy-done.10, bf16[16,128,128]{2,1,0:T(8,128)(2,1)} %copy-done.12, f32[2,16,4096]{2,1,0:T(8,128)} %refs_2_.1, ...), custom_call_target="tpu_custom_call" | custom-call | flops 10000000000 | bytes 1000000000 | tf_op jit(solution)/shard_map/spectral/pallas_call | solution.py:616
  138.6 1.3 collective-permute-done.18.refs_3_
  139.8 2.7 %collective-permute-done.17.refs_2_ = bf16[16,2560]{1,0:T(8,128)(2,1)S(1)} collective-permute-done((bf16[16,2560]{1,0:T(8,128)(2,1)S(1)}, bf16[16,2560]{1,0:T(8,128)(2,1)S(1)}, u32[]{:S(2)}, u32[]{:S(2)}) %collective-permute-start.17) | collective-permute-done | bytes 81952 | tf_op jit(solution)/shard_map/ppermute | solution.py:98
  142.5 1.8 %rows.1 = (f32[1,1]{1,0:T(1,128)}, f32[16,5134]{1,0:T(8,128)}, f32[16,5134]{1,0:T(8,128)}, f32[16,5134]{1,0:T(8,128)}, f32[16,5134]{1,0:T(8,128)}, /*index=5*/bf16[16,5134]{1,0:T(8,128)(2,1)}) custom-call(f32[32,8,128]{2,1,0:T(8,128)S(1)} %all-to-all-done.4.got_ref, f32[8,128]{1,0:T(8,128)S(1)} %get-tuple-element.98.thin_ref, ...), custom_call_target="tpu_custom_call" | custom-call | tf_op jit(solution)/shard_map/rows/pallas_call | solution.py:616
  (72 shorter events, 3.3 us)
Async XLA Ops:
  0.6 11.2 %copy-start.17 = (f32[2,16,4096]{2,1,0:T(8,128)S(1)}, f32[2,16,4096]{2,1,0:T(8,128)}, u32[]{:S(2)}) copy-start(f32[2,16,4096]{2,1,0:T(8,128)} %refs_2_.1) | copy-start | bytes 1572868
  2.7 12.8 %collective-permute-start.4 = (bf16[16,2688]{1,0:T(8,128)(2,1)}, bf16[16,2688]{1,0:T(8,128)(2,1)S(1)}, u32[]{:S(2)}, u32[]{:S(2)}) collective-permute-start(bf16[16,2688]{1,0:T(8,128)(2,1)} %get-tuple-element.80), channel_id=1, source_target_pairs={{0,24},{4,28},{8,16},{12,20},{16,8},{20,12},{24,0},{28,4},{1,25},{... | collective-permute-start | bytes 258056 | tf_op jit(solution)/shard_map/ppermute | solution.py:98
  7.8 7.7 %collective-permute-start.3 = (bf16[16,2688]{1,0:T(8,128)(2,1)}, bf16[16,2688]{1,0:T(8,128)(2,1)S(1)}, u32[]{:S(2)}, u32[]{:S(2)}) collective-permute-start(bf16[16,2688]{1,0:T(8,128)(2,1)} %get-tuple-element.80), channel_id=1, source_target_pairs={{0,16},{4,20},{8,24},{12,28},{16,0},{20,4},{24,8},{28,12},{1,17},{... | collective-permute-start | bytes 258056 | tf_op jit(solution)/shard_map/ppermute | solution.py:98
  7.8 5.9 %collective-permute-start = (bf16[16,2688]{1,0:T(8,128)(2,1)}, bf16[16,2688]{1,0:T(8,128)(2,1)S(1)}, u32[]{:S(2)}, u32[]{:S(2)}) collective-permute-start(bf16[16,2688]{1,0:T(8,128)(2,1)} %get-tuple-element.80), channel_id=1, source_target_pairs={{0,8},{4,12},{8,0},{12,4},{16,24},{20,28},{24,16},{28,20},{1,9},{5... | collective-permute-start | bytes 258056 | tf_op jit(solution)/shard_map/ppermute | solution.py:98
  8.5 9.4 %all-to-all-start = ((f32[4,64,192]{2,1,0:T(8,128)}), f32[4,64,192]{2,1,0:T(8,128)S(1)}, u32[]{:S(2)}, u32[]{:S(2)}) async-start(f32[4,64,192]{2,1,0:T(8,128)} %get-tuple-element.70), calls=%async_computation | async-start | bytes 524288 | tf_op jit(solution)/shard_map/all_to_all | solution.py:80
  11.9 0.7 copy-start.19
  12.2 1.5 %copy-start.18 = (bf16[16,2688]{1,0:T(8,128)(2,1)S(1)}, bf16[16,2688]{1,0:T(8,128)(2,1)}, u32[]{:S(2)}) copy-start(bf16[16,2688]{1,0:T(8,128)(2,1)} %get-tuple-element.80) | copy-start | bytes 258052
  12.3 5.6 %copy-start = (f32[16,5134]{1,0:T(8,128)S(1)}, f32[16,5134]{1,0:T(8,128)}, u32[]{:S(2)}) copy-start(f32[16,5134]{1,0:T(8,128)} %w_ref.1) | copy-start | bytes 985732
  13.8 11.0 %collective-permute-start.1 = (bf16[2,16,2688]{2,1,0:T(8,128)(2,1)S(1)}, bf16[2,16,2688]{2,1,0:T(8,128)(2,1)S(1)}, u32[]{:S(2)}, u32[]{:S(2)}) collective-permute-start(bf16[2,16,2688]{2,1,0:T(8,128)(2,1)S(1)} %pad_maximum_fusion.2), channel_id=1, source_target_pairs={{0,4},{4,0},{8,12},{12,8},{16,20},{20,16},{24,28},{28,24},{1,5},{5... | collective-permute-start | bytes 516104 | tf_op jit(solution)/shard_map/ppermute | solution.py:98
  15.5 11.2 %collective-permute-start.5 = (bf16[2,16,2688]{2,1,0:T(8,128)(2,1)S(1)}, bf16[2,16,2688]{2,1,0:T(8,128)(2,1)S(1)}, u32[]{:S(2)}, u32[]{:S(2)}) collective-permute-start(bf16[2,16,2688]{2,1,0:T(8,128)(2,1)S(1)} %pad_maximum_fusion.3), channel_id=1, source_target_pairs={{0,2},{1,3},{2,0},{3,1},{4,6},{5,7},{6,4},{7,5},{8,10},{9,11},{10,... | collective-permute-start | bytes 516104 | tf_op jit(solution)/shard_map/ppermute | solution.py:98
  19.3 16.2 %all-to-all-start.1 = ((f32[32,16,128]{2,1,0:T(8,128)}), f32[32,16,128]{2,1,0:T(8,128)S(1)}, u32[]{:S(2)}, u32[]{:S(2)}) async-start(f32[32,16,128]{2,1,0:T(8,128)} %spectra.1), calls=%async_computation.1 | async-start | bytes 524288 | tf_op jit(solution)/shard_map/all_to_all | solution.py:80
  24.9 17.9 %copy-start.14 = (bf16[4,16,2688]{2,1,0:T(8,128)(2,1)}, bf16[4,16,2688]{2,1,0:T(8,128)(2,1)S(1)}, u32[]{:S(2)}) copy-start(bf16[4,16,2688]{2,1,0:T(8,128)(2,1)S(1)} %pad_maximum_fusion.refs_0_) | copy-start | bytes 1032196
  24.9 13.2 %collective-permute-start.2 = (bf16[4,16,2688]{2,1,0:T(8,128)(2,1)S(1)}, bf16[4,16,2688]{2,1,0:T(8,128)(2,1)}, u32[]{:S(2)}, u32[]{:S(2)}) collective-permute-start(bf16[4,16,2688]{2,1,0:T(8,128)(2,1)S(1)} %pad_maximum_fusion.refs_0_), channel_id=1, source_target_pairs={{0,2},{1,3},{2,0},{3,1},{4,6},{5,7},{6,4},{7,5},{8,10},{9,11},{10,... | collective-permute-start | bytes 1032200 | tf_op jit(solution)/shard_map/ppermute | solution.py:98
  26.8 16.6 %copy-start.15 = (bf16[4,16,2688]{2,1,0:T(8,128)(2,1)}, bf16[4,16,2688]{2,1,0:T(8,128)(2,1)S(1)}, u32[]{:S(2)}) copy-start(bf16[4,16,2688]{2,1,0:T(8,128)(2,1)S(1)} %pad_maximum_fusion.1.refs_2_) | copy-start | bytes 1032196
  26.8 11.8 %collective-permute-start.6 = (bf16[4,16,2688]{2,1,0:T(8,128)(2,1)S(1)}, bf16[4,16,2688]{2,1,0:T(8,128)(2,1)}, u32[]{:S(2)}, u32[]{:S(2)}) collective-permute-start(bf16[4,16,2688]{2,1,0:T(8,128)(2,1)S(1)} %pad_maximum_fusion.1.refs_2_), channel_id=1, source_target_pairs={{0,4},{4,0},{8,12},{12,8},{16,20},{20,16},{24,28},{28,24},{1,5},{5... | collective-permute-start | bytes 1032200 | tf_op jit(solution)/shard_map/ppermute | solution.py:98
  28.8 0.7 copy-start.1
  29.6 0.7 copy-start.2
  30.3 0.7 copy-start.3
  31.1 0.7 copy-start.7
  31.8 0.7 copy-start.8
  32.5 0.7 copy-start.9
  38.1 60.0 %copy-start.10 = (bf16[16,128,128]{2,1,0:T(8,128)(2,1)}, bf16[16,128,128]{2,1,0:T(8,128)(2,1)S(1)}, u32[]{:S(2)}) copy-start(bf16[16,128,128]{2,1,0:T(8,128)(2,1)S(1)} %get-tuple-element.122.refs_0_) | copy-start | bytes 1572868
  38.6 21.9 %all-to-all-start.2 = ((bf16[32,80,128]{2,1,0:T(8,128)(2,1)}), bf16[32,80,128]{2,1,0:T(8,128)(2,1)S(1)}, u32[]{:S(2)}, u32[]{:S(2)}) async-start(bf16[32,80,128]{2,1,0:T(8,128)(2,1)} %get-tuple-element.85), calls=%async_computation.2 | async-start | bytes 1310720 | tf_op jit(solution)/shard_map/all_to_all | solution.py:80
  42.8 2.3 %collective-permute-start.7 = (bf16[4,16,2688]{2,1,0:T(8,128)(2,1)S(1)}, bf16[4,16,2688]{2,1,0:T(8,128)(2,1)}, u32[]{:S(2)}, u32[]{:S(2)}) collective-permute-start(bf16[4,16,2688]{2,1,0:T(8,128)(2,1)S(1)} %pad_maximum_fusion.refs_0_), channel_id=1, source_target_pairs={{0,1},{1,0},{2,3},{3,2},{4,5},{5,4},{6,7},{7,6},{8,9},{9,8},{10,11... | collective-permute-start | bytes 1032200 | tf_op jit(solution)/shard_map/ppermute | solution.py:98
  42.9 2.4 %collective-permute-start.8 = (bf16[4,16,2688]{2,1,0:T(8,128)(2,1)}, bf16[4,16,2688]{2,1,0:T(8,128)(2,1)}, u32[]{:S(2)}, u32[]{:S(2)}) collective-permute-start(bf16[4,16,2688]{2,1,0:T(8,128)(2,1)} %collective-permute-done.2.refs_1_), channel_id=1, source_target_pairs={{0,1},{1,0},{2,3},{3,2},{4,5},{5,4},{6,7},{7,6},{8,9},{9,8},{10,11... | collective-permute-start | bytes 1032200 | tf_op jit(solution)/shard_map/ppermute | solution.py:98
  43.4 2.7 %collective-permute-start.9 = (bf16[4,16,2688]{2,1,0:T(8,128)(2,1)S(1)}, bf16[4,16,2688]{2,1,0:T(8,128)(2,1)}, u32[]{:S(2)}, u32[]{:S(2)}) collective-permute-start(bf16[4,16,2688]{2,1,0:T(8,128)(2,1)S(1)} %pad_maximum_fusion.1.refs_2_), channel_id=1, source_target_pairs={{0,1},{1,0},{2,3},{3,2},{4,5},{5,4},{6,7},{7,6},{8,9},{9,8},{10,11... | collective-permute-start | bytes 1032200 | tf_op jit(solution)/shard_map/ppermute | solution.py:98
  43.4 2.9 %collective-permute-start.10 = (bf16[4,16,2688]{2,1,0:T(8,128)(2,1)}, bf16[4,16,2688]{2,1,0:T(8,128)(2,1)}, u32[]{:S(2)}, u32[]{:S(2)}) collective-permute-start(bf16[4,16,2688]{2,1,0:T(8,128)(2,1)} %collective-permute-done.6.refs_3_), channel_id=1, source_target_pairs={{0,1},{1,0},{2,3},{3,2},{4,5},{5,4},{6,7},{7,6},{8,9},{9,8},{10,11... | collective-permute-start | bytes 1032200 | tf_op jit(solution)/shard_map/ppermute | solution.py:98
  60.5 0.8 copy-start.13
  98.0 3.7 %copy-start.16 = (bf16[4,4,16,2560]{3,2,1,0:T(8,128)(2,1)S(1)}, bf16[4,4,16,2560]{3,2,1,0:T(8,128)(2,1)}, u32[]{:S(2)}) copy-start(bf16[4,4,16,2560]{3,2,1,0:T(8,128)(2,1)} %get-tuple-element.93) | copy-start | bytes 3932164
  98.0 3.8 %collective-permute-start.11 = (bf16[4,4,16,2560]{3,2,1,0:T(8,128)(2,1)}, bf16[4,4,16,2560]{3,2,1,0:T(8,128)(2,1)}, u32[]{:S(2)}, u32[]{:S(2)}) collective-permute-start(bf16[4,4,16,2560]{3,2,1,0:T(8,128)(2,1)} %get-tuple-element.94), channel_id=1, source_target_pairs={{0,1},{1,0},{2,3},{3,2},{4,5},{5,4},{6,7},{7,6},{8,9},{9,8},{10,11... | collective-permute-start | bytes 3932168 | tf_op jit(solution)/shard_map/ppermute | solution.py:98
  98.2 21.5 %all-to-all-start.3 = ((bf16[32,80,128]{2,1,0:T(8,128)(2,1)}), bf16[32,80,128]{2,1,0:T(8,128)(2,1)S(1)}, u32[]{:S(2)}, u32[]{:S(2)}) async-start(bf16[32,80,128]{2,1,0:T(8,128)(2,1)} %get-tuple-element.92), calls=%async_computation.3 | async-start | bytes 1310720 | tf_op jit(solution)/shard_map/all_to_all | solution.py:80
  103.1 15.0 %collective-permute-start.13 = (bf16[4,16,2560]{2,1,0:T(8,128)(2,1)S(1)}, bf16[4,16,2560]{2,1,0:T(8,128)(2,1)S(1)}, u32[]{:S(2)}, u32[]{:S(2)}) collective-permute-start(bf16[4,16,2560]{2,1,0:T(8,128)(2,1)S(1)} %get-tuple-element.129), channel_id=1, source_target_pairs={{0,4},{4,0},{8,12},{12,8},{16,20},{20,16},{24,28},{28,24},{1,5},{5... | collective-permute-start | bytes 983048 | tf_op jit(solution)/shard_map/ppermute | solution.py:98
  104.9 14.2 %collective-permute-start.12 = (bf16[4,16,2560]{2,1,0:T(8,128)(2,1)S(1)}, bf16[4,16,2560]{2,1,0:T(8,128)(2,1)S(1)}, u32[]{:S(2)}, u32[]{:S(2)}) collective-permute-start(bf16[4,16,2560]{2,1,0:T(8,128)(2,1)S(1)} %get-tuple-element.130), channel_id=1, source_target_pairs={{0,2},{1,3},{2,0},{3,1},{4,6},{5,7},{6,4},{7,5},{8,10},{9,11},{10,... | collective-permute-start | bytes 983048 | tf_op jit(solution)/shard_map/ppermute | solution.py:98
  107.5 15.0 %copy-start.11 = (f32[8,128]{1,0:T(8,128)S(1)}, f32[8,128]{1,0:T(8,128)}, u32[]{:S(2)}) copy-start(f32[8,128]{1,0:T(8,128)} %get-tuple-element.96.stat_ref) | copy-start | bytes 12292
  119.7 9.3 %collective-permute-start.14 = (bf16[2,16,2560]{2,1,0:T(8,128)(2,1)S(1)}, bf16[2,16,2560]{2,1,0:T(8,128)(2,1)S(1)}, u32[]{:S(2)}, u32[]{:S(2)}) collective-permute-start(bf16[2,16,2560]{2,1,0:T(8,128)(2,1)S(1)} %fusion.9), channel_id=1, source_target_pairs={{0,4},{4,0},{8,12},{12,8},{16,20},{20,16},{24,28},{28,24},{1,5},{5... | collective-permute-start | bytes 491528 | tf_op jit(solution)/shard_map/ppermute | solution.py:98
  121.1 7.9 %collective-permute-start.15 = (bf16[2,16,2560]{2,1,0:T(8,128)(2,1)S(1)}, bf16[2,16,2560]{2,1,0:T(8,128)(2,1)S(1)}, u32[]{:S(2)}, u32[]{:S(2)}) collective-permute-start(bf16[2,16,2560]{2,1,0:T(8,128)(2,1)S(1)} %fusion.10), channel_id=1, source_target_pairs={{0,2},{1,3},{2,0},{3,1},{4,6},{5,7},{6,4},{7,5},{8,10},{9,11},{10,... | collective-permute-start | bytes 491528 | tf_op jit(solution)/shard_map/ppermute | solution.py:98
  124.7 0.8 copy-start.12
  125.5 17.1 %all-to-all-start.4 = ((f32[32,8,128]{2,1,0:T(8,128)}), f32[32,8,128]{2,1,0:T(8,128)S(1)}, u32[]{:S(2)}, u32[]{:S(2)}) async-start(f32[32,8,128]{2,1,0:T(8,128)} %get-tuple-element.97), calls=%async_computation.4 | async-start | bytes 262144 | tf_op jit(solution)/shard_map/all_to_all | solution.py:80
  129.0 9.5 %collective-permute-start.16 = (bf16[16,2560]{1,0:T(8,128)(2,1)S(1)}, bf16[16,2560]{1,0:T(8,128)(2,1)S(1)}, u32[]{:S(2)}, u32[]{:S(2)}) collective-permute-start(bf16[16,2560]{1,0:T(8,128)(2,1)S(1)} %get-tuple-element.137), channel_id=1, source_target_pairs={{0,8},{4,12},{8,0},{12,4},{16,24},{20,28},{24,16},{28,20},{1,9},{5... | collective-permute-start | bytes 245768 | tf_op jit(solution)/shard_map/ppermute | solution.py:98
  131.0 8.9 %collective-permute-start.18 = (bf16[16,2560]{1,0:T(8,128)(2,1)S(1)}, bf16[16,2560]{1,0:T(8,128)(2,1)S(1)}, u32[]{:S(2)}, u32[]{:S(2)}) collective-permute-start(bf16[16,2560]{1,0:T(8,128)(2,1)S(1)} %get-tuple-element.135), channel_id=1, source_target_pairs={{0,24},{4,28},{8,16},{12,20},{16,8},{20,12},{24,0},{28,4},{1,25},{... | collective-permute-start | bytes 245768 | tf_op jit(solution)/shard_map/ppermute | solution.py:98
  133.4 9.1 %collective-permute-start.17 = (bf16[16,2560]{1,0:T(8,128)(2,1)S(1)}, bf16[16,2560]{1,0:T(8,128)(2,1)S(1)}, u32[]{:S(2)}, u32[]{:S(2)}) collective-permute-start(bf16[16,2560]{1,0:T(8,128)(2,1)S(1)} %get-tuple-element.136), channel_id=1, source_target_pairs={{0,16},{4,20},{8,24},{12,28},{16,0},{20,4},{24,8},{28,12},{1,17},{... | collective-permute-start | bytes 245768 | tf_op jit(solution)/shard_map/ppermute | solution.py:98
  133.5 9.0 %copy-start.4 = (f32[16,5134]{1,0:T(8,128)S(1)}, f32[16,5134]{1,0:T(8,128)}, u32[]{:S(2)}) copy-start(f32[16,5134]{1,0:T(8,128)} %m_ref.1) | copy-start | bytes 985732
  133.5 9.0 %copy-start.5 = (f32[16,5134]{1,0:T(8,128)S(1)}, f32[16,5134]{1,0:T(8,128)}, u32[]{:S(2)}) copy-start(f32[16,5134]{1,0:T(8,128)} %v_ref.1) | copy-start | bytes 985732
  133.5 9.0 %copy-start.6 = (f32[16,5134]{1,0:T(8,128)S(1)}, f32[16,5134]{1,0:T(8,128)}, u32[]{:S(2)}) copy-start(f32[16,5134]{1,0:T(8,128)} %ema_ref.1) | copy-start | bytes 985732

commit v5 on v4

--- a/solution.py
+++ b/solution.py
@@ -184,7 +184,7 @@
         other = lax.ppermute(held, "mode", partners(step))
         first = bit_of(step) == 0
         pair = [jnp.where(first, held, other), jnp.where(first, other, held)]
-        held = jnp.concatenate(pair, axis=1) if step > 1 else jnp.stack(pair, axis=2)
+        held = jnp.stack(pair, axis=2).reshape(n_data, -1, *x.shape)
     return held.reshape(-1, x.shape[1])
 
 

time: 145 us -> 145 us (level)
  no operation moved by 1% of the time
where the time goes in v5:
time: 145 us; the launch traced here: 144 us
  Pallas kernels  52.2 us (36%)
  starting transfers between devices  44.7 us (31%)
  waiting for transfers between devices  34.6 us (24%)
  local copies, waits for them, and re-layouts  8.29 us (6%)
  other arithmetic  3.5 us (2%)
    pallas_call x1, Pallas kernels, block(): pl.pallas_call(partial(block_kernel, sizes), out_shape=(jax.ShapeDtypeStr...  36.7 us
    ppermute x19, starting transfers between devices, by_xor(): lax.ppermute(x, axis, [(index, index ^ step) for index in range(count)])  24.6 us
    all_to_all x5, starting transfers between devices, exchange(): return lax.all_to_all(x, axes, 0, 0, tiled=True)  20.1 us
    all_to_all x5, waiting for transfers between devices, exchange(): return lax.all_to_all(x, axes, 0, 0, tiled=True)  17.3 us
    ppermute x19, waiting for transfers between devices, by_xor(): lax.ppermute(x, axis, [(index, index ^ step) for index in range(count)])  17.3 us
    pallas_call x7, Pallas kernels, call(): pl.pallas_call(kernel, out_shape=outs, in_specs=in_specs, out_specs=jax.t...  15.5 us
    unnamed x40, local copies, waits for them, and re-layouts  5.99 us
  transfers between devices with their start and end apart: 24, of which 12 were waited for; matrix products, arithmetic and copies ran while one was open for 4% of the time, Pallas kernels for 8%

profile of v5, /device:TPU:0, one launch (start us, length us, event | category | flops | bytes accessed | tf_op | source)
XLA Modules:
  0.0 144.3 jit_solution(9420869315209190493)
XLA Ops:
  0.7 2.0 %pack.1 = (f32[4,64,192]{2,1,0:T(8,128)}, bf16[16,2688]{1,0:T(8,128)(2,1)}) custom-call(bf16[7,16,192]{2,1,0:T(8,128)(2,1)} %bitcast.102, f32[7,16,192]{2,1,0:T(8,128)} %bitcast.101, s32[16,192]{1,0:T(8,128)} %bitcast.103, f32[16,5134]{1,0:T(8,128)} %w_ref.1), custom_call_target="tpu_custom_call" | custom-call | tf_op jit(solution)/shard_map/pack/pallas_call | solution.py:616
  2.7 5.1 %collective-permute-start.4 = (bf16[16,2688]{1,0:T(8,128)(2,1)}, bf16[16,2688]{1,0:T(8,128)(2,1)S(1)}, u32[]{:S(2)}, u32[]{:S(2)}) collective-permute-start(bf16[16,2688]{1,0:T(8,128)(2,1)} %get-tuple-element.80), channel_id=1, source_target_pairs={{0,24},{4,28},{8,16},{12,20},{16,8},{20,12},{24,0},{28,4},{1,25},{... | collective-permute-start | bytes 258056 | tf_op jit(solution)/shard_map/ppermute | solution.py:98
  7.8 0.6 collective-permute-start
  8.5 3.4 %all-to-all-start = ((f32[4,64,192]{2,1,0:T(8,128)}), f32[4,64,192]{2,1,0:T(8,128)S(1)}, u32[]{:S(2)}, u32[]{:S(2)}) async-start(f32[4,64,192]{2,1,0:T(8,128)} %get-tuple-element.70), calls=%async_computation | async-start | bytes 524288 | tf_op jit(solution)/shard_map/all_to_all | solution.py:80
  12.6 0.9 fusion.6
  13.8 1.7 %collective-permute-start.1 = (bf16[2,16,2688]{2,1,0:T(8,128)(2,1)S(1)}, bf16[2,16,2688]{2,1,0:T(8,128)(2,1)S(1)}, u32[]{:S(2)}, u32[]{:S(2)}) collective-permute-start(bf16[2,16,2688]{2,1,0:T(8,128)(2,1)S(1)} %pad_maximum_fusion.2), channel_id=1, source_target_pairs={{0,4},{4,0},{8,12},{12,8},{16,20},{20,16},{24,28},{28,24},{1,5},{5... | collective-permute-start | bytes 516104 | tf_op jit(solution)/shard_map/ppermute | solution.py:98
  15.5 2.0 %collective-permute-start.5 = (bf16[2,16,2688]{2,1,0:T(8,128)(2,1)S(1)}, bf16[2,16,2688]{2,1,0:T(8,128)(2,1)S(1)}, u32[]{:S(2)}, u32[]{:S(2)}) collective-permute-start(bf16[2,16,2688]{2,1,0:T(8,128)(2,1)S(1)} %pad_maximum_fusion.3), channel_id=1, source_target_pairs={{0,2},{1,3},{2,0},{3,1},{4,6},{5,7},{6,4},{7,5},{8,10},{9,11},{10,... | collective-permute-start | bytes 516104 | tf_op jit(solution)/shard_map/ppermute | solution.py:98
  17.9 1.4 spectra.1
  19.3 5.5 %all-to-all-start.1 = ((f32[32,16,128]{2,1,0:T(8,128)}), f32[32,16,128]{2,1,0:T(8,128)S(1)}, u32[]{:S(2)}, u32[]{:S(2)}) async-start(f32[32,16,128]{2,1,0:T(8,128)} %spectra.1), calls=%async_computation.1 | async-start | bytes 524288 | tf_op jit(solution)/shard_map/all_to_all | solution.py:80
  24.9 1.8 %collective-permute-start.2 = (bf16[4,16,2688]{2,1,0:T(8,128)(2,1)S(1)}, bf16[4,16,2688]{2,1,0:T(8,128)(2,1)}, u32[]{:S(2)}, u32[]{:S(2)}) collective-permute-start(bf16[4,16,2688]{2,1,0:T(8,128)(2,1)S(1)} %pad_maximum_fusion.refs_0_), channel_id=1, source_target_pairs={{0,2},{1,3},{2,0},{3,1},{4,6},{5,7},{6,4},{7,5},{8,10},{9,11},{10,... | collective-permute-start | bytes 1032200 | tf_op jit(solution)/shard_map/ppermute | solution.py:98
  26.8 1.5 %collective-permute-start.6 = (bf16[4,16,2688]{2,1,0:T(8,128)(2,1)S(1)}, bf16[4,16,2688]{2,1,0:T(8,128)(2,1)}, u32[]{:S(2)}, u32[]{:S(2)}) collective-permute-start(bf16[4,16,2688]{2,1,0:T(8,128)(2,1)S(1)} %pad_maximum_fusion.1.refs_2_), channel_id=1, source_target_pairs={{0,4},{4,0},{8,12},{12,8},{16,20},{20,16},{24,28},{28,24},{1,5},{5... | collective-permute-start | bytes 1032200 | tf_op jit(solution)/shard_map/ppermute | solution.py:98
  28.3 0.5 tables.1
  28.8 0.7 copy-done.1
  29.6 0.7 copy-done.2
  30.3 0.7 copy-done.3
  31.1 0.7 copy-done.7
  31.8 0.7 copy-done.8
  32.5 0.7 copy-done.9
  33.1 2.4 %all-to-all-done.1.got_ref.first_ref = f32[32,16,128]{2,1,0:T(8,128)S(1)} async-done(((f32[32,16,128]{2,1,0:T(8,128)}), f32[32,16,128]{2,1,0:T(8,128)S(1)}, u32[]{:S(2)}, u32[]{:S(2)}) %all-to-all-start.1) | async-done | bytes 262176 | tf_op jit(solution)/shard_map/all_to_all | solution.py:80
  35.5 2.6 %mix.1 = (bf16[32,80,128]{2,1,0:T(8,128)(2,1)}, bf16[16,128,128]{2,1,0:T(8,128)(2,1)S(1)}, f32[16,128]{1,0:T(8,128)S(1)}) custom-call(f32[32,16,128]{2,1,0:T(8,128)S(1)} %all-to-all-done.1.got_ref.first_ref, bf16[16,128,128]{2,1,0:T(8,128)(2,1)S(1)} %maximum_maximum_fusion.mixer_ref), custom_call_target="tpu_custom_call" | custom-call | tf_op jit(solution)/shard_map/mix/pallas_call | solution.py:616
  38.1 0.6 collective-permute-done.6.refs_3_
  38.6 4.1 %all-to-all-start.2 = ((bf16[32,80,128]{2,1,0:T(8,128)(2,1)}), bf16[32,80,128]{2,1,0:T(8,128)(2,1)S(1)}, u32[]{:S(2)}, u32[]{:S(2)}) async-start(bf16[32,80,128]{2,1,0:T(8,128)(2,1)} %get-tuple-element.85), calls=%async_computation.2 | async-start | bytes 1310720 | tf_op jit(solution)/shard_map/all_to_all | solution.py:80
  42.9 0.4 collective-permute-start.8
  43.4 0.4 collective-permute-start.10
  43.9 0.6 pad_add_fusion.me_ref
  44.5 0.6 slice.123
  45.3 0.8 collective-permute-done.9.refs_6_
  46.3 14.2 %all-to-all-done.2.refs_8_ = bf16[32,80,128]{2,1,0:T(8,128)(2,1)S(1)} async-done(((bf16[32,80,128]{2,1,0:T(8,128)(2,1)}), bf16[32,80,128]{2,1,0:T(8,128)(2,1)S(1)}, u32[]{:S(2)}, u32[]{:S(2)}) %all-to-all-start.2) | async-done | bytes 655392 | tf_op jit(solution)/shard_map/all_to_all | solution.py:80
  60.5 0.8 copy-done.13
  61.3 36.7 %block.1 = (bf16[32,80,128]{2,1,0:T(8,128)(2,1)}, f32[8,128]{1,0:T(8,128)}, bf16[4,4,16,2560]{3,2,1,0:T(8,128)(2,1)}, bf16[4,4,16,2560]{3,2,1,0:T(8,128)(2,1)}) custom-call(f32[1]{0:T(128)} %bitcast.3.count_ref, s32[2]{0:T(128)} %pad_add_fusion.me_ref, bf16[4,16,2688]{2,1,0:T(8,128)(2,1)} %copy-done.14, bf16[4,16,2688]{2,1,0:T(8,128)(2,1)} %collective-permute-done.2.refs_1_, ...), custom_call_target="tpu_custom_call" | custom-call | tf_op jit(solution)/shard_map/block/pallas_call | solution.py:545
  98.2 3.6 %all-to-all-start.3 = ((bf16[32,80,128]{2,1,0:T(8,128)(2,1)}), bf16[32,80,128]{2,1,0:T(8,128)(2,1)S(1)}, u32[]{:S(2)}, u32[]{:S(2)}) async-start(bf16[32,80,128]{2,1,0:T(8,128)(2,1)} %get-tuple-element.92), calls=%async_computation.3 | async-start | bytes 1310720 | tf_op jit(solution)/shard_map/all_to_all | solution.py:80
  101.8 1.3 fusion.1
  103.1 1.8 %collective-permute-start.13 = (bf16[4,16,2560]{2,1,0:T(8,128)(2,1)S(1)}, bf16[4,16,2560]{2,1,0:T(8,128)(2,1)S(1)}, u32[]{:S(2)}, u32[]{:S(2)}) collective-permute-start(bf16[4,16,2560]{2,1,0:T(8,128)(2,1)S(1)} %get-tuple-element.129), channel_id=1, source_target_pairs={{0,4},{4,0},{8,12},{12,8},{16,20},{20,16},{24,28},{28,24},{1,5},{5... | collective-permute-start | bytes 983048 | tf_op jit(solution)/shard_map/ppermute | solution.py:98
  104.9 1.5 %collective-permute-start.12 = (bf16[4,16,2560]{2,1,0:T(8,128)(2,1)S(1)}, bf16[4,16,2560]{2,1,0:T(8,128)(2,1)S(1)}, u32[]{:S(2)}, u32[]{:S(2)}) collective-permute-start(bf16[4,16,2560]{2,1,0:T(8,128)(2,1)S(1)} %get-tuple-element.130), channel_id=1, source_target_pairs={{0,2},{1,3},{2,0},{3,1},{4,6},{5,7},{6,4},{7,5},{8,10},{9,11},{10,... | collective-permute-start | bytes 983048 | tf_op jit(solution)/shard_map/ppermute | solution.py:98
  106.4 1.1 fusion.15
  107.6 10.6 %collective-permute-done.13 = bf16[4,16,2560]{2,1,0:T(8,128)(2,1)S(1)} collective-permute-done((bf16[4,16,2560]{2,1,0:T(8,128)(2,1)S(1)}, bf16[4,16,2560]{2,1,0:T(8,128)(2,1)S(1)}, u32[]{:S(2)}, u32[]{:S(2)}) %collective-permute-start.13) | collective-permute-done | bytes 327712 | tf_op jit(solution)/shard_map/ppermute | solution.py:98
  118.2 1.0 collective-permute-done.12
  119.7 1.4 collective-permute-start.14
  121.1 1.4 collective-permute-start.15
  122.5 2.1 %mix_back.1 = (f32[32,8,128]{2,1,0:T(8,128)}, bf16[16,128,128]{2,1,0:T(8,128)(2,1)S(1)}, f32[8,128]{1,0:T(8,128)S(1)}) custom-call(bf16[32,80,128]{2,1,0:T(8,128)(2,1)S(1)} %all-to-all-done.3.got_ref, bf16[16,128,128]{2,1,0:T(8,128)(2,1)S(1)} %maximum_maximum_fusion.mixer_ref, f32[32,16,128]{2,1,0:T(8,128)S(1)} %all-to-all-done.1.got_ref.first_ref, ...), custom_call_target="tpu_custom_call" | custom-call | flops 10000000000 | bytes 1000000000 | tf_op jit(solution)/shard_map/mix_back/pallas_call | solution.py:616
  124.7 0.8 copy-done.12
  125.5 3.5 %all-to-all-start.4 = ((f32[32,8,128]{2,1,0:T(8,128)}), f32[32,8,128]{2,1,0:T(8,128)S(1)}, u32[]{:S(2)}, u32[]{:S(2)}) async-start(f32[32,8,128]{2,1,0:T(8,128)} %get-tuple-element.97), calls=%async_computation.4 | async-start | bytes 262144 | tf_op jit(solution)/shard_map/all_to_all | solution.py:80
  129.0 1.8 %collective-permute-start.16 = (bf16[16,2560]{1,0:T(8,128)(2,1)S(1)}, bf16[16,2560]{1,0:T(8,128)(2,1)S(1)}, u32[]{:S(2)}, u32[]{:S(2)}) collective-permute-start(bf16[16,2560]{1,0:T(8,128)(2,1)S(1)} %get-tuple-element.137), channel_id=1, source_target_pairs={{0,8},{4,12},{8,0},{12,4},{16,24},{20,28},{24,16},{28,20},{1,9},{5... | collective-permute-start | bytes 245768 | tf_op jit(solution)/shard_map/ppermute | solution.py:98
  131.0 2.4 %collective-permute-start.18 = (bf16[16,2560]{1,0:T(8,128)(2,1)S(1)}, bf16[16,2560]{1,0:T(8,128)(2,1)S(1)}, u32[]{:S(2)}, u32[]{:S(2)}) collective-permute-start(bf16[16,2560]{1,0:T(8,128)(2,1)S(1)} %get-tuple-element.135), channel_id=1, source_target_pairs={{0,24},{4,28},{8,16},{12,20},{16,8},{20,12},{24,0},{28,4},{1,25},{... | collective-permute-start | bytes 245768 | tf_op jit(solution)/shard_map/ppermute | solution.py:98
  133.5 5.0 %spectral.1 = (f32[2,16,4096]{2,1,0:T(8,128)}, f32[2,16,4096]{2,1,0:T(8,128)}, f32[2,16,4096]{2,1,0:T(8,128)}, f32[2,16,4096]{2,1,0:T(8,128)}, bf16[2,16,4096]{2,1,0:T(8,128)(2,1)}) custom-call(bf16[16,128,128]{2,1,0:T(8,128)(2,1)} %copy-done.10, bf16[16,128,128]{2,1,0:T(8,128)(2,1)} %copy-done.12, f32[2,16,4096]{2,1,0:T(8,128)} %refs_2_.1, ...), custom_call_target="tpu_custom_call" | custom-call | flops 10000000000 | bytes 1000000000 | tf_op jit(solution)/shard_map/spectral/pallas_call | solution.py:616
  138.6 1.3 collective-permute-done.18.refs_3_
  139.8 2.7 %collective-permute-done.17.refs_2_ = bf16[16,2560]{1,0:T(8,128)(2,1)S(1)} collective-permute-done((bf16[16,2560]{1,0:T(8,128)(2,1)S(1)}, bf16[16,2560]{1,0:T(8,128)(2,1)S(1)}, u32[]{:S(2)}, u32[]{:S(2)}) %collective-permute-start.17) | collective-permute-done | bytes 81952 | tf_op jit(solution)/shard_map/ppermute | solution.py:98
  142.5 1.8 %rows.1 = (f32[1,1]{1,0:T(1,128)}, f32[16,5134]{1,0:T(8,128)}, f32[16,5134]{1,0:T(8,128)}, f32[16,5134]{1,0:T(8,128)}, f32[16,5134]{1,0:T(8,128)}, /*index=5*/bf16[16,5134]{1,0:T(8,128)(2,1)}) custom-call(f32[32,8,128]{2,1,0:T(8,128)S(1)} %all-to-all-done.4.got_ref, f32[8,128]{1,0:T(8,128)S(1)} %get-tuple-element.98.thin_ref, ...), custom_call_target="tpu_custom_call" | custom-call | tf_op jit(solution)/shard_map/rows/pallas_call | solution.py:616
  (72 shorter events, 3.3 us)
Async XLA Ops:
  0.6 11.2 %copy-start.17 = (f32[2,16,4096]{2,1,0:T(8,128)S(1)}, f32[2,16,4096]{2,1,0:T(8,128)}, u32[]{:S(2)}) copy-start(f32[2,16,4096]{2,1,0:T(8,128)} %refs_2_.1) | copy-start | bytes 1572868
  2.7 12.8 %collective-permute-start.4 = (bf16[16,2688]{1,0:T(8,128)(2,1)}, bf16[16,2688]{1,0:T(8,128)(2,1)S(1)}, u32[]{:S(2)}, u32[]{:S(2)}) collective-permute-start(bf16[16,2688]{1,0:T(8,128)(2,1)} %get-tuple-element.80), channel_id=1, source_target_pairs={{0,24},{4,28},{8,16},{12,20},{16,8},{20,12},{24,0},{28,4},{1,25},{... | collective-permute-start | bytes 258056 | tf_op jit(solution)/shard_map/ppermute | solution.py:98
  7.8 7.7 %collective-permute-start.3 = (bf16[16,2688]{1,0:T(8,128)(2,1)}, bf16[16,2688]{1,0:T(8,128)(2,1)S(1)}, u32[]{:S(2)}, u32[]{:S(2)}) collective-permute-start(bf16[16,2688]{1,0:T(8,128)(2,1)} %get-tuple-element.80), channel_id=1, source_target_pairs={{0,16},{4,20},{8,24},{12,28},{16,0},{20,4},{24,8},{28,12},{1,17},{... | collective-permute-start | bytes 258056 | tf_op jit(solution)/shard_map/ppermute | solution.py:98
  7.8 5.9 %collective-permute-start = (bf16[16,2688]{1,0:T(8,128)(2,1)}, bf16[16,2688]{1,0:T(8,128)(2,1)S(1)}, u32[]{:S(2)}, u32[]{:S(2)}) collective-permute-start(bf16[16,2688]{1,0:T(8,128)(2,1)} %get-tuple-element.80), channel_id=1, source_target_pairs={{0,8},{4,12},{8,0},{12,4},{16,24},{20,28},{24,16},{28,20},{1,9},{5... | collective-permute-start | bytes 258056 | tf_op jit(solution)/shard_map/ppermute | solution.py:98
  8.5 9.4 %all-to-all-start = ((f32[4,64,192]{2,1,0:T(8,128)}), f32[4,64,192]{2,1,0:T(8,128)S(1)}, u32[]{:S(2)}, u32[]{:S(2)}) async-start(f32[4,64,192]{2,1,0:T(8,128)} %get-tuple-element.70), calls=%async_computation | async-start | bytes 524288 | tf_op jit(solution)/shard_map/all_to_all | solution.py:80
  11.9 0.7 copy-start.19
  12.2 1.5 %copy-start.18 = (bf16[16,2688]{1,0:T(8,128)(2,1)S(1)}, bf16[16,2688]{1,0:T(8,128)(2,1)}, u32[]{:S(2)}) copy-start(bf16[16,2688]{1,0:T(8,128)(2,1)} %get-tuple-element.80) | copy-start | bytes 258052
  12.3 5.6 %copy-start = (f32[16,5134]{1,0:T(8,128)S(1)}, f32[16,5134]{1,0:T(8,128)}, u32[]{:S(2)}) copy-start(f32[16,5134]{1,0:T(8,128)} %w_ref.1) | copy-start | bytes 985732
  13.8 11.0 %collective-permute-start.1 = (bf16[2,16,2688]{2,1,0:T(8,128)(2,1)S(1)}, bf16[2,16,2688]{2,1,0:T(8,128)(2,1)S(1)}, u32[]{:S(2)}, u32[]{:S(2)}) collective-permute-start(bf16[2,16,2688]{2,1,0:T(8,128)(2,1)S(1)} %pad_maximum_fusion.2), channel_id=1, source_target_pairs={{0,4},{4,0},{8,12},{12,8},{16,20},{20,16},{24,28},{28,24},{1,5},{5... | collective-permute-start | bytes 516104 | tf_op jit(solution)/shard_map/ppermute | solution.py:98
  15.5 11.2 %collective-permute-start.5 = (bf16[2,16,2688]{2,1,0:T(8,128)(2,1)S(1)}, bf16[2,16,2688]{2,1,0:T(8,128)(2,1)S(1)}, u32[]{:S(2)}, u32[]{:S(2)}) collective-permute-start(bf16[2,16,2688]{2,1,0:T(8,128)(2,1)S(1)} %pad_maximum_fusion.3), channel_id=1, source_target_pairs={{0,2},{1,3},{2,0},{3,1},{4,6},{5,7},{6,4},{7,5},{8,10},{9,11},{10,... | collective-permute-start | bytes 516104 | tf_op jit(solution)/shard_map/ppermute | solution.py:98
  19.3 16.2 %all-to-all-start.1 = ((f32[32,16,128]{2,1,0:T(8,128)}), f32[32,16,128]{2,1,0:T(8,128)S(1)}, u32[]{:S(2)}, u32[]{:S(2)}) async-start(f32[32,16,128]{2,1,0:T(8,128)} %spectra.1), calls=%async_computation.1 | async-start | bytes 524288 | tf_op jit(solution)/shard_map/all_to_all | solution.py:80
  24.9 17.9 %copy-start.14 = (bf16[4,16,2688]{2,1,0:T(8,128)(2,1)}, bf16[4,16,2688]{2,1,0:T(8,128)(2,1)S(1)}, u32[]{:S(2)}) copy-start(bf16[4,16,2688]{2,1,0:T(8,128)(2,1)S(1)} %pad_maximum_fusion.refs_0_) | copy-start | bytes 1032196
  24.9 13.2 %collective-permute-start.2 = (bf16[4,16,2688]{2,1,0:T(8,128)(2,1)S(1)}, bf16[4,16,2688]{2,1,0:T(8,128)(2,1)}, u32[]{:S(2)}, u32[]{:S(2)}) collective-permute-start(bf16[4,16,2688]{2,1,0:T(8,128)(2,1)S(1)} %pad_maximum_fusion.refs_0_), channel_id=1, source_target_pairs={{0,2},{1,3},{2,0},{3,1},{4,6},{5,7},{6,4},{7,5},{8,10},{9,11},{10,... | collective-permute-start | bytes 1032200 | tf_op jit(solution)/shard_map/ppermute | solution.py:98
  26.8 16.6 %copy-start.15 = (bf16[4,16,2688]{2,1,0:T(8,128)(2,1)}, bf16[4,16,2688]{2,1,0:T(8,128)(2,1)S(1)}, u32[]{:S(2)}) copy-start(bf16[4,16,2688]{2,1,0:T(8,128)(2,1)S(1)} %pad_maximum_fusion.1.refs_2_) | copy-start | bytes 1032196
  26.8 11.8 %collective-permute-start.6 = (bf16[4,16,2688]{2,1,0:T(8,128)(2,1)S(1)}, bf16[4,16,2688]{2,1,0:T(8,128)(2,1)}, u32[]{:S(2)}, u32[]{:S(2)}) collective-permute-start(bf16[4,16,2688]{2,1,0:T(8,128)(2,1)S(1)} %pad_maximum_fusion.1.refs_2_), channel_id=1, source_target_pairs={{0,4},{4,0},{8,12},{12,8},{16,20},{20,16},{24,28},{28,24},{1,5},{5... | collective-permute-start | bytes 1032200 | tf_op jit(solution)/shard_map/ppermute | solution.py:98
  28.8 0.7 copy-start.1
  29.6 0.7 copy-start.2
  30.3 0.7 copy-start.3
  31.1 0.7 copy-start.7
  31.8 0.7 copy-start.8
  32.5 0.7 copy-start.9
  38.1 60.0 %copy-start.10 = (bf16[16,128,128]{2,1,0:T(8,128)(2,1)}, bf16[16,128,128]{2,1,0:T(8,128)(2,1)S(1)}, u32[]{:S(2)}) copy-start(bf16[16,128,128]{2,1,0:T(8,128)(2,1)S(1)} %get-tuple-element.122.refs_0_) | copy-start | bytes 1572868
  38.6 21.9 %all-to-all-start.2 = ((bf16[32,80,128]{2,1,0:T(8,128)(2,1)}), bf16[32,80,128]{2,1,0:T(8,128)(2,1)S(1)}, u32[]{:S(2)}, u32[]{:S(2)}) async-start(bf16[32,80,128]{2,1,0:T(8,128)(2,1)} %get-tuple-element.85), calls=%async_computation.2 | async-start | bytes 1310720 | tf_op jit(solution)/shard_map/all_to_all | solution.py:80
  42.8 2.3 %collective-permute-start.7 = (bf16[4,16,2688]{2,1,0:T(8,128)(2,1)S(1)}, bf16[4,16,2688]{2,1,0:T(8,128)(2,1)}, u32[]{:S(2)}, u32[]{:S(2)}) collective-permute-start(bf16[4,16,2688]{2,1,0:T(8,128)(2,1)S(1)} %pad_maximum_fusion.refs_0_), channel_id=1, source_target_pairs={{0,1},{1,0},{2,3},{3,2},{4,5},{5,4},{6,7},{7,6},{8,9},{9,8},{10,11... | collective-permute-start | bytes 1032200 | tf_op jit(solution)/shard_map/ppermute | solution.py:98
  42.9 2.4 %collective-permute-start.8 = (bf16[4,16,2688]{2,1,0:T(8,128)(2,1)}, bf16[4,16,2688]{2,1,0:T(8,128)(2,1)}, u32[]{:S(2)}, u32[]{:S(2)}) collective-permute-start(bf16[4,16,2688]{2,1,0:T(8,128)(2,1)} %collective-permute-done.2.refs_1_), channel_id=1, source_target_pairs={{0,1},{1,0},{2,3},{3,2},{4,5},{5,4},{6,7},{7,6},{8,9},{9,8},{10,11... | collective-permute-start | bytes 1032200 | tf_op jit(solution)/shard_map/ppermute | solution.py:98
  43.4 2.7 %collective-permute-start.9 = (bf16[4,16,2688]{2,1,0:T(8,128)(2,1)S(1)}, bf16[4,16,2688]{2,1,0:T(8,128)(2,1)}, u32[]{:S(2)}, u32[]{:S(2)}) collective-permute-start(bf16[4,16,2688]{2,1,0:T(8,128)(2,1)S(1)} %pad_maximum_fusion.1.refs_2_), channel_id=1, source_target_pairs={{0,1},{1,0},{2,3},{3,2},{4,5},{5,4},{6,7},{7,6},{8,9},{9,8},{10,11... | collective-permute-start | bytes 1032200 | tf_op jit(solution)/shard_map/ppermute | solution.py:98
  43.4 2.9 %collective-permute-start.10 = (bf16[4,16,2688]{2,1,0:T(8,128)(2,1)}, bf16[4,16,2688]{2,1,0:T(8,128)(2,1)}, u32[]{:S(2)}, u32[]{:S(2)}) collective-permute-start(bf16[4,16,2688]{2,1,0:T(8,128)(2,1)} %collective-permute-done.6.refs_3_), channel_id=1, source_target_pairs={{0,1},{1,0},{2,3},{3,2},{4,5},{5,4},{6,7},{7,6},{8,9},{9,8},{10,11... | collective-permute-start | bytes 1032200 | tf_op jit(solution)/shard_map/ppermute | solution.py:98
  60.5 0.8 copy-start.13
  98.0 3.7 %copy-start.16 = (bf16[4,4,16,2560]{3,2,1,0:T(8,128)(2,1)S(1)}, bf16[4,4,16,2560]{3,2,1,0:T(8,128)(2,1)}, u32[]{:S(2)}) copy-start(bf16[4,4,16,2560]{3,2,1,0:T(8,128)(2,1)} %get-tuple-element.93) | copy-start | bytes 3932164
  98.0 3.8 %collective-permute-start.11 = (bf16[4,4,16,2560]{3,2,1,0:T(8,128)(2,1)}, bf16[4,4,16,2560]{3,2,1,0:T(8,128)(2,1)}, u32[]{:S(2)}, u32[]{:S(2)}) collective-permute-start(bf16[4,4,16,2560]{3,2,1,0:T(8,128)(2,1)} %get-tuple-element.94), channel_id=1, source_target_pairs={{0,1},{1,0},{2,3},{3,2},{4,5},{5,4},{6,7},{7,6},{8,9},{9,8},{10,11... | collective-permute-start | bytes 3932168 | tf_op jit(solution)/shard_map/ppermute | solution.py:98
  98.2 21.5 %all-to-all-start.3 = ((bf16[32,80,128]{2,1,0:T(8,128)(2,1)}), bf16[32,80,128]{2,1,0:T(8,128)(2,1)S(1)}, u32[]{:S(2)}, u32[]{:S(2)}) async-start(bf16[32,80,128]{2,1,0:T(8,128)(2,1)} %get-tuple-element.92), calls=%async_computation.3 | async-start | bytes 1310720 | tf_op jit(solution)/shard_map/all_to_all | solution.py:80
  103.1 15.0 %collective-permute-start.13 = (bf16[4,16,2560]{2,1,0:T(8,128)(2,1)S(1)}, bf16[4,16,2560]{2,1,0:T(8,128)(2,1)S(1)}, u32[]{:S(2)}, u32[]{:S(2)}) collective-permute-start(bf16[4,16,2560]{2,1,0:T(8,128)(2,1)S(1)} %get-tuple-element.129), channel_id=1, source_target_pairs={{0,4},{4,0},{8,12},{12,8},{16,20},{20,16},{24,28},{28,24},{1,5},{5... | collective-permute-start | bytes 983048 | tf_op jit(solution)/shard_map/ppermute | solution.py:98
  104.9 14.2 %collective-permute-start.12 = (bf16[4,16,2560]{2,1,0:T(8,128)(2,1)S(1)}, bf16[4,16,2560]{2,1,0:T(8,128)(2,1)S(1)}, u32[]{:S(2)}, u32[]{:S(2)}) collective-permute-start(bf16[4,16,2560]{2,1,0:T(8,128)(2,1)S(1)} %get-tuple-element.130), channel_id=1, source_target_pairs={{0,2},{1,3},{2,0},{3,1},{4,6},{5,7},{6,4},{7,5},{8,10},{9,11},{10,... | collective-permute-start | bytes 983048 | tf_op jit(solution)/shard_map/ppermute | solution.py:98
  107.5 15.0 %copy-start.11 = (f32[8,128]{1,0:T(8,128)S(1)}, f32[8,128]{1,0:T(8,128)}, u32[]{:S(2)}) copy-start(f32[8,128]{1,0:T(8,128)} %get-tuple-element.96.stat_ref) | copy-start | bytes 12292
  119.7 9.3 %collective-permute-start.14 = (bf16[2,16,2560]{2,1,0:T(8,128)(2,1)S(1)}, bf16[2,16,2560]{2,1,0:T(8,128)(2,1)S(1)}, u32[]{:S(2)}, u32[]{:S(2)}) collective-permute-start(bf16[2,16,2560]{2,1,0:T(8,128)(2,1)S(1)} %fusion.9), channel_id=1, source_target_pairs={{0,4},{4,0},{8,12},{12,8},{16,20},{20,16},{24,28},{28,24},{1,5},{5... | collective-permute-start | bytes 491528 | tf_op jit(solution)/shard_map/ppermute | solution.py:98
  121.1 7.9 %collective-permute-start.15 = (bf16[2,16,2560]{2,1,0:T(8,128)(2,1)S(1)}, bf16[2,16,2560]{2,1,0:T(8,128)(2,1)S(1)}, u32[]{:S(2)}, u32[]{:S(2)}) collective-permute-start(bf16[2,16,2560]{2,1,0:T(8,128)(2,1)S(1)} %fusion.10), channel_id=1, source_target_pairs={{0,2},{1,3},{2,0},{3,1},{4,6},{5,7},{6,4},{7,5},{8,10},{9,11},{10,... | collective-permute-start | bytes 491528 | tf_op jit(solution)/shard_map/ppermute | solution.py:98
  124.7 0.8 copy-start.12
  125.5 17.1 %all-to-all-start.4 = ((f32[32,8,128]{2,1,0:T(8,128)}), f32[32,8,128]{2,1,0:T(8,128)S(1)}, u32[]{:S(2)}, u32[]{:S(2)}) async-start(f32[32,8,128]{2,1,0:T(8,128)} %get-tuple-element.97), calls=%async_computation.4 | async-start | bytes 262144 | tf_op jit(solution)/shard_map/all_to_all | solution.py:80
  129.0 9.5 %collective-permute-start.16 = (bf16[16,2560]{1,0:T(8,128)(2,1)S(1)}, bf16[16,2560]{1,0:T(8,128)(2,1)S(1)}, u32[]{:S(2)}, u32[]{:S(2)}) collective-permute-start(bf16[16,2560]{1,0:T(8,128)(2,1)S(1)} %get-tuple-element.137), channel_id=1, source_target_pairs={{0,8},{4,12},{8,0},{12,4},{16,24},{20,28},{24,16},{28,20},{1,9},{5... | collective-permute-start | bytes 245768 | tf_op jit(solution)/shard_map/ppermute | solution.py:98
  131.0 8.9 %collective-permute-start.18 = (bf16[16,2560]{1,0:T(8,128)(2,1)S(1)}, bf16[16,2560]{1,0:T(8,128)(2,1)S(1)}, u32[]{:S(2)}, u32[]{:S(2)}) collective-permute-start(bf16[16,2560]{1,0:T(8,128)(2,1)S(1)} %get-tuple-element.135), channel_id=1, source_target_pairs={{0,24},{4,28},{8,16},{12,20},{16,8},{20,12},{24,0},{28,4},{1,25},{... | collective-permute-start | bytes 245768 | tf_op jit(solution)/shard_map/ppermute | solution.py:98
  133.4 9.1 %collective-permute-start.17 = (bf16[16,2560]{1,0:T(8,128)(2,1)S(1)}, bf16[16,2560]{1,0:T(8,128)(2,1)S(1)}, u32[]{:S(2)}, u32[]{:S(2)}) collective-permute-start(bf16[16,2560]{1,0:T(8,128)(2,1)S(1)} %get-tuple-element.136), channel_id=1, source_target_pairs={{0,16},{4,20},{8,24},{12,28},{16,0},{20,4},{24,8},{28,12},{1,17},{... | collective-permute-start | bytes 245768 | tf_op jit(solution)/shard_map/ppermute | solution.py:98
  133.5 9.0 %copy-start.4 = (f32[16,5134]{1,0:T(8,128)S(1)}, f32[16,5134]{1,0:T(8,128)}, u32[]{:S(2)}) copy-start(f32[16,5134]{1,0:T(8,128)} %m_ref.1) | copy-start | bytes 985732
  133.5 9.0 %copy-start.5 = (f32[16,5134]{1,0:T(8,128)S(1)}, f32[16,5134]{1,0:T(8,128)}, u32[]{:S(2)}) copy-start(f32[16,5134]{1,0:T(8,128)} %v_ref.1) | copy-start | bytes 985732
  133.5 9.0 %copy-start.6 = (f32[16,5134]{1,0:T(8,128)S(1)}, f32[16,5134]{1,0:T(8,128)}, u32[]{:S(2)}) copy-start(f32[16,5134]{1,0:T(8,128)} %ema_ref.1) | copy-start | bytes 985732

commit v6 on v5

--- a/solution.py
+++ b/solution.py
@@ -208,7 +208,7 @@
 FIRST = 2.0 * math.sqrt(2.0 / math.pi)
 THIRD = FIRST * 0.044715
 GATES = 1024
-UNROLL = 4
+UNROLL = 2
 LEAD = 8
 HALF = 64
 

time: 145 us -> 146 us (level)
  no operation moved by 1% of the time
where the time goes in v6:
time: 146 us; the launch traced here: 145 us
  Pallas kernels  52.9 us (36%)
  starting transfers between devices  44.7 us (31%)
  waiting for transfers between devices  34.6 us (24%)
  local copies, waits for them, and re-layouts  8.29 us (6%)
  other arithmetic  3.5 us (2%)
    pallas_call x1, Pallas kernels, block(): pl.pallas_call(partial(block_kernel, sizes), out_shape=(jax.ShapeDtypeStr...  37.4 us
    ppermute x19, starting transfers between devices, by_xor(): lax.ppermute(x, axis, [(index, index ^ step) for index in range(count)])  24.6 us
    all_to_all x5, starting transfers between devices, exchange(): return lax.all_to_all(x, axes, 0, 0, tiled=True)  20.1 us
    all_to_all x5, waiting for transfers between devices, exchange(): return lax.all_to_all(x, axes, 0, 0, tiled=True)  17.3 us
    ppermute x19, waiting for transfers between devices, by_xor(): lax.ppermute(x, axis, [(index, index ^ step) for index in range(count)])  17.3 us
    pallas_call x7, Pallas kernels, call(): pl.pallas_call(kernel, out_shape=outs, in_specs=in_specs, out_specs=jax.t...  15.5 us
    unnamed x40, local copies, waits for them, and re-layouts  5.99 us
  transfers between devices with their start and end apart: 24, of which 12 were waited for; matrix products, arithmetic and copies ran while one was open for 4% of the time, Pallas kernels for 8%

profile of v6, /device:TPU:0, one launch (start us, length us, event | category | flops | bytes accessed | tf_op | source)
XLA Modules:
  0.0 145.1 jit_solution(10062461150685098215)
XLA Ops:
  0.7 2.0 %pack.1 = (f32[4,64,192]{2,1,0:T(8,128)}, bf16[16,2688]{1,0:T(8,128)(2,1)}) custom-call(bf16[7,16,192]{2,1,0:T(8,128)(2,1)} %bitcast.102, f32[7,16,192]{2,1,0:T(8,128)} %bitcast.101, s32[16,192]{1,0:T(8,128)} %bitcast.103, f32[16,5134]{1,0:T(8,128)} %w_ref.1), custom_call_target="tpu_custom_call" | custom-call | tf_op jit(solution)/shard_map/pack/pallas_call | solution.py:616
  2.7 5.1 %collective-permute-start.4 = (bf16[16,2688]{1,0:T(8,128)(2,1)}, bf16[16,2688]{1,0:T(8,128)(2,1)S(1)}, u32[]{:S(2)}, u32[]{:S(2)}) collective-permute-start(bf16[16,2688]{1,0:T(8,128)(2,1)} %get-tuple-element.80), channel_id=1, source_target_pairs={{0,24},{4,28},{8,16},{12,20},{16,8},{20,12},{24,0},{28,4},{1,25},{... | collective-permute-start | bytes 258056 | tf_op jit(solution)/shard_map/ppermute | solution.py:98
  7.8 0.6 collective-permute-start
  8.5 3.4 %all-to-all-start = ((f32[4,64,192]{2,1,0:T(8,128)}), f32[4,64,192]{2,1,0:T(8,128)S(1)}, u32[]{:S(2)}, u32[]{:S(2)}) async-start(f32[4,64,192]{2,1,0:T(8,128)} %get-tuple-element.70), calls=%async_computation | async-start | bytes 524288 | tf_op jit(solution)/shard_map/all_to_all | solution.py:80
  12.6 0.9 fusion.6
  13.8 1.7 %collective-permute-start.1 = (bf16[2,16,2688]{2,1,0:T(8,128)(2,1)S(1)}, bf16[2,16,2688]{2,1,0:T(8,128)(2,1)S(1)}, u32[]{:S(2)}, u32[]{:S(2)}) collective-permute-start(bf16[2,16,2688]{2,1,0:T(8,128)(2,1)S(1)} %pad_maximum_fusion.2), channel_id=1, source_target_pairs={{0,4},{4,0},{8,12},{12,8},{16,20},{20,16},{24,28},{28,24},{1,5},{5... | collective-permute-start | bytes 516104 | tf_op jit(solution)/shard_map/ppermute | solution.py:98
  15.5 2.0 %collective-permute-start.5 = (bf16[2,16,2688]{2,1,0:T(8,128)(2,1)S(1)}, bf16[2,16,2688]{2,1,0:T(8,128)(2,1)S(1)}, u32[]{:S(2)}, u32[]{:S(2)}) collective-permute-start(bf16[2,16,2688]{2,1,0:T(8,128)(2,1)S(1)} %pad_maximum_fusion.3), channel_id=1, source_target_pairs={{0,2},{1,3},{2,0},{3,1},{4,6},{5,7},{6,4},{7,5},{8,10},{9,11},{10,... | collective-permute-start | bytes 516104 | tf_op jit(solution)/shard_map/ppermute | solution.py:98
  17.9 1.4 spectra.1
  19.3 5.5 %all-to-all-start.1 = ((f32[32,16,128]{2,1,0:T(8,128)}), f32[32,16,128]{2,1,0:T(8,128)S(1)}, u32[]{:S(2)}, u32[]{:S(2)}) async-start(f32[32,16,128]{2,1,0:T(8,128)} %spectra.1), calls=%async_computation.1 | async-start | bytes 524288 | tf_op jit(solution)/shard_map/all_to_all | solution.py:80
  24.9 1.8 %collective-permute-start.2 = (bf16[4,16,2688]{2,1,0:T(8,128)(2,1)S(1)}, bf16[4,16,2688]{2,1,0:T(8,128)(2,1)}, u32[]{:S(2)}, u32[]{:S(2)}) collective-permute-start(bf16[4,16,2688]{2,1,0:T(8,128)(2,1)S(1)} %pad_maximum_fusion.refs_0_), channel_id=1, source_target_pairs={{0,2},{1,3},{2,0},{3,1},{4,6},{5,7},{6,4},{7,5},{8,10},{9,11},{10,... | collective-permute-start | bytes 1032200 | tf_op jit(solution)/shard_map/ppermute | solution.py:98
  26.8 1.5 %collective-permute-start.6 = (bf16[4,16,2688]{2,1,0:T(8,128)(2,1)S(1)}, bf16[4,16,2688]{2,1,0:T(8,128)(2,1)}, u32[]{:S(2)}, u32[]{:S(2)}) collective-permute-start(bf16[4,16,2688]{2,1,0:T(8,128)(2,1)S(1)} %pad_maximum_fusion.1.refs_2_), channel_id=1, source_target_pairs={{0,4},{4,0},{8,12},{12,8},{16,20},{20,16},{24,28},{28,24},{1,5},{5... | collective-permute-start | bytes 1032200 | tf_op jit(solution)/shard_map/ppermute | solution.py:98
  28.3 0.5 tables.1
  28.8 0.7 copy-done.1
  29.6 0.7 copy-done.2
  30.3 0.7 copy-done.3
  31.1 0.7 copy-done.7
  31.8 0.7 copy-done.8
  32.5 0.7 copy-done.9
  33.1 2.4 %all-to-all-done.1.got_ref.first_ref = f32[32,16,128]{2,1,0:T(8,128)S(1)} async-done(((f32[32,16,128]{2,1,0:T(8,128)}), f32[32,16,128]{2,1,0:T(8,128)S(1)}, u32[]{:S(2)}, u32[]{:S(2)}) %all-to-all-start.1) | async-done | bytes 262176 | tf_op jit(solution)/shard_map/all_to_all | solution.py:80
  35.5 2.6 %mix.1 = (bf16[32,80,128]{2,1,0:T(8,128)(2,1)}, bf16[16,128,128]{2,1,0:T(8,128)(2,1)S(1)}, f32[16,128]{1,0:T(8,128)S(1)}) custom-call(f32[32,16,128]{2,1,0:T(8,128)S(1)} %all-to-all-done.1.got_ref.first_ref, bf16[16,128,128]{2,1,0:T(8,128)(2,1)S(1)} %maximum_maximum_fusion.mixer_ref), custom_call_target="tpu_custom_call" | custom-call | tf_op jit(solution)/shard_map/mix/pallas_call | solution.py:616
  38.1 0.6 collective-permute-done.6.refs_3_
  38.6 4.1 %all-to-all-start.2 = ((bf16[32,80,128]{2,1,0:T(8,128)(2,1)}), bf16[32,80,128]{2,1,0:T(8,128)(2,1)S(1)}, u32[]{:S(2)}, u32[]{:S(2)}) async-start(bf16[32,80,128]{2,1,0:T(8,128)(2,1)} %get-tuple-element.85), calls=%async_computation.2 | async-start | bytes 1310720 | tf_op jit(solution)/shard_map/all_to_all | solution.py:80
  42.9 0.4 collective-permute-start.8
  43.4 0.4 collective-permute-start.10
  43.9 0.6 pad_add_fusion.me_ref
  44.5 0.6 slice.123
  45.3 0.8 collective-permute-done.9.refs_6_
  46.3 14.2 %all-to-all-done.2.refs_8_ = bf16[32,80,128]{2,1,0:T(8,128)(2,1)S(1)} async-done(((bf16[32,80,128]{2,1,0:T(8,128)(2,1)}), bf16[32,80,128]{2,1,0:T(8,128)(2,1)S(1)}, u32[]{:S(2)}, u32[]{:S(2)}) %all-to-all-start.2) | async-done | bytes 655392 | tf_op jit(solution)/shard_map/all_to_all | solution.py:80
  60.5 0.8 copy-done.13
  61.3 37.4 %block.1 = (bf16[32,80,128]{2,1,0:T(8,128)(2,1)}, f32[8,128]{1,0:T(8,128)}, bf16[4,4,16,2560]{3,2,1,0:T(8,128)(2,1)}, bf16[4,4,16,2560]{3,2,1,0:T(8,128)(2,1)}) custom-call(f32[1]{0:T(128)} %bitcast.3.count_ref, s32[2]{0:T(128)} %pad_add_fusion.me_ref, bf16[4,16,2688]{2,1,0:T(8,128)(2,1)} %copy-done.14, bf16[4,16,2688]{2,1,0:T(8,128)(2,1)} %collective-permute-done.2.refs_1_, ...), custom_call_target="tpu_custom_call" | custom-call | tf_op jit(solution)/shard_map/block/pallas_call | solution.py:545
  98.9 3.6 %all-to-all-start.3 = ((bf16[32,80,128]{2,1,0:T(8,128)(2,1)}), bf16[32,80,128]{2,1,0:T(8,128)(2,1)S(1)}, u32[]{:S(2)}, u32[]{:S(2)}) async-start(bf16[32,80,128]{2,1,0:T(8,128)(2,1)} %get-tuple-element.92), calls=%async_computation.3 | async-start | bytes 1310720 | tf_op jit(solution)/shard_map/all_to_all | solution.py:80
  102.6 1.3 fusion.1
  103.8 1.8 %collective-permute-start.13 = (bf16[4,16,2560]{2,1,0:T(8,128)(2,1)S(1)}, bf16[4,16,2560]{2,1,0:T(8,128)(2,1)S(1)}, u32[]{:S(2)}, u32[]{:S(2)}) collective-permute-start(bf16[4,16,2560]{2,1,0:T(8,128)(2,1)S(1)} %get-tuple-element.129), channel_id=1, source_target_pairs={{0,4},{4,0},{8,12},{12,8},{16,20},{20,16},{24,28},{28,24},{1,5},{5... | collective-permute-start | bytes 983048 | tf_op jit(solution)/shard_map/ppermute | solution.py:98
  105.7 1.5 %collective-permute-start.12 = (bf16[4,16,2560]{2,1,0:T(8,128)(2,1)S(1)}, bf16[4,16,2560]{2,1,0:T(8,128)(2,1)S(1)}, u32[]{:S(2)}, u32[]{:S(2)}) collective-permute-start(bf16[4,16,2560]{2,1,0:T(8,128)(2,1)S(1)} %get-tuple-element.130), channel_id=1, source_target_pairs={{0,2},{1,3},{2,0},{3,1},{4,6},{5,7},{6,4},{7,5},{8,10},{9,11},{10,... | collective-permute-start | bytes 983048 | tf_op jit(solution)/shard_map/ppermute | solution.py:98
  107.1 1.1 fusion.15
  108.3 10.6 %collective-permute-done.13 = bf16[4,16,2560]{2,1,0:T(8,128)(2,1)S(1)} collective-permute-done((bf16[4,16,2560]{2,1,0:T(8,128)(2,1)S(1)}, bf16[4,16,2560]{2,1,0:T(8,128)(2,1)S(1)}, u32[]{:S(2)}, u32[]{:S(2)}) %collective-permute-start.13) | collective-permute-done | bytes 327712 | tf_op jit(solution)/shard_map/ppermute | solution.py:98
  119.0 1.0 collective-permute-done.12
  120.4 1.4 collective-permute-start.14
  121.8 1.4 collective-permute-start.15
  123.3 2.1 %mix_back.1 = (f32[32,8,128]{2,1,0:T(8,128)}, bf16[16,128,128]{2,1,0:T(8,128)(2,1)S(1)}, f32[8,128]{1,0:T(8,128)S(1)}) custom-call(bf16[32,80,128]{2,1,0:T(8,128)(2,1)S(1)} %all-to-all-done.3.got_ref, bf16[16,128,128]{2,1,0:T(8,128)(2,1)S(1)} %maximum_maximum_fusion.mixer_ref, f32[32,16,128]{2,1,0:T(8,128)S(1)} %all-to-all-done.1.got_ref.first_ref, ...), custom_call_target="tpu_custom_call" | custom-call | flops 10000000000 | bytes 1000000000 | tf_op jit(solution)/shard_map/mix_back/pallas_call | solution.py:616
  125.4 0.8 copy-done.12
  126.2 3.5 %all-to-all-start.4 = ((f32[32,8,128]{2,1,0:T(8,128)}), f32[32,8,128]{2,1,0:T(8,128)S(1)}, u32[]{:S(2)}, u32[]{:S(2)}) async-start(f32[32,8,128]{2,1,0:T(8,128)} %get-tuple-element.97), calls=%async_computation.4 | async-start | bytes 262144 | tf_op jit(solution)/shard_map/all_to_all | solution.py:80
  129.8 1.8 %collective-permute-start.16 = (bf16[16,2560]{1,0:T(8,128)(2,1)S(1)}, bf16[16,2560]{1,0:T(8,128)(2,1)S(1)}, u32[]{:S(2)}, u32[]{:S(2)}) collective-permute-start(bf16[16,2560]{1,0:T(8,128)(2,1)S(1)} %get-tuple-element.137), channel_id=1, source_target_pairs={{0,8},{4,12},{8,0},{12,4},{16,24},{20,28},{24,16},{28,20},{1,9},{5... | collective-permute-start | bytes 245768 | tf_op jit(solution)/shard_map/ppermute | solution.py:98
  131.7 2.4 %collective-permute-start.18 = (bf16[16,2560]{1,0:T(8,128)(2,1)S(1)}, bf16[16,2560]{1,0:T(8,128)(2,1)S(1)}, u32[]{:S(2)}, u32[]{:S(2)}) collective-permute-start(bf16[16,2560]{1,0:T(8,128)(2,1)S(1)} %get-tuple-element.135), channel_id=1, source_target_pairs={{0,24},{4,28},{8,16},{12,20},{16,8},{20,12},{24,0},{28,4},{1,25},{... | collective-permute-start | bytes 245768 | tf_op jit(solution)/shard_map/ppermute | solution.py:98
  134.3 5.0 %spectral.1 = (f32[2,16,4096]{2,1,0:T(8,128)}, f32[2,16,4096]{2,1,0:T(8,128)}, f32[2,16,4096]{2,1,0:T(8,128)}, f32[2,16,4096]{2,1,0:T(8,128)}, bf16[2,16,4096]{2,1,0:T(8,128)(2,1)}) custom-call(bf16[16,128,128]{2,1,0:T(8,128)(2,1)} %copy-done.10, bf16[16,128,128]{2,1,0:T(8,128)(2,1)} %copy-done.12, f32[2,16,4096]{2,1,0:T(8,128)} %refs_2_.1, ...), custom_call_target="tpu_custom_call" | custom-call | flops 10000000000 | bytes 1000000000 | tf_op jit(solution)/shard_map/spectral/pallas_call | solution.py:616
  139.3 1.3 collective-permute-done.18.refs_3_
  140.6 2.7 %collective-permute-done.17.refs_2_ = bf16[16,2560]{1,0:T(8,128)(2,1)S(1)} collective-permute-done((bf16[16,2560]{1,0:T(8,128)(2,1)S(1)}, bf16[16,2560]{1,0:T(8,128)(2,1)S(1)}, u32[]{:S(2)}, u32[]{:S(2)}) %collective-permute-start.17) | collective-permute-done | bytes 81952 | tf_op jit(solution)/shard_map/ppermute | solution.py:98
  143.3 1.8 %rows.1 = (f32[1,1]{1,0:T(1,128)}, f32[16,5134]{1,0:T(8,128)}, f32[16,5134]{1,0:T(8,128)}, f32[16,5134]{1,0:T(8,128)}, f32[16,5134]{1,0:T(8,128)}, /*index=5*/bf16[16,5134]{1,0:T(8,128)(2,1)}) custom-call(f32[32,8,128]{2,1,0:T(8,128)S(1)} %all-to-all-done.4.got_ref, f32[8,128]{1,0:T(8,128)S(1)} %get-tuple-element.98.thin_ref, ...), custom_call_target="tpu_custom_call" | custom-call | tf_op jit(solution)/shard_map/rows/pallas_call | solution.py:616
  (72 shorter events, 3.3 us)
Async XLA Ops:
  0.6 11.2 %copy-start.17 = (f32[2,16,4096]{2,1,0:T(8,128)S(1)}, f32[2,16,4096]{2,1,0:T(8,128)}, u32[]{:S(2)}) copy-start(f32[2,16,4096]{2,1,0:T(8,128)} %refs_2_.1) | copy-start | bytes 1572868
  2.7 12.8 %collective-permute-start.4 = (bf16[16,2688]{1,0:T(8,128)(2,1)}, bf16[16,2688]{1,0:T(8,128)(2,1)S(1)}, u32[]{:S(2)}, u32[]{:S(2)}) collective-permute-start(bf16[16,2688]{1,0:T(8,128)(2,1)} %get-tuple-element.80), channel_id=1, source_target_pairs={{0,24},{4,28},{8,16},{12,20},{16,8},{20,12},{24,0},{28,4},{1,25},{... | collective-permute-start | bytes 258056 | tf_op jit(solution)/shard_map/ppermute | solution.py:98
  7.8 7.7 %collective-permute-start.3 = (bf16[16,2688]{1,0:T(8,128)(2,1)}, bf16[16,2688]{1,0:T(8,128)(2,1)S(1)}, u32[]{:S(2)}, u32[]{:S(2)}) collective-permute-start(bf16[16,2688]{1,0:T(8,128)(2,1)} %get-tuple-element.80), channel_id=1, source_target_pairs={{0,16},{4,20},{8,24},{12,28},{16,0},{20,4},{24,8},{28,12},{1,17},{... | collective-permute-start | bytes 258056 | tf_op jit(solution)/shard_map/ppermute | solution.py:98
  7.8 5.9 %collective-permute-start = (bf16[16,2688]{1,0:T(8,128)(2,1)}, bf16[16,2688]{1,0:T(8,128)(2,1)S(1)}, u32[]{:S(2)}, u32[]{:S(2)}) collective-permute-start(bf16[16,2688]{1,0:T(8,128)(2,1)} %get-tuple-element.80), channel_id=1, source_target_pairs={{0,8},{4,12},{8,0},{12,4},{16,24},{20,28},{24,16},{28,20},{1,9},{5... | collective-permute-start | bytes 258056 | tf_op jit(solution)/shard_map/ppermute | solution.py:98
  8.5 9.4 %all-to-all-start = ((f32[4,64,192]{2,1,0:T(8,128)}), f32[4,64,192]{2,1,0:T(8,128)S(1)}, u32[]{:S(2)}, u32[]{:S(2)}) async-start(f32[4,64,192]{2,1,0:T(8,128)} %get-tuple-element.70), calls=%async_computation | async-start | bytes 524288 | tf_op jit(solution)/shard_map/all_to_all | solution.py:80
  11.9 0.7 copy-start.19
  12.2 1.5 %copy-start.18 = (bf16[16,2688]{1,0:T(8,128)(2,1)S(1)}, bf16[16,2688]{1,0:T(8,128)(2,1)}, u32[]{:S(2)}) copy-start(bf16[16,2688]{1,0:T(8,128)(2,1)} %get-tuple-element.80) | copy-start | bytes 258052
  12.3 5.6 %copy-start = (f32[16,5134]{1,0:T(8,128)S(1)}, f32[16,5134]{1,0:T(8,128)}, u32[]{:S(2)}) copy-start(f32[16,5134]{1,0:T(8,128)} %w_ref.1) | copy-start | bytes 985732
  13.8 11.0 %collective-permute-start.1 = (bf16[2,16,2688]{2,1,0:T(8,128)(2,1)S(1)}, bf16[2,16,2688]{2,1,0:T(8,128)(2,1)S(1)}, u32[]{:S(2)}, u32[]{:S(2)}) collective-permute-start(bf16[2,16,2688]{2,1,0:T(8,128)(2,1)S(1)} %pad_maximum_fusion.2), channel_id=1, source_target_pairs={{0,4},{4,0},{8,12},{12,8},{16,20},{20,16},{24,28},{28,24},{1,5},{5... | collective-permute-start | bytes 516104 | tf_op jit(solution)/shard_map/ppermute | solution.py:98
  15.5 11.2 %collective-permute-start.5 = (bf16[2,16,2688]{2,1,0:T(8,128)(2,1)S(1)}, bf16[2,16,2688]{2,1,0:T(8,128)(2,1)S(1)}, u32[]{:S(2)}, u32[]{:S(2)}) collective-permute-start(bf16[2,16,2688]{2,1,0:T(8,128)(2,1)S(1)} %pad_maximum_fusion.3), channel_id=1, source_target_pairs={{0,2},{1,3},{2,0},{3,1},{4,6},{5,7},{6,4},{7,5},{8,10},{9,11},{10,... | collective-permute-start | bytes 516104 | tf_op jit(solution)/shard_map/ppermute | solution.py:98
  19.3 16.2 %all-to-all-start.1 = ((f32[32,16,128]{2,1,0:T(8,128)}), f32[32,16,128]{2,1,0:T(8,128)S(1)}, u32[]{:S(2)}, u32[]{:S(2)}) async-start(f32[32,16,128]{2,1,0:T(8,128)} %spectra.1), calls=%async_computation.1 | async-start | bytes 524288 | tf_op jit(solution)/shard_map/all_to_all | solution.py:80
  24.9 17.9 %copy-start.14 = (bf16[4,16,2688]{2,1,0:T(8,128)(2,1)}, bf16[4,16,2688]{2,1,0:T(8,128)(2,1)S(1)}, u32[]{:S(2)}) copy-start(bf16[4,16,2688]{2,1,0:T(8,128)(2,1)S(1)} %pad_maximum_fusion.refs_0_) | copy-start | bytes 1032196
  24.9 13.2 %collective-permute-start.2 = (bf16[4,16,2688]{2,1,0:T(8,128)(2,1)S(1)}, bf16[4,16,2688]{2,1,0:T(8,128)(2,1)}, u32[]{:S(2)}, u32[]{:S(2)}) collective-permute-start(bf16[4,16,2688]{2,1,0:T(8,128)(2,1)S(1)} %pad_maximum_fusion.refs_0_), channel_id=1, source_target_pairs={{0,2},{1,3},{2,0},{3,1},{4,6},{5,7},{6,4},{7,5},{8,10},{9,11},{10,... | collective-permute-start | bytes 1032200 | tf_op jit(solution)/shard_map/ppermute | solution.py:98
  26.8 16.6 %copy-start.15 = (bf16[4,16,2688]{2,1,0:T(8,128)(2,1)}, bf16[4,16,2688]{2,1,0:T(8,128)(2,1)S(1)}, u32[]{:S(2)}) copy-start(bf16[4,16,2688]{2,1,0:T(8,128)(2,1)S(1)} %pad_maximum_fusion.1.refs_2_) | copy-start | bytes 1032196
  26.8 11.8 %collective-permute-start.6 = (bf16[4,16,2688]{2,1,0:T(8,128)(2,1)S(1)}, bf16[4,16,2688]{2,1,0:T(8,128)(2,1)}, u32[]{:S(2)}, u32[]{:S(2)}) collective-permute-start(bf16[4,16,2688]{2,1,0:T(8,128)(2,1)S(1)} %pad_maximum_fusion.1.refs_2_), channel_id=1, source_target_pairs={{0,4},{4,0},{8,12},{12,8},{16,20},{20,16},{24,28},{28,24},{1,5},{5... | collective-permute-start | bytes 1032200 | tf_op jit(solution)/shard_map/ppermute | solution.py:98
  28.8 0.7 copy-start.1
  29.6 0.7 copy-start.2
  30.3 0.7 copy-start.3
  31.1 0.7 copy-start.7
  31.8 0.7 copy-start.8
  32.5 0.7 copy-start.9
  38.1 60.7 %copy-start.10 = (bf16[16,128,128]{2,1,0:T(8,128)(2,1)}, bf16[16,128,128]{2,1,0:T(8,128)(2,1)S(1)}, u32[]{:S(2)}) copy-start(bf16[16,128,128]{2,1,0:T(8,128)(2,1)S(1)} %get-tuple-element.122.refs_0_) | copy-start | bytes 1572868
  38.6 21.9 %all-to-all-start.2 = ((bf16[32,80,128]{2,1,0:T(8,128)(2,1)}), bf16[32,80,128]{2,1,0:T(8,128)(2,1)S(1)}, u32[]{:S(2)}, u32[]{:S(2)}) async-start(bf16[32,80,128]{2,1,0:T(8,128)(2,1)} %get-tuple-element.85), calls=%async_computation.2 | async-start | bytes 1310720 | tf_op jit(solution)/shard_map/all_to_all | solution.py:80
  42.8 2.3 %collective-permute-start.7 = (bf16[4,16,2688]{2,1,0:T(8,128)(2,1)S(1)}, bf16[4,16,2688]{2,1,0:T(8,128)(2,1)}, u32[]{:S(2)}, u32[]{:S(2)}) collective-permute-start(bf16[4,16,2688]{2,1,0:T(8,128)(2,1)S(1)} %pad_maximum_fusion.refs_0_), channel_id=1, source_target_pairs={{0,1},{1,0},{2,3},{3,2},{4,5},{5,4},{6,7},{7,6},{8,9},{9,8},{10,11... | collective-permute-start | bytes 1032200 | tf_op jit(solution)/shard_map/ppermute | solution.py:98
  42.9 2.4 %collective-permute-start.8 = (bf16[4,16,2688]{2,1,0:T(8,128)(2,1)}, bf16[4,16,2688]{2,1,0:T(8,128)(2,1)}, u32[]{:S(2)}, u32[]{:S(2)}) collective-permute-start(bf16[4,16,2688]{2,1,0:T(8,128)(2,1)} %collective-permute-done.2.refs_1_), channel_id=1, source_target_pairs={{0,1},{1,0},{2,3},{3,2},{4,5},{5,4},{6,7},{7,6},{8,9},{9,8},{10,11... | collective-permute-start | bytes 1032200 | tf_op jit(solution)/shard_map/ppermute | solution.py:98
  43.4 2.7 %collective-permute-start.9 = (bf16[4,16,2688]{2,1,0:T(8,128)(2,1)S(1)}, bf16[4,16,2688]{2,1,0:T(8,128)(2,1)}, u32[]{:S(2)}, u32[]{:S(2)}) collective-permute-start(bf16[4,16,2688]{2,1,0:T(8,128)(2,1)S(1)} %pad_maximum_fusion.1.refs_2_), channel_id=1, source_target_pairs={{0,1},{1,0},{2,3},{3,2},{4,5},{5,4},{6,7},{7,6},{8,9},{9,8},{10,11... | collective-permute-start | bytes 1032200 | tf_op jit(solution)/shard_map/ppermute | solution.py:98
  43.4 2.9 %collective-permute-start.10 = (bf16[4,16,2688]{2,1,0:T(8,128)(2,1)}, bf16[4,16,2688]{2,1,0:T(8,128)(2,1)}, u32[]{:S(2)}, u32[]{:S(2)}) collective-permute-start(bf16[4,16,2688]{2,1,0:T(8,128)(2,1)} %collective-permute-done.6.refs_3_), channel_id=1, source_target_pairs={{0,1},{1,0},{2,3},{3,2},{4,5},{5,4},{6,7},{7,6},{8,9},{9,8},{10,11... | collective-permute-start | bytes 1032200 | tf_op jit(solution)/shard_map/ppermute | solution.py:98
  60.5 0.8 copy-start.13
  98.8 3.7 %copy-start.16 = (bf16[4,4,16,2560]{3,2,1,0:T(8,128)(2,1)S(1)}, bf16[4,4,16,2560]{3,2,1,0:T(8,128)(2,1)}, u32[]{:S(2)}) copy-start(bf16[4,4,16,2560]{3,2,1,0:T(8,128)(2,1)} %get-tuple-element.93) | copy-start | bytes 3932164
  98.8 3.8 %collective-permute-start.11 = (bf16[4,4,16,2560]{3,2,1,0:T(8,128)(2,1)}, bf16[4,4,16,2560]{3,2,1,0:T(8,128)(2,1)}, u32[]{:S(2)}, u32[]{:S(2)}) collective-permute-start(bf16[4,4,16,2560]{3,2,1,0:T(8,128)(2,1)} %get-tuple-element.94), channel_id=1, source_target_pairs={{0,1},{1,0},{2,3},{3,2},{4,5},{5,4},{6,7},{7,6},{8,9},{9,8},{10,11... | collective-permute-start | bytes 3932168 | tf_op jit(solution)/shard_map/ppermute | solution.py:98
  98.9 21.5 %all-to-all-start.3 = ((bf16[32,80,128]{2,1,0:T(8,128)(2,1)}), bf16[32,80,128]{2,1,0:T(8,128)(2,1)S(1)}, u32[]{:S(2)}, u32[]{:S(2)}) async-start(bf16[32,80,128]{2,1,0:T(8,128)(2,1)} %get-tuple-element.92), calls=%async_computation.3 | async-start | bytes 1310720 | tf_op jit(solution)/shard_map/all_to_all | solution.py:80
  103.8 15.0 %collective-permute-start.13 = (bf16[4,16,2560]{2,1,0:T(8,128)(2,1)S(1)}, bf16[4,16,2560]{2,1,0:T(8,128)(2,1)S(1)}, u32[]{:S(2)}, u32[]{:S(2)}) collective-permute-start(bf16[4,16,2560]{2,1,0:T(8,128)(2,1)S(1)} %get-tuple-element.129), channel_id=1, source_target_pairs={{0,4},{4,0},{8,12},{12,8},{16,20},{20,16},{24,28},{28,24},{1,5},{5... | collective-permute-start | bytes 983048 | tf_op jit(solution)/shard_map/ppermute | solution.py:98
  105.7 14.2 %collective-permute-start.12 = (bf16[4,16,2560]{2,1,0:T(8,128)(2,1)S(1)}, bf16[4,16,2560]{2,1,0:T(8,128)(2,1)S(1)}, u32[]{:S(2)}, u32[]{:S(2)}) collective-permute-start(bf16[4,16,2560]{2,1,0:T(8,128)(2,1)S(1)} %get-tuple-element.130), channel_id=1, source_target_pairs={{0,2},{1,3},{2,0},{3,1},{4,6},{5,7},{6,4},{7,5},{8,10},{9,11},{10,... | collective-permute-start | bytes 983048 | tf_op jit(solution)/shard_map/ppermute | solution.py:98
  108.3 15.0 %copy-start.11 = (f32[8,128]{1,0:T(8,128)S(1)}, f32[8,128]{1,0:T(8,128)}, u32[]{:S(2)}) copy-start(f32[8,128]{1,0:T(8,128)} %get-tuple-element.96.stat_ref) | copy-start | bytes 12292
  120.4 9.3 %collective-permute-start.14 = (bf16[2,16,2560]{2,1,0:T(8,128)(2,1)S(1)}, bf16[2,16,2560]{2,1,0:T(8,128)(2,1)S(1)}, u32[]{:S(2)}, u32[]{:S(2)}) collective-permute-start(bf16[2,16,2560]{2,1,0:T(8,128)(2,1)S(1)} %fusion.9), channel_id=1, source_target_pairs={{0,4},{4,0},{8,12},{12,8},{16,20},{20,16},{24,28},{28,24},{1,5},{5... | collective-permute-start | bytes 491528 | tf_op jit(solution)/shard_map/ppermute | solution.py:98
  121.8 7.9 %collective-permute-start.15 = (bf16[2,16,2560]{2,1,0:T(8,128)(2,1)S(1)}, bf16[2,16,2560]{2,1,0:T(8,128)(2,1)S(1)}, u32[]{:S(2)}, u32[]{:S(2)}) collective-permute-start(bf16[2,16,2560]{2,1,0:T(8,128)(2,1)S(1)} %fusion.10), channel_id=1, source_target_pairs={{0,2},{1,3},{2,0},{3,1},{4,6},{5,7},{6,4},{7,5},{8,10},{9,11},{10,... | collective-permute-start | bytes 491528 | tf_op jit(solution)/shard_map/ppermute | solution.py:98
  125.4 0.8 copy-start.12
  126.2 17.1 %all-to-all-start.4 = ((f32[32,8,128]{2,1,0:T(8,128)}), f32[32,8,128]{2,1,0:T(8,128)S(1)}, u32[]{:S(2)}, u32[]{:S(2)}) async-start(f32[32,8,128]{2,1,0:T(8,128)} %get-tuple-element.97), calls=%async_computation.4 | async-start | bytes 262144 | tf_op jit(solution)/shard_map/all_to_all | solution.py:80
  129.8 9.5 %collective-permute-start.16 = (bf16[16,2560]{1,0:T(8,128)(2,1)S(1)}, bf16[16,2560]{1,0:T(8,128)(2,1)S(1)}, u32[]{:S(2)}, u32[]{:S(2)}) collective-permute-start(bf16[16,2560]{1,0:T(8,128)(2,1)S(1)} %get-tuple-element.137), channel_id=1, source_target_pairs={{0,8},{4,12},{8,0},{12,4},{16,24},{20,28},{24,16},{28,20},{1,9},{5... | collective-permute-start | bytes 245768 | tf_op jit(solution)/shard_map/ppermute | solution.py:98
  131.7 8.9 %collective-permute-start.18 = (bf16[16,2560]{1,0:T(8,128)(2,1)S(1)}, bf16[16,2560]{1,0:T(8,128)(2,1)S(1)}, u32[]{:S(2)}, u32[]{:S(2)}) collective-permute-start(bf16[16,2560]{1,0:T(8,128)(2,1)S(1)} %get-tuple-element.135), channel_id=1, source_target_pairs={{0,24},{4,28},{8,16},{12,20},{16,8},{20,12},{24,0},{28,4},{1,25},{... | collective-permute-start | bytes 245768 | tf_op jit(solution)/shard_map/ppermute | solution.py:98
  134.1 9.1 %collective-permute-start.17 = (bf16[16,2560]{1,0:T(8,128)(2,1)S(1)}, bf16[16,2560]{1,0:T(8,128)(2,1)S(1)}, u32[]{:S(2)}, u32[]{:S(2)}) collective-permute-start(bf16[16,2560]{1,0:T(8,128)(2,1)S(1)} %get-tuple-element.136), channel_id=1, source_target_pairs={{0,16},{4,20},{8,24},{12,28},{16,0},{20,4},{24,8},{28,12},{1,17},{... | collective-permute-start | bytes 245768 | tf_op jit(solution)/shard_map/ppermute | solution.py:98
  134.3 9.0 %copy-start.4 = (f32[16,5134]{1,0:T(8,128)S(1)}, f32[16,5134]{1,0:T(8,128)}, u32[]{:S(2)}) copy-start(f32[16,5134]{1,0:T(8,128)} %m_ref.1) | copy-start | bytes 985732
  134.3 9.0 %copy-start.5 = (f32[16,5134]{1,0:T(8,128)S(1)}, f32[16,5134]{1,0:T(8,128)}, u32[]{:S(2)}) copy-start(f32[16,5134]{1,0:T(8,128)} %v_ref.1) | copy-start | bytes 985732
  134.3 9.0 %copy-start.6 = (f32[16,5134]{1,0:T(8,128)S(1)}, f32[16,5134]{1,0:T(8,128)}, u32[]{:S(2)}) copy-start(f32[16,5134]{1,0:T(8,128)} %ema_ref.1) | copy-start | bytes 985732
